TPU v7x, 32 devices: a whole 2x2x4 slice. The times are simulated.
32 devices in a mesh: ctx: 16 (over z, y, x), head: 2 (over core).
Axes of the slice: x: 2, y: 2, z: 4, core: 2. Of those that a mesh axis runs over, the one named last changes fastest.
Arguments:
- q_raw: bfloat16 [8192, 4096], P('ctx', 'head'), may hold values from -60 to 60
- k_raw: bfloat16 [8192, 2048], P('ctx', 'head'), may hold values from -60 to 60
- values: bfloat16 [8192, 2048], P('ctx', 'head'), may hold values from -6 to 6
- d_out: bfloat16 [8192, 4096], P('ctx', 'head'), may hold values from -24 to 24
- doc_ids: int32 [8192], replicated, may hold values from 0 to 7, never falling along the last dimension, each value on 1 to 2048 neighbouring positions
- q_gain: float32 [128], replicated, may hold values from 0.7 to 6.5
- k_gain: float32 [128], replicated, may hold values from 0.7 to 6.5
Outputs:
- q_raw_grad: bfloat16 [8192, 4096], P('ctx', 'head')
- k_raw_grad: bfloat16 [8192, 2048], P('ctx', 'head')
- value_grad: bfloat16 [8192, 2048], P('ctx', 'head')
- q_gain_grad: float32 [128], replicated
- k_gain_grad: float32 [128], replicated
All inputs are finite; a program needn't handle non-finite values.
Results may differ from a plain program's by a relative error of at most 0.009.
The roundings to bfloat16 on the way count: a program that leaves them out, or rounds other values in their place, can miss the bound.
Values may be sent and summed in bfloat16 or wider, within the bound.
No kernel may reach another device: no remote copies, remote signals or barrier semaphores. Data moves between devices by JAX's collectives and lax.ppermute only.
A program may use at most 128 MiB of HBM per device.

v0:
```python
import math

import jax
import jax.numpy as jnp
from jax import lax
from jax.sharding import PartitionSpec as P

D_HEAD = 128
Q_HEADS = 32
KV_HEADS = 16
W = 1024
QUERY_SCALE = 168


epsilon = 1e-06


def shifted(value, axis, steps):
    count = lax.axis_size(axis)
    initial, last = (max(0, -steps), min(count, count - steps))
    return lax.ppermute(value, axis, [(source, source + steps) for source in range(initial, last)])


def normalize(raw_data):
    as_float = raw_data.astype(jnp.float32)
    inverse = lax.rsqrt(jnp.mean(as_float * as_float, axis=-1, keepdims=True) + epsilon)
    return (as_float * inverse, inverse)


def norm_back(grad_rows, unit_rows, inverse, gain_vec, factor):
    scaled_grad = grad_rows * (gain_vec * factor)
    raw_grad = inverse * (
        scaled_grad - unit_rows * jnp.mean(scaled_grad * unit_rows, axis=-1, keepdims=True)
    )
    gain_grad = jnp.sum((grad_rows * unit_rows).reshape(-1, unit_rows.shape[-1]), axis=0) * factor
    return (raw_grad, gain_grad)


def visible_tiles(q_pos, q_ids, k_pos, k_ids):
    offset = q_pos[:, :, None] - k_pos[:, None, :]
    return (q_ids[:, :, None] == k_ids[:, None, :]) & (offset >= 0) & (offset < W)


def row_stats(scores, seen_mask):
    masked = jnp.where(seen_mask, scores, -jnp.inf)
    row_max = jnp.max(masked, axis=-1, keepdims=True)
    row_sum = jnp.sum(jnp.exp(masked - row_max), axis=-1, keepdims=True)
    log_total = row_max + jnp.log(row_sum)
    softmax = jnp.where(seen_mask, jnp.exp(scores - log_total), 0.0)
    return (softmax, log_total[..., 0])


def slice_cols(matrix, column_group, col_width):
    return lax.dynamic_slice_in_dim(matrix, column_group * col_width, col_width, 1)


def tile_windows(array, tile_count, tile_rows, reach_rows):
    return jnp.stack(
        [array[index * tile_rows : index * tile_rows + reach_rows] for index in range(tile_count)]
    )


def on_device(q_raw, k_raw, values, d_out, doc_ids, q_gain, k_gain):
    shard_rows = q_raw.shape[0]
    kv_local = k_raw.shape[1] // D_HEAD
    q_local = q_raw.shape[1] // D_HEAD
    group_size = q_local // kv_local
    group_cols = group_size * D_HEAD
    halo_shards = W // shard_rows
    span_rows = (halo_shards + 1) * shard_rows
    tile_rows = min(128, shard_rows)
    tile_count = shard_rows // tile_rows
    reach_rows = W + tile_rows
    factor = QUERY_SCALE ** (-0.5)
    ctx_index = lax.axis_index("ctx")
    own_start = ctx_index * shard_rows
    q_unit, q_inverse = normalize(q_raw.reshape(shard_rows, q_local, D_HEAD))
    k_unit, k_inverse = normalize(k_raw.reshape(shard_rows, kv_local, D_HEAD))
    q_hat = (q_unit * (q_gain * factor)).astype(jnp.bfloat16).reshape(shard_rows, q_local * D_HEAD)
    k_hat = (k_unit * k_gain).astype(jnp.bfloat16).reshape(shard_rows, kv_local * D_HEAD)
    edge_ids = jnp.full((halo_shards * shard_rows,), -1, jnp.int32)
    padded_ids = jnp.concatenate([edge_ids, doc_ids, edge_ids - 1])
    k_ids = lax.dynamic_slice_in_dim(padded_ids, own_start, span_rows)
    q_ids = lax.dynamic_slice_in_dim(padded_ids, own_start + halo_shards * shard_rows, shard_rows)
    q_pos = own_start + jnp.arange(shard_rows, dtype=jnp.int32)
    k_pos = own_start - halo_shards * shard_rows + jnp.arange(span_rows, dtype=jnp.int32)
    q_pos_tiles = q_pos.reshape(tile_count, tile_rows)
    q_ids_tiles = q_ids.reshape(tile_count, tile_rows)
    key_pieces = []
    value_pieces = []
    for distance in range(halo_shards, 0, -1):
        received = shifted((k_hat, values), "ctx", distance)
        key_pieces.append(received[0])
        value_pieces.append(received[1])
    all_keys = jnp.concatenate(key_pieces + [k_hat], axis=0)
    all_values = jnp.concatenate(value_pieces + [values], axis=0)
    own_mask = visible_tiles(
        q_pos_tiles,
        q_ids_tiles,
        tile_windows(k_pos, tile_count, tile_rows, reach_rows),
        tile_windows(k_ids, tile_count, tile_rows, reach_rows),
    )

    def own_queries(kv_head):
        q_block = slice_cols(q_hat, kv_head, group_cols).reshape(
            tile_count, tile_rows, group_size, D_HEAD
        )
        g_block = slice_cols(d_out, kv_head, group_cols).reshape(
            tile_count, tile_rows, group_size, D_HEAD
        )
        k_tiles = tile_windows(
            slice_cols(all_keys, kv_head, D_HEAD), tile_count, tile_rows, reach_rows
        )
        v_tiles = tile_windows(
            slice_cols(all_values, kv_head, D_HEAD), tile_count, tile_rows, reach_rows
        )
        scores = jnp.einsum("ntgd,nsd->gnts", q_block, k_tiles, preferred_element_type=jnp.float32)
        softmax, log_total = row_stats(scores, own_mask)
        weights = softmax.astype(jnp.bfloat16)
        attended = jnp.einsum(
            "gnts,nsd->ntgd", weights, v_tiles, preferred_element_type=jnp.float32
        )
        row_delta = jnp.transpose(
            jnp.sum(g_block.astype(jnp.float32) * attended, axis=-1), (2, 0, 1)
        )
        prob_grad = jnp.einsum(
            "ntgd,nsd->gnts", g_block, v_tiles, preferred_element_type=jnp.float32
        )
        score_grad = (softmax * (prob_grad - row_delta[..., None])).astype(jnp.bfloat16)
        query_part = jnp.einsum(
            "gnts,nsd->ntgd", score_grad, k_tiles, preferred_element_type=jnp.float32
        )
        return (
            q_block,
            g_block,
            weights,
            score_grad,
            query_part.reshape(shard_rows, group_cols),
            log_total.reshape(group_size, shard_rows),
            row_delta.reshape(group_size, shard_rows),
        )

    def whole_head(kv_head):
        q_block, g_block, weights, score_grad, query_part, log_total, row_delta = own_queries(
            kv_head
        )
        key_part = jnp.einsum(
            "gnts,ntgd->nsd", score_grad, q_block, preferred_element_type=jnp.float32
        )
        value_part = jnp.einsum(
            "gnts,ntgd->nsd", weights, g_block, preferred_element_type=jnp.float32
        )
        key_span = jnp.zeros((span_rows, D_HEAD), jnp.float32)
        value_span = jnp.zeros((span_rows, D_HEAD), jnp.float32)
        for index in range(tile_count):
            key_span = key_span.at[index * tile_rows : index * tile_rows + reach_rows].add(
                key_part[index]
            )
            value_span = value_span.at[index * tile_rows : index * tile_rows + reach_rows].add(
                value_part[index]
            )
        return (query_part, key_span, value_span)

    query_stack, key_stack, value_stack = lax.map(whole_head, jnp.arange(kv_local, dtype=jnp.int32))
    key_sum = key_stack[:, halo_shards * shard_rows :, :]
    value_sum = value_stack[:, halo_shards * shard_rows :, :]
    for distance in range(1, halo_shards + 1):
        offset_rows = (halo_shards - distance) * shard_rows
        returned = (
            shifted(
                key_stack[:, offset_rows : offset_rows + shard_rows, :].astype(jnp.bfloat16),
                "ctx",
                -distance,
            ).astype(jnp.float32),
            shifted(
                value_stack[:, offset_rows : offset_rows + shard_rows, :].astype(jnp.bfloat16),
                "ctx",
                -distance,
            ).astype(jnp.float32),
        )
        key_sum = key_sum + returned[0]
        value_sum = value_sum + returned[1]
    query_grad = jnp.transpose(query_stack, (1, 0, 2)).reshape(shard_rows, q_local, D_HEAD)
    key_grad = jnp.transpose(key_sum, (1, 0, 2))
    q_raw_grad, q_gain_part = norm_back(query_grad, q_unit, q_inverse, q_gain, factor)
    k_raw_grad, k_gain_part = norm_back(key_grad, k_unit, k_inverse, k_gain, 1.0)
    gain_totals = lax.psum((q_gain_part, k_gain_part), ("ctx", "head"))
    total_rows = shard_rows * lax.axis_size("ctx")
    value_grad = jnp.transpose(value_sum, (1, 0, 2)).reshape(shard_rows, kv_local * D_HEAD)
    return (
        q_raw_grad.reshape(shard_rows, q_local * D_HEAD).astype(jnp.bfloat16),
        k_raw_grad.reshape(shard_rows, kv_local * D_HEAD).astype(jnp.bfloat16),
        value_grad.astype(jnp.bfloat16),
        gain_totals[0] / math.sqrt(total_rows * Q_HEADS),
        gain_totals[1] / math.sqrt(total_rows * KV_HEADS),
    )


def solution(mesh):
    return jax.shard_map(
        on_device,
        mesh=mesh,
        in_specs=(
            P("ctx", "head"),
            P("ctx", "head"),
            P("ctx", "head"),
            P("ctx", "head"),
            P(),
            P(),
            P(),
        ),
        out_specs=(P("ctx", "head"), P("ctx", "head"), P("ctx", "head"), P(), P()),
        check_vma=False,
    )
```

profile of v0, /device:TPU:0, one launch (start us, length us, event | category | flops | bytes accessed | tf_op | source)
XLA Modules:
  0.0 519.8 jit_solution(8081570817609136354)
XLA Ops:
  4.6 5.8 %collective-permute-start = (bf16[512,1024]{0,1:T(8,128)(2,1)}, bf16[512,1024]{0,1:T(8,128)(2,1)}, u32[]{:S(2)}, u32[]{:S(2)}) collective-permute-start(bf16[512,1024]{0,1:T(8,128)(2,1)} %fusion.42), channel_id=1, source_target_pairs={{0,4},{2,6},{4,8},{6,10},{8,12},{10,14},{12,16},{14,18},{16,20},{1... | collective-permute-start | bytes 3145736 | tf_op jit(solution)/shard_map/ppermute | solution.py:21
  10.4 4.4 collective-permute-start.1
  17.3 4.4 collective-permute-start.3
  21.7 3.0 copy.53
  28.2 2.8 reshape.382
  33.7 5.4 %copy.60 = f32[512,2048]{1,0:T(8,128)} copy(f32[512,2048]{0,1:T(8,128)} %bitcast.277) | data formatting | bytes 8388608 | tf_op jit(solution)/shard_map/mul | solution.py:32
  40.0 4.2 multiply_convert_fusion
  44.2 34.0 %collective-permute-done = bf16[512,1024]{0,1:T(8,128)(2,1)} collective-permute-done((bf16[512,1024]{0,1:T(8,128)(2,1)}, bf16[512,1024]{0,1:T(8,128)(2,1)}, u32[]{:S(2)}, u32[]{:S(2)}) %collective-permute-start) | collective-permute-done | bytes 1048608 | tf_op jit(solution)/shard_map/ppermute | solution.py:21
  78.2 3.2 pad_maximum_fusion
  81.4 18.1 %collective-permute-done.2 = bf16[512,1024]{1,0:T(8,128)(2,1)} collective-permute-done((bf16[512,1024]{1,0:T(8,128)(2,1)}, bf16[512,1024]{1,0:T(8,128)(2,1)}, u32[]{:S(2)}, u32[]{:S(2)}) %collective-permute-start.2) | collective-permute-done | bytes 1048608 | tf_op jit(solution)/shard_map/ppermute | solution.py:21
  99.6 3.2 pad_maximum_fusion.1
  103.3 252.9 %while.26 = (s32[]{:T(128)}, f32[8,512,256]{2,1,0:T(8,128)}, f32[8,1536,128]{1,2,0:T(8,128)}, f32[8,1536,128]{2,1,0:T(8,128)}, s32[8]{0:T(128)}, /*index=5*/bf16...) while((s32[]{:T(128)}, f32[8,512,256]{2,1,0:T(8,128)}, ...), condition=%wide.region_6.7_spmd.clone, body=%wide.region_2.6_spmd.clone.sunk | while | flops 1854502912 | bytes 122116240 | solution.py:164
  115.4 3.3 convolution_bitcast_fusion.9
  141.0 2.8 fusion.77
  147.1 3.3 convolution_bitcast_fusion.9
  178.6 3.3 convolution_bitcast_fusion.9
  210.3 3.3 convolution_bitcast_fusion.9
  241.9 3.3 convolution_bitcast_fusion.9
  267.4 2.8 fusion.77
  273.5 3.3 convolution_bitcast_fusion.9
  305.0 3.3 convolution_bitcast_fusion.9
  336.6 3.3 convolution_bitcast_fusion.9
  356.2 3.2 convert.11
  363.5 5.6 %copy.57 = f32[8,512,256]{1,2,0:T(8,128)} copy(f32[8,512,256]{2,1,0:T(8,128)} %get-tuple-element.268) | data formatting | bytes 8388608 | tf_op jit(solution)/shard_map/while | solution.py:164
  369.1 6.7 %copy.64 = f32[512,8,256]{2,1,0:T(8,128)} copy(f32[512,8,256]{2,0,1:T(8,128)} %bitcast.276) | data formatting | bytes 8388608 | tf_op jit(solution)/shard_map/transpose | solution.py:183
  375.8 4.7 reshape.379
  380.5 3.4 convert.12
  389.6 5.4 %copy.58 = f32[512,2048]{1,0:T(8,128)} copy(f32[512,2048]{0,1:T(8,128)} %bitcast.271) | data formatting | bytes 8388608 | tf_op jit(solution)/shard_map/reshape | solution.py:183
  395.0 4.2 multiply_reduce_fusion
  403.2 6.3 %fusion.39 = bf16[512,2048]{1,0:T(8,128)(2,1)} fusion(f32[512,2048]{1,0:T(8,128)S(1)} %copy-done.5, f32[64,8,16,128]{3,2,1,0:T(8,128)} %bitcast.278, f32[512,2048]{1,0:T(8,128)S(1)} %copy-done.8, f32[2048]{0:T(1024)S(1)} %copy-done.21, bf16[512,2048]{1,0:T(8,128)(2,1)S(1)} %copy-done.7), kind=kLoop, calls=%fused_computation.68 | loop fusion | flops 7340032 | bytes 16785408 | tf_op jit(solution)/shard_map/convert_element_type | solution.py:191
  415.2 100.1 %all-reduce.2 = (f32[128]{0:T(128)S(1)}, f32[128]{0:T(128)S(1)}) all-reduce(f32[128]{0:T(128)S(1)} %broadcast_multiply_fusion.4, f32[128]{0:T(128)S(1)} %get-tuple-element.339), channel_id=1, replica_groups=mesh['ctx'=16,'head'=2] {'ctx','head'}, use_global_device_ids=true, to_apply=%region_10.11 | all-reduce | flops 256 | bytes 2048 | tf_op jit(solution)/shard_map/psum | solution.py:187
  516.3 3.5 copy_bitcast_fusion
  (550 shorter events, 242.0 us)
Async XLA Ops:
  0.6 21.1 %copy-start.6 = (bf16[512,2048]{1,0:T(8,128)(2,1)S(1)}, bf16[512,2048]{1,0:T(8,128)(2,1)}, u32[]{:S(2)}) copy-start(bf16[512,2048]{1,0:T(8,128)(2,1)} %param.25) | copy-start | bytes 6291460
  2.3 22.4 %copy-start.3 = (bf16[512,1024]{0,1:T(8,128)(2,1)}, bf16[512,1024]{0,1:T(8,128)(2,1)S(1)}, u32[]{:S(2)}) copy-start(bf16[512,1024]{0,1:T(8,128)(2,1)S(1)} %copy.54) | copy-start | bytes 3145732
  4.6 73.7 %collective-permute-start = (bf16[512,1024]{0,1:T(8,128)(2,1)}, bf16[512,1024]{0,1:T(8,128)(2,1)}, u32[]{:S(2)}, u32[]{:S(2)}) collective-permute-start(bf16[512,1024]{0,1:T(8,128)(2,1)} %fusion.42), channel_id=1, source_target_pairs={{0,4},{2,6},{4,8},{6,10},{8,12},{10,14},{12,16},{14,18},{16,20},{1... | collective-permute-start | bytes 3145736 | tf_op jit(solution)/shard_map/ppermute | solution.py:21
  10.4 67.8 %collective-permute-start.1 = (bf16[512,1024]{0,1:T(8,128)(2,1)}, bf16[512,1024]{0,1:T(8,128)(2,1)}, u32[]{:S(2)}, u32[]{:S(2)}) collective-permute-start(bf16[512,1024]{0,1:T(8,128)(2,1)} %fusion.42), channel_id=1, source_target_pairs={{0,2},{2,4},{4,6},{6,8},{8,10},{10,12},{12,14},{14,16},{16,18},{18... | collective-permute-start | bytes 3145736 | tf_op jit(solution)/shard_map/ppermute | solution.py:21
  14.8 84.8 %collective-permute-start.2 = (bf16[512,1024]{1,0:T(8,128)(2,1)}, bf16[512,1024]{1,0:T(8,128)(2,1)}, u32[]{:S(2)}, u32[]{:S(2)}) collective-permute-start(bf16[512,1024]{1,0:T(8,128)(2,1)} %param.27), channel_id=1, source_target_pairs={{0,4},{2,6},{4,8},{6,10},{8,12},{10,14},{12,16},{14,18},{16,20},{1... | collective-permute-start | bytes 3145736 | tf_op jit(solution)/shard_map/ppermute | solution.py:21
  17.3 82.3 %collective-permute-start.3 = (bf16[512,1024]{1,0:T(8,128)(2,1)}, bf16[512,1024]{1,0:T(8,128)(2,1)}, u32[]{:S(2)}, u32[]{:S(2)}) collective-permute-start(bf16[512,1024]{1,0:T(8,128)(2,1)} %param.27), channel_id=1, source_target_pairs={{0,2},{2,4},{4,6},{6,8},{8,10},{10,12},{12,14},{14,16},{16,18},{18... | collective-permute-start | bytes 3145736 | tf_op jit(solution)/shard_map/ppermute | solution.py:21
  27.6 12.5 %copy-start.20 = (f32[2048]{0:T(1024)}, f32[2048]{0:T(1024)S(1)}, u32[]{:S(2)}) copy-start(f32[2048]{0:T(1024)S(1)} %broadcast_bitcast_fusion) | copy-start | bytes 24580
  115.3 6.4 %slice-start = ((s8[4718592]{0:T(1024)(128)(4,1)}), s8[4194304]{0:T(1024)(128)(4,1)S(1)}, s32[]{:S(2)}) async-start(s8[4718592]{0:T(1024)(128)(4,1)} %bitcast.267), calls=%async_computation | async-start | bytes 8388608 | tf_op jit(solution)/shard_map/while
  147.0 6.3 %slice-start = ((s8[4718592]{0:T(1024)(128)(4,1)}), s8[4194304]{0:T(1024)(128)(4,1)S(1)}, s32[]{:S(2)}) async-start(s8[4718592]{0:T(1024)(128)(4,1)} %bitcast.267), calls=%async_computation | async-start | bytes 8388608 | tf_op jit(solution)/shard_map/while
  170.1 6.1 %copy-start.9 = (bf16[1152,128]{1,0:T(8,128)(2,1)}, bf16[1152,128]{1,0:T(8,128)(2,1)S(1)}, u32[]{:S(2)}) copy-start(bf16[1152,128]{1,0:T(8,128)(2,1)S(1)} %copy.115) | copy-start | bytes 884740 | tf_op jit(solution)/shard_map/while
  178.6 6.4 %slice-start = ((s8[4718592]{0:T(1024)(128)(4,1)}), s8[4194304]{0:T(1024)(128)(4,1)S(1)}, s32[]{:S(2)}) async-start(s8[4718592]{0:T(1024)(128)(4,1)} %bitcast.267), calls=%async_computation | async-start | bytes 8388608 | tf_op jit(solution)/shard_map/while
  201.8 6.1 %copy-start.9 = (bf16[1152,128]{1,0:T(8,128)(2,1)}, bf16[1152,128]{1,0:T(8,128)(2,1)S(1)}, u32[]{:S(2)}) copy-start(bf16[1152,128]{1,0:T(8,128)(2,1)S(1)} %copy.115) | copy-start | bytes 884740 | tf_op jit(solution)/shard_map/while
  210.3 6.4 %slice-start = ((s8[4718592]{0:T(1024)(128)(4,1)}), s8[4194304]{0:T(1024)(128)(4,1)S(1)}, s32[]{:S(2)}) async-start(s8[4718592]{0:T(1024)(128)(4,1)} %bitcast.267), calls=%async_computation | async-start | bytes 8388608 | tf_op jit(solution)/shard_map/while
  233.4 6.1 %copy-start.9 = (bf16[1152,128]{1,0:T(8,128)(2,1)}, bf16[1152,128]{1,0:T(8,128)(2,1)S(1)}, u32[]{:S(2)}) copy-start(bf16[1152,128]{1,0:T(8,128)(2,1)S(1)} %copy.115) | copy-start | bytes 884740 | tf_op jit(solution)/shard_map/while
  241.9 6.3 %slice-start = ((s8[4718592]{0:T(1024)(128)(4,1)}), s8[4194304]{0:T(1024)(128)(4,1)S(1)}, s32[]{:S(2)}) async-start(s8[4718592]{0:T(1024)(128)(4,1)} %bitcast.267), calls=%async_computation | async-start | bytes 8388608 | tf_op jit(solution)/shard_map/while
  273.5 6.3 %slice-start = ((s8[4718592]{0:T(1024)(128)(4,1)}), s8[4194304]{0:T(1024)(128)(4,1)S(1)}, s32[]{:S(2)}) async-start(s8[4718592]{0:T(1024)(128)(4,1)} %bitcast.267), calls=%async_computation | async-start | bytes 8388608 | tf_op jit(solution)/shard_map/while
  305.0 6.3 %slice-start = ((s8[4718592]{0:T(1024)(128)(4,1)}), s8[4194304]{0:T(1024)(128)(4,1)S(1)}, s32[]{:S(2)}) async-start(s8[4718592]{0:T(1024)(128)(4,1)} %bitcast.267), calls=%async_computation | async-start | bytes 8388608 | tf_op jit(solution)/shard_map/while
  328.1 6.1 %copy-start.9 = (bf16[1152,128]{1,0:T(8,128)(2,1)}, bf16[1152,128]{1,0:T(8,128)(2,1)S(1)}, u32[]{:S(2)}) copy-start(bf16[1152,128]{1,0:T(8,128)(2,1)S(1)} %copy.115) | copy-start | bytes 884740 | tf_op jit(solution)/shard_map/while
  336.6 6.5 %slice-start = ((s8[4718592]{0:T(1024)(128)(4,1)}), s8[4194304]{0:T(1024)(128)(4,1)S(1)}, s32[]{:S(2)}) async-start(s8[4718592]{0:T(1024)(128)(4,1)} %bitcast.267), calls=%async_computation | async-start | bytes 8388608 | tf_op jit(solution)/shard_map/while
  360.9 48.6 %collective-permute-start.4 = (bf16[8,512,128]{1,2,0:T(8,128)(2,1)}, bf16[8,512,128]{1,2,0:T(8,128)(2,1)S(1)}, u32[]{:S(2)}, u32[]{:S(2)}) collective-permute-start(bf16[8,512,128]{1,2,0:T(8,128)(2,1)} %get-tuple-element.383), channel_id=1, source_target_pairs={{2,0},{4,2},{6,4},{8,6},{10,8},{12,10},{14,12},{16,14},{18,16},{20... | collective-permute-start | bytes 3145736 | tf_op jit(solution)/shard_map/ppermute | solution.py:21
  362.2 47.3 %collective-permute-start.5 = (bf16[8,512,128]{1,2,0:T(8,128)(2,1)}, bf16[8,512,128]{1,2,0:T(8,128)(2,1)}, u32[]{:S(2)}, u32[]{:S(2)}) collective-permute-start(bf16[8,512,128]{1,2,0:T(8,128)(2,1)} %get-tuple-element.384), channel_id=1, source_target_pairs={{4,0},{6,2},{8,4},{10,6},{12,8},{14,10},{16,12},{18,14},{20,16},{2... | collective-permute-start | bytes 3145736 | tf_op jit(solution)/shard_map/ppermute | solution.py:21
  380.5 7.7 %copy-start.2 = (f32[8,512,256]{1,2,0:T(8,128)S(1)}, f32[8,512,256]{1,2,0:T(8,128)}, u32[]{:S(2)}) copy-start(f32[8,512,256]{1,2,0:T(8,128)} %copy.57) | copy-start | bytes 12582916
  380.5 7.8 %copy-start.16 = (f32[512,16]{0,1:T(8,128)S(1)}, f32[512,16]{0,1:T(8,128)}, u32[]{:S(2)}) copy-start(f32[512,16]{0,1:T(8,128)} %copy-done.15) | copy-start | bytes 98308
  385.5 130.8 %collective-permute-start.6 = (bf16[8,512,128]{2,1,0:T(8,128)(2,1)}, bf16[8,512,128]{2,1,0:T(8,128)(2,1)}, u32[]{:S(2)}, u32[]{:S(2)}) collective-permute-start(bf16[8,512,128]{2,1,0:T(8,128)(2,1)} %get-tuple-element.381), channel_id=1, source_target_pairs={{2,0},{4,2},{6,4},{8,6},{10,8},{12,10},{14,12},{16,14},{18,16},{20... | collective-permute-start | bytes 3145736 | tf_op jit(solution)/shard_map/ppermute | solution.py:21
  386.9 129.3 %collective-permute-start.7 = (bf16[8,512,128]{2,1,0:T(8,128)(2,1)}, bf16[8,512,128]{2,1,0:T(8,128)(2,1)}, u32[]{:S(2)}, u32[]{:S(2)}) collective-permute-start(bf16[8,512,128]{2,1,0:T(8,128)(2,1)} %get-tuple-element.382), channel_id=1, source_target_pairs={{4,0},{6,2},{8,4},{10,6},{12,8},{14,10},{16,12},{18,14},{20,16},{2... | collective-permute-start | bytes 3145736 | tf_op jit(solution)/shard_map/ppermute | solution.py:21
  395.0 7.0 %copy-start.7 = (bf16[512,2048]{1,0:T(8,128)(2,1)S(1)}, bf16[512,2048]{1,0:T(8,128)(2,1)}, u32[]{:S(2)}) copy-start(bf16[512,2048]{1,0:T(8,128)(2,1)} %param.25) | copy-start | bytes 6291460
  395.0 7.1 %copy-start.8 = (f32[512,2048]{1,0:T(8,128)S(1)}, f32[512,2048]{1,0:T(8,128)}, u32[]{:S(2)}) copy-start(f32[512,2048]{1,0:T(8,128)} %copy.58) | copy-start | bytes 12582916
  399.3 10.2 %slice-start.2 = ((s8[6291456]{0:T(1024)(128)(4,1)}), s8[4194304]{0:T(1024)(128)(4,1)S(1)}, s32[]{:S(2)}) async-start(s8[6291456]{0:T(1024)(128)(4,1)} %bitcast.274), calls=%async_computation.2 | async-start | bytes 8388608
  403.2 6.3 %copy-start.4 = (bf16[512,1024]{0,1:T(8,128)(2,1)S(1)}, bf16[512,1024]{0,1:T(8,128)(2,1)}, u32[]{:S(2)}) copy-start(bf16[512,1024]{0,1:T(8,128)(2,1)} %copy-done.3) | copy-start | bytes 3145732
  403.2 6.4 %slice-start.3 = ((s8[6291456]{0:T(1024)(128)(4,1)}), s8[2097152]{0:T(1024)(128)(4,1)S(1)}, s32[]{:S(2)}) async-start(s8[6291456]{0:T(1024)(128)(4,1)} %bitcast.274), calls=%async_computation.3 | async-start | bytes 4194304
  403.2 6.4 %copy-start.18 = (f32[512,8]{0,1:T(8,128)S(1)}, f32[512,8]{0,1:T(8,128)}, u32[]{:S(2)}) copy-start(f32[512,8]{0,1:T(8,128)} %copy-done.17) | copy-start | bytes 49156
  403.2 6.4 %copy-start.24 = (f32[128]{0:T(128)S(1)}, f32[128]{0:T(128)}, u32[]{:S(2)}) copy-start(f32[128]{0:T(128)} %param.31) | copy-start | bytes 1540
  (71 other events, 319.4 us)
where the time goes:
time: 522 us; the launch traced here: 520 us
  local copies, waits for them, and re-layouts  174 us (33%)
  blocking collectives  100 us (19%)
  other arithmetic  83.7 us (16%)
  matrix products  73.4 us (14%)
  waiting for transfers between devices  52.1 us (10%)
  starting transfers between devices  22.4 us (4%)
  loops' own time  12.7 us (2%)
    psum x1, blocking collectives, on_device(): gain_totals = lax.psum((q_gain_part, k_gain_part), ('ctx', 'head'))  100 us
    ppermute x8, waiting for transfers between devices, shifted(): lax.ppermute(value, axis, [(source, source + steps) for source in range(i...  52.1 us
    dynamic_update_slice x32, local copies, waits for them, and re-layouts, on_device(): lax.map(whole_head, jnp.arange(kv_local, dtype=jnp.int32))  49.4 us
    dot_general x8, matrix products, whole_head(): jnp.einsum('gnts,ntgd->nsd', weights, g_block, preferred_element_type=jnp...  26.7 us
    while x192, local copies, waits for them, and re-layouts  23.7 us
    and x8, other arithmetic, visible_tiles(): (q_ids[:, :, None] == k_ids[:, None, :]) & (offset >= 0) & (offset < W)  22.5 us
    ppermute x8, starting transfers between devices, shifted(): lax.ppermute(value, axis, [(source, source + steps) for source in range(i...  22.4 us
    dot_general x8, matrix products, own_queries(): jnp.einsum('gnts,nsd->ntgd', score_grad, k_tiles, preferred_element_type=...  13.3 us
  transfers between devices with their start and end apart: 8, of which 2 were waited for; matrix products, arithmetic and copies ran while one was open for 14% of the time, Pallas kernels for 0%

commit v1 on v0

v1 whole, which is shorter than its diff:
```python
import functools
import math

import jax
import jax.numpy as jnp
from jax import lax
from jax.experimental import pallas as pl
from jax.experimental.pallas import tpu as pltpu
from jax.sharding import PartitionSpec as P

Q_HEADS = 32
KV_HEADS = 16
W = 1024
QUERY_SCALE = 168
EPS = 1e-06
CHUNKS = (2, 2, 2, 2)
D=128
BF=jnp.bfloat16
F32=jnp.float32
NT=(((1,),(1,)),((),()))
NN=(((1,),(0,)),((),()))
def dotf(a,b,dims):
    return lax.dot_general(a,b,dims,preferred_element_type=F32)

def attn_body(T, rows, halo, par_ref, lo_ref, gq_ref, q_ref, g_ref, own_ref, h1a_ref, h1b_ref, h2_ref,
              qg_ref, own_out, r1_out, r2_out, qgain_ref, kgain_ref,
              ks, vs, kt, s_s, dp_s, ds_s, dk_acc, dv_acc):
    h = pl.program_id(0); i = pl.program_id(1)
    nb = halo // T + 1
    win = halo + T
    @pl.when(i == 0)
    def _():
        def put(ref, at):
            ks[at:at+rows] = ref[:, :D]; vs[at:at+rows] = ref[:, D:]
        put(h2_ref, 0)
        @pl.when(par_ref[0] == 1)
        def _(): put(h1a_ref, rows)
        @pl.when(par_ref[0] == 0)
        def _(): put(h1b_ref, rows)
        put(own_ref, 2*rows)
        kt[...] = ks[...].T
        dk_acc[...] = jnp.zeros_like(dk_acc); dv_acc[...] = jnp.zeros_like(dv_acc)
    @pl.when((i == 0) & (h == 0))
    def _():
        qgain_ref[...] = jnp.zeros_like(qgain_ref); kgain_ref[...] = jnp.zeros_like(kgain_ref)
    w0 = pl.multiple_of(i * T, T)
    def cols(ref):
        return jnp.concatenate([ref[:, :D].T, ref[:, D:].T], axis=1)
    gq = gq_ref[...]
    qf = cols(q_ref).astype(F32)
    q_inv = lax.rsqrt(jnp.mean(qf*qf, axis=0, keepdims=True) + 1e-6)
    q_unit = qf * q_inv
    qt = (q_unit * gq).astype(BF)
    gt = cols(g_ref)
    lo = lo_ref[...] - i*T
    lo = jnp.concatenate([lo, lo], axis=1)
    iota = lax.broadcasted_iota(jnp.int32, (T, 2*T), 0)
    lane = lax.broadcasted_iota(jnp.int32, (T, 2*T), 1)
    tok = jnp.where(lane >= T, lane - T, lane)
    def fold(x, op):
        return op(x.reshape(T//8, 8, 2*T), axis=0)
    m8 = None
    for kb in range(nb):
        s = dotf(ks[pl.ds(w0 + kb*T, T), :], qt, NN)
        see = iota >= lo - kb*T
        if kb == nb-1: see = see & (iota <= tok)
        s = jnp.where(see, s, -1e30)
        s_s[kb*T:(kb+1)*T] = s
        f = fold(s, jnp.max)
        m8 = f if m8 is None else jnp.maximum(m8, f)
    m = jnp.max(m8, axis=0, keepdims=True)
    l8 = None
    for kb in range(nb):
        e = jnp.exp(s_s[kb*T:(kb+1)*T] - m)
        s_s[kb*T:(kb+1)*T] = e
        f = fold(e, jnp.sum)
        l8 = f if l8 is None else l8 + f
        dp_s[kb*T:(kb+1)*T] = dotf(vs[pl.ds(w0 + kb*T, T), :], gt, NN)
    inv_l = 1.0 / jnp.sum(l8, axis=0, keepdims=True)
    d8 = None
    for kb in range(nb):
        w = (s_s[kb*T:(kb+1)*T] * inv_l).astype(BF)
        f = fold(w.astype(F32) * dp_s[kb*T:(kb+1)*T], jnp.sum)
        d8 = f if d8 is None else d8 + f
        at = pl.ds(w0 + kb*T, T)
        dv_acc[at, :] = dv_acc[at, :] + dotf(w, gt, NT)
    delta = jnp.sum(d8, axis=0, keepdims=True)
    for kb in range(nb):
        p = s_s[kb*T:(kb+1)*T] * inv_l
        ds = (p * (dp_s[kb*T:(kb+1)*T] - delta)).astype(BF)
        ds_s[kb*T:(kb+1)*T] = ds
        at = pl.ds(w0 + kb*T, T)
        dk_acc[at, :] = dk_acc[at, :] + dotf(ds, qt, NT)
    dq = dotf(kt[:, pl.ds(w0, win)], ds_s[...], NN)
    qgain_ref[...] += dq * q_unit
    up = dq * gq
    mean = jnp.mean(up * q_unit, axis=0, keepdims=True)
    qr = (q_inv * (up - q_unit * mean)).astype(BF)
    qg_ref[:, :D] = qr[:, :T].T
    qg_ref[:, D:] = qr[:, T:].T
    @pl.when(i == rows // T - 1)
    def _():
        own_out[:, :D] = dk_acc[2*rows:]; own_out[:, D:] = dv_acc[2*rows:]
        r1_out[:, :D] = dk_acc[rows:2*rows].astype(BF); r1_out[:, D:] = dv_acc[rows:2*rows].astype(BF)
        r2_out[:, :D] = dk_acc[:rows].astype(BF); r2_out[:, D:] = dv_acc[:rows].astype(BF)
        kgain_ref[...] += jnp.sum((dk_acc[...] * ks[...].astype(F32)).reshape(-1, 8, D), axis=0)

def attn(par, lo, gq, q, g, own, h1a, h1b, h2, off, hc, qg_prev=None):
    rows = q.shape[0]; T = 128; halo = 2*rows
    win = halo + T
    kvs = pl.BlockSpec((rows, 2*D), lambda h, i: (0, h))
    in_specs=[pl.BlockSpec(memory_space=pltpu.SMEM),
              pl.BlockSpec((1,T), lambda h,i:(0,i)),
              pl.BlockSpec((D,1), lambda h,i:(0,0)),
              pl.BlockSpec((T,2*D), lambda h,i:(i,off+h)),
              pl.BlockSpec((T,2*D), lambda h,i:(i,off+h)),
              kvs,kvs,kvs,kvs]
    args=[par,lo,gq,q,g,own,h1a,h1b,h2]
    body = functools.partial(attn_body, T, rows, halo)
    alias={}
    if qg_prev is not None:
        in_specs.append(pl.BlockSpec(memory_space=pl.ANY)); args.append(qg_prev); alias={9:0}
        inner = body
        body = lambda *r: inner(*r[:9], *r[10:])
    return pl.pallas_call(body, grid=(hc, rows//T), in_specs=in_specs,
        out_specs=[pl.BlockSpec((T,2*D), lambda h,i:(i,off+h)), kvs,kvs,kvs,
                   pl.BlockSpec((D,2*T), lambda h,i:(0,0)), pl.BlockSpec((8,D), lambda h,i:(0,0))],
        out_shape=[jax.ShapeDtypeStruct(q.shape,BF), jax.ShapeDtypeStruct((rows,hc*2*D),F32),
                   jax.ShapeDtypeStruct((rows,hc*2*D),BF), jax.ShapeDtypeStruct((rows,hc*2*D),BF),
                   jax.ShapeDtypeStruct((D,2*T),F32), jax.ShapeDtypeStruct((8,D),F32)],
        scratch_shapes=[pltpu.VMEM((3*rows,D),BF),pltpu.VMEM((3*rows,D),BF),pltpu.VMEM((D,3*rows),BF),
            pltpu.VMEM((win,2*T),F32),pltpu.VMEM((win,2*T),F32),pltpu.VMEM((win,2*T),BF),
            pltpu.VMEM((3*rows,D),F32),pltpu.VMEM((3*rows,D),F32)],
        input_output_aliases=alias,
        compiler_params=pltpu.CompilerParams(dimension_semantics=("arbitrary","arbitrary"), vmem_limit_bytes=40*1024*1024),
        name="attn_grad")(*args)


def pack_body(hc, k_ref, v_ref, gain_ref, out_ref):
    for h in range(hc):
        k = k_ref[:, h*D:(h+1)*D].astype(F32)
        inv = lax.rsqrt(jnp.mean(k*k, axis=1, keepdims=True) + EPS)
        out_ref[:, 2*h*D:(2*h+1)*D] = (k * inv * gain_ref[...]).astype(BF)
        out_ref[:, (2*h+1)*D:(2*h+2)*D] = v_ref[:, h*D:(h+1)*D]


def pack(k_raw, values, k_gain, off, hc):
    rows = k_raw.shape[0]
    cb = [pl.BlockSpec((rows, D), lambda h: (0, off + h))] * 2
    return pl.pallas_call(
        functools.partial(pack_body, 1), grid=(hc,),
        in_specs=cb + [pl.BlockSpec((1, D), lambda h: (0, 0))],
        out_specs=pl.BlockSpec((rows, 2*D), lambda h: (0, h)),
        out_shape=jax.ShapeDtypeStruct((rows, hc*2*D), BF),
        name="pack_kv")(k_raw, values, k_gain)


def finish_body(par_ref, own_ref, x_ref, y_ref, k_ref, gain_ref, *refs):
    kg_ref, vg_ref = refs[-2:]
    even = jnp.where(par_ref[0] == 0, 1.0, 0.0)
    t = own_ref[...] + y_ref[...].astype(F32) + x_ref[...].astype(F32) * even
    vg_ref[...] = t[:, D:].astype(BF)
    k = k_ref[...].astype(F32)
    inv = lax.rsqrt(jnp.mean(k*k, axis=1, keepdims=True) + EPS)
    unit = k * inv
    up = t[:, :D] * gain_ref[...]
    kg_ref[...] = (inv * (up - unit * jnp.mean(up * unit, axis=1, keepdims=True))).astype(BF)


def finish(par, own, x, y, k_raw, k_gain, off, hc, prev):
    rows = own.shape[0]
    kvs = pl.BlockSpec((rows, 2*D), lambda h: (0, h))
    cb = pl.BlockSpec((rows, D), lambda h: (0, off + h))
    in_specs = [pl.BlockSpec(memory_space=pltpu.SMEM), kvs, kvs, kvs, cb, pl.BlockSpec((1, D), lambda h: (0, 0))]
    args = [par, own, x, y, k_raw, k_gain]
    alias = {}
    if prev is not None:
        in_specs += [pl.BlockSpec(memory_space=pl.ANY)] * 2
        args += list(prev)
        alias = {6: 0, 7: 1}
    return pl.pallas_call(
        finish_body, grid=(hc,), in_specs=in_specs, out_specs=[cb, cb],
        out_shape=[jax.ShapeDtypeStruct(k_raw.shape, BF)] * 2,
        input_output_aliases=alias, name="finish_kv")(*args)


def on_device(q_raw, k_raw, values, d_out, doc_ids, q_gain, k_gain):
    rows = q_raw.shape[0]
    kv_local = k_raw.shape[1] // D
    count = lax.axis_size("ctx")
    assert 2 * rows == W and count % 2 == 0 and q_raw.shape[1] == 2 * k_raw.shape[1]
    chunks = CHUNKS if kv_local == sum(CHUNKS) else (1,) * kv_local
    factor = QUERY_SCALE ** (-0.5)
    me = lax.axis_index("ctx")
    par = (me % 2).astype(jnp.int32).reshape(1)
    onward = [(i, i + 2) for i in range(count - 2)]
    back = [(i + 2, i) for i in range(count - 2)]
    swap = [(i, i ^ 1) for i in range(count)]
    up = [(i, i + 1) for i in range(0, count, 2)]
    down = [(i + 1, i) for i in range(0, count, 2)]

    gk = k_gain.reshape(1, D)
    own, far, near_a, near_b = [], [], [], []
    off = 0
    for hc in chunks:
        own.append(pack(k_raw, values, gk, off, hc))
        off += hc
    for c in range(len(chunks)):
        far.append(lax.ppermute(own[c], "ctx", onward))
        near_a.append(lax.ppermute(own[c], "ctx", up))
    for c in range(len(chunks)):
        near_b.append(lax.ppermute(far[c], "ctx", down))

    padded = jnp.concatenate([jnp.full((W,), -1, jnp.int32), doc_ids])
    span_ids = lax.dynamic_slice_in_dim(padded, me * rows, W + rows)
    q_ids = span_ids[W:]
    first = jnp.sum((span_ids[:, None] < q_ids[None, :]).astype(jnp.int32), axis=0)
    lo = jnp.maximum(first, jnp.arange(1, rows + 1, dtype=jnp.int32)).reshape(1, rows)
    gq = (q_gain * factor).reshape(D, 1)

    qg = None
    mine, r1, r2, qs, kss = [], [], [], [], []
    off = 0
    for c, hc in enumerate(chunks):
        qg, o, a, b, s, t = attn(par, lo, gq, q_raw, d_out, own[c], near_a[c], near_b[c], far[c], off, hc, qg)
        mine.append(o); r1.append(a); r2.append(b); qs.append(s); kss.append(t)
        off += hc
    q_part = jnp.sum(sum(qs), axis=1) * factor
    k_part = jnp.sum(sum(kss), axis=0) / k_gain
    gains = lax.psum(jnp.stack([q_part, k_part]), ("ctx", "head"))

    out = None
    off = 0
    for c, hc in enumerate(chunks):
        x = lax.ppermute(r1[c], "ctx", swap)
        both = (r2[c].astype(F32) + x.astype(F32)).astype(BF)
        y = lax.ppermute(jnp.where(par[0] == 1, both, r2[c]), "ctx", back)
        out = finish(par, mine[c], x, y, k_raw, gk, off, hc, out)
        off += hc
    total = rows * count
    return (qg, out[0], out[1], gains[0] / math.sqrt(total * Q_HEADS), gains[1] / math.sqrt(total * KV_HEADS))


def solution(mesh):
    split = P("ctx", "head")
    return jax.shard_map(
        on_device,
        mesh=mesh,
        in_specs=(split, split, split, split, P(), P(), P()),
        out_specs=(split, split, split, P(), P()),
        check_vma=False,
    )
```

time: 522 us -> 235 us (0.45)
  local copies, waits for them, and re-layouts: 174 us -> 8.87 us
  Pallas kernels: 0 us -> 84.3 us
  other arithmetic: 83.7 us -> 4.75 us
  matrix products: 73.4 us -> 0 us
  waiting for transfers between devices: 52.1 us -> 11.2 us
  starting transfers between devices: 22.4 us -> 50.5 us
  blocking collectives: 100 us -> 73.4 us
  loops' own time: 12.7 us -> 0 us
    pallas_call x0 -> x12, Pallas kernels: none -> 84.3 us  [the longest x4 66.1 us: attn(): pl.pallas_call(body, grid=(hc, rows // T), in_specs=in_specs, out_specs=[...]
    dot_general x48 -> x0, matrix products: 73.4 us -> none  [the longest x8 26.7 us: whole_head(): jnp.einsum('gnts,ntgd->nsd', weights, g_block, preferred_element_type=jnp...]
    dynamic_update_slice x32 -> x0, local copies, waits for them, and re-layouts: 49.4 us -> none  [on_device(): lax.map(whole_head, jnp.arange(kv_local, dtype=jnp.int32))]
    ppermute x8 -> x20, waiting for transfers between devices: 52.1 us -> 11.2 us  [the longest x4 7.33 us: on_device(): far.append(lax.ppermute(own[c], 'ctx', onward))]
    while x193 -> x0, local copies, waits for them, and re-layouts: 29.3 us -> none
    ppermute x8 -> x20, starting transfers between devices: 22.4 us -> 50.5 us  [the longest x4 17.3 us: on_device(): near_a.append(lax.ppermute(own[c], 'ctx', up))]
    psum x1, blocking collectives: 100 us -> 73.4 us  [on_device(): gains = lax.psum(jnp.stack([q_part, k_part]), ('ctx', 'head'))]
    and x8 -> x0, other arithmetic: 22.5 us -> none  [visible_tiles(): (q_ids[:, :, None] == k_ids[:, None, :]) & (offset >= 0) & (offset < W)]
  transfers between devices with their start and end apart: 8 -> 20, of which waited for: 2 -> 3; matrix products, arithmetic and copies ran while one was open for 14% -> 2% of each run, Pallas kernels for 0% -> 34%
where the time goes in v1:
time: 235 us; the launch traced here: 234 us
  Pallas kernels  84.3 us (36%)
  blocking collectives  73.4 us (31%)
  starting transfers between devices  50.5 us (21%)
  waiting for transfers between devices  11.2 us (5%)
  local copies, waits for them, and re-layouts  8.87 us (4%)
  other arithmetic  4.75 us (2%)
    psum x1, blocking collectives, on_device(): gains = lax.psum(jnp.stack([q_part, k_part]), ('ctx', 'head'))  73.4 us
    pallas_call x4, Pallas kernels, attn(): pl.pallas_call(body, grid=(hc, rows // T), in_specs=in_specs, out_specs=[...  66.1 us
    ppermute x4, starting transfers between devices, on_device(): near_a.append(lax.ppermute(own[c], 'ctx', up))  17.3 us
    ppermute x4, starting transfers between devices, on_device(): far.append(lax.ppermute(own[c], 'ctx', onward))  16.4 us
    pallas_call x4, Pallas kernels, finish(): pl.pallas_call(finish_body, grid=(hc,), in_specs=in_specs, out_specs=[cb,...  10.1 us
    unnamed x40, local copies, waits for them, and re-layouts  8.59 us
    pallas_call x4, Pallas kernels, pack(): pl.pallas_call(functools.partial(pack_body, 1), grid=(hc,), in_specs=cb +...  8.18 us
    ppermute x4, waiting for transfers between devices, on_device(): far.append(lax.ppermute(own[c], 'ctx', onward))  7.33 us
  transfers between devices with their start and end apart: 20, of which 3 were waited for; matrix products, arithmetic and copies ran while one was open for 2% of the time, Pallas kernels for 34%

profile of v1, /device:TPU:0, one launch (start us, length us, event | category | flops | bytes accessed | tf_op | source)
XLA Modules:
  0.0 234.0 jit_solution(15678349689683437118)
XLA Ops:
  0.6 2.0 pack_kv.7.own_ref
  2.7 5.7 %collective-permute-start.10 = (bf16[512,512]{1,0:T(8,128)(2,1)}, bf16[512,512]{1,0:T(8,128)(2,1)}, u32[]{:S(2)}, u32[]{:S(2)}) collective-permute-start(bf16[512,512]{1,0:T(8,128)(2,1)} %pack_kv.7.own_ref), channel_id=1, source_target_pairs={{0,4},{2,6},{4,8},{6,10},{8,12},{10,14},{12,16},{14,18},{16,20},{1... | collective-permute-start | bytes 1572872 | tf_op jit(solution)/shard_map/ppermute | solution.py:209
  8.4 4.2 %collective-permute-start.9 = (bf16[512,512]{1,0:T(8,128)(2,1)}, bf16[512,512]{1,0:T(8,128)(2,1)}, u32[]{:S(2)}, u32[]{:S(2)}) collective-permute-start(bf16[512,512]{1,0:T(8,128)(2,1)} %pack_kv.7.own_ref), channel_id=1, source_target_pairs={{0,2},{4,6},{8,10},{12,14},{16,18},{20,22},{24,26},{28,30},{1,3},{... | collective-permute-start | bytes 1572872 | tf_op jit(solution)/shard_map/ppermute | solution.py:210
  12.6 2.1 pack_kv.6.r_5_
  14.6 3.7 %collective-permute-start.7 = (bf16[512,512]{1,0:T(8,128)(2,1)}, bf16[512,512]{1,0:T(8,128)(2,1)}, u32[]{:S(2)}, u32[]{:S(2)}) collective-permute-start(bf16[512,512]{1,0:T(8,128)(2,1)} %pack_kv.6.r_5_), channel_id=1, source_target_pairs={{0,4},{2,6},{4,8},{6,10},{8,12},{10,14},{12,16},{14,18},{16,20},{1... | collective-permute-start | bytes 1572872 | tf_op jit(solution)/shard_map/ppermute | solution.py:209
  18.4 2.1 collective-permute-start.6
  20.4 2.0 pack_kv.5.r_5_
  22.5 3.6 %collective-permute-start.4 = (bf16[512,512]{1,0:T(8,128)(2,1)}, bf16[512,512]{1,0:T(8,128)(2,1)}, u32[]{:S(2)}, u32[]{:S(2)}) collective-permute-start(bf16[512,512]{1,0:T(8,128)(2,1)} %pack_kv.5.r_5_), channel_id=1, source_target_pairs={{0,4},{2,6},{4,8},{6,10},{8,12},{10,14},{12,16},{14,18},{16,20},{1... | collective-permute-start | bytes 1572872 | tf_op jit(solution)/shard_map/ppermute | solution.py:209
  26.0 2.0 pack_kv.4.r_5_
  28.1 3.5 %collective-permute-start.1 = (bf16[512,512]{1,0:T(8,128)(2,1)}, bf16[512,512]{1,0:T(8,128)(2,1)}, u32[]{:S(2)}, u32[]{:S(2)}) collective-permute-start(bf16[512,512]{1,0:T(8,128)(2,1)} %pack_kv.4.r_5_), channel_id=1, source_target_pairs={{0,4},{2,6},{4,8},{6,10},{8,12},{10,14},{12,16},{14,18},{16,20},{1... | collective-permute-start | bytes 1572872 | tf_op jit(solution)/shard_map/ppermute | solution.py:209
  32.9 1.3 collective-permute-start.8
  34.3 6.9 %collective-permute-start.3 = (bf16[512,512]{1,0:T(8,128)(2,1)S(1)}, bf16[512,512]{1,0:T(8,128)(2,1)}, u32[]{:S(2)}, u32[]{:S(2)}) collective-permute-start(bf16[512,512]{1,0:T(8,128)(2,1)S(1)} %copy-done.4), channel_id=1, source_target_pairs={{0,2},{4,6},{8,10},{12,14},{16,18},{20,22},{24,26},{28,30},{1,3},{... | collective-permute-start | bytes 1572872 | tf_op jit(solution)/shard_map/ppermute | solution.py:210
  41.2 1.4 collective-permute-done.4.r_8_
  42.6 4.2 %collective-permute-start = (bf16[512,512]{1,0:T(8,128)(2,1)}, bf16[512,512]{1,0:T(8,128)(2,1)}, u32[]{:S(2)}, u32[]{:S(2)}) collective-permute-start(bf16[512,512]{1,0:T(8,128)(2,1)} %pack_kv.4.r_5_), channel_id=1, source_target_pairs={{0,2},{4,6},{8,10},{12,14},{16,18},{20,22},{24,26},{28,30},{1,3},{... | collective-permute-start | bytes 1572872 | tf_op jit(solution)/shard_map/ppermute | solution.py:210
  46.8 5.9 %collective-permute-done.1.r_8_ = bf16[512,512]{1,0:T(8,128)(2,1)} collective-permute-done((bf16[512,512]{1,0:T(8,128)(2,1)}, bf16[512,512]{1,0:T(8,128)(2,1)}, u32[]{:S(2)}, u32[]{:S(2)}) %collective-permute-start.1) | collective-permute-done | bytes 524320 | tf_op jit(solution)/shard_map/ppermute | solution.py:209
  55.9 1.6 copy-done.1
  57.5 16.6 %attn_grad.4 = (bf16[512,2048]{1,0:T(8,128)(2,1)}, f32[512,512]{1,0:T(8,128)S(1)}, bf16[512,512]{1,0:T(8,128)(2,1)}, bf16[512,512]{1,0:T(8,128)(2,1)S(1)}, f32[128,256]{1,0:T(8,128)S(1)}, /*index=5*/f32[8,128]{1,0:T(8,128)S(1)}) custom-call(s32[1]{0:T(128)} %bitcast.par_ref.r_0_, s32[1,512]{1,0:T(1,128)S(1)} %add_maximum_fusion.lo_ref.r_1_, ...), custom_call_target="tpu_custom_call" | custom-call | tf_op jit(solution)/shard_map/attn_grad/pallas_call | solution.py:125
  75.8 4.2 %collective-permute-start.18 = (bf16[512,512]{1,0:T(8,128)(2,1)}, bf16[512,512]{1,0:T(8,128)(2,1)}, u32[]{:S(2)}, u32[]{:S(2)}) collective-permute-start(bf16[512,512]{1,0:T(8,128)(2,1)} %get-tuple-element.51), channel_id=1, source_target_pairs={{0,2},{2,0},{4,6},{6,4},{8,10},{10,8},{12,14},{14,12},{16,18},{18,... | collective-permute-start | bytes 1572872 | tf_op jit(solution)/shard_map/ppermute | solution.py:235
  80.1 16.6 %attn_grad.5 = (bf16[512,2048]{1,0:T(8,128)(2,1)}, f32[512,512]{1,0:T(8,128)S(1)}, bf16[512,512]{1,0:T(8,128)(2,1)}, bf16[512,512]{1,0:T(8,128)(2,1)S(1)}, f32[128,256]{1,0:T(8,128)S(1)}, /*index=5*/f32[8,128]{1,0:T(8,128)S(1)}) custom-call(s32[1]{0:T(128)} %bitcast.par_ref.r_0_, ...), custom_call_target="tpu_custom_call", output_to_operand_aliasing={{0}: (9, {})} | custom-call | tf_op jit(solution)/shard_map/attn_grad/pallas_call | solution.py:125
  97.7 1.6 copy-done.2
  99.3 16.4 %attn_grad.6 = (bf16[512,2048]{1,0:T(8,128)(2,1)}, f32[512,512]{1,0:T(8,128)S(1)}, bf16[512,512]{1,0:T(8,128)(2,1)S(1)}, bf16[512,512]{1,0:T(8,128)(2,1)S(1)}, f...) custom-call(s32[1]{0:T(128)} %bitcast.par_ref.r_0_, ...), custom_call_target="tpu_custom_call", output_to_operand_aliasing={{0}: (9, {})} | custom-call | tf_op jit(solution)/shard_map/attn_grad/pallas_call | solution.py:125
  116.7 2.0 collective-permute-start.14
  118.7 16.5 %attn_grad.7 = (bf16[512,2048]{1,0:T(8,128)(2,1)}, f32[512,512]{1,0:T(8,128)S(1)}, bf16[512,512]{1,0:T(8,128)(2,1)S(1)}, bf16[512,512]{1,0:T(8,128)(2,1)S(1)}, f...) custom-call(s32[1]{0:T(128)} %bitcast.par_ref.r_0_, ...), custom_call_target="tpu_custom_call", output_to_operand_aliasing={{0}: (9, {})} | custom-call | tf_op jit(solution)/shard_map/attn_grad/pallas_call | solution.py:125
  135.4 2.1 fusion.3
  137.5 1.5 collective-permute-start.19
  143.0 3.8 %collective-permute-done.12.x_ref = bf16[512,512]{1,0:T(8,128)(2,1)S(1)} collective-permute-done((bf16[512,512]{1,0:T(8,128)(2,1)S(1)}, bf16[512,512]{1,0:T(8,128)(2,1)S(1)}, u32[]{:S(2)}, u32[]{:S(2)}) %collective-permute-start.12) | collective-permute-done | bytes 524320 | tf_op jit(solution)/shard_map/ppermute | solution.py:235
  147.0 1.3 collective-permute-start.13
  148.4 73.4 %psum.7 = f32[2,128]{1,0:T(2,128)S(1)} all-reduce(f32[2,128]{1,0:T(2,128)S(1)} %pad_maximum_fusion), channel_id=1, replica_groups=mesh['ctx'=16,'head'=2] {'ctx','head'}, use_global_device_ids=true, to_apply=%region_3.4 | all-reduce | flops 256 | bytes 2048 | tf_op jit(solution)/shard_map/psum | solution.py:230
  223.1 2.5 %finish_kv.4 = (bf16[512,1024]{1,0:T(8,128)(2,1)}, bf16[512,1024]{1,0:T(8,128)(2,1)}) custom-call(s32[1]{0:T(128)} %bitcast.par_ref.r_0_, f32[512,512]{1,0:T(8,128)} %copy-done.7, bf16[512,512]{1,0:T(8,128)(2,1)} %collective-permute-done.18.x_ref, bf16[512,512]{1,0:T(8,128)(2,1)} %copy-done.15, bf16[512,1024]{1,0:T(8,128)(2,1)} %k_ref.15, f32[1,128]{1,0:T(1,128)} %bitcast.17), custom_call_target="tpu_custom_call" | custom-call | tf_op jit(solution)/shard_map/finish_kv/pallas_call | solution.py:181
  225.6 2.5 %finish_kv.5 = (bf16[512,1024]{1,0:T(8,128)(2,1)}, bf16[512,1024]{1,0:T(8,128)(2,1)}) custom-call(s32[1]{0:T(128)} %bitcast.par_ref.r_0_, f32[512,512]{1,0:T(8,128)} %copy-done.8, bf16[512,512]{1,0:T(8,128)(2,1)} %collective-permute-done.16.x_ref, bf16[512,512]{1,0:T(8,128)(2,1)} %collective-permute-done.17.y_ref, ...), custom_call_target="tpu_custom_call", output_to_operand_aliasing={{0}: (6, {}), {1}: (7, {})} | custom-call | tf_op jit(solution)/shard_map/finish_kv/pallas_call | solution.py:181
  228.1 2.5 %finish_kv.6 = (bf16[512,1024]{1,0:T(8,128)(2,1)}, bf16[512,1024]{1,0:T(8,128)(2,1)}) custom-call(s32[1]{0:T(128)} %bitcast.par_ref.r_0_, f32[512,512]{1,0:T(8,128)} %copy-done.9, bf16[512,512]{1,0:T(8,128)(2,1)} %copy-done.13, bf16[512,512]{1,0:T(8,128)(2,1)} %collective-permute-done.15.y_ref, ...), custom_call_target="tpu_custom_call", output_to_operand_aliasing={{0}: (6, {}), {1}: (7, {})} | custom-call | tf_op jit(solution)/shard_map/finish_kv/pallas_call | solution.py:181
  231.5 2.5 %finish_kv.7 = (bf16[512,1024]{1,0:T(8,128)(2,1)}, bf16[512,1024]{1,0:T(8,128)(2,1)}) custom-call(s32[1]{0:T(128)} %bitcast.par_ref.r_0_, f32[512,512]{1,0:T(8,128)} %copy-done.10, bf16[512,512]{1,0:T(8,128)(2,1)} %copy-done.14, bf16[512,512]{1,0:T(8,128)(2,1)} %copy-done.16, ...), custom_call_target="tpu_custom_call", output_to_operand_aliasing={{0}: (6, {}), {1}: (7, {})} | custom-call | tf_op jit(solution)/shard_map/finish_kv/pallas_call | solution.py:181
  (76 shorter events, 14.9 us)
Async XLA Ops:
  2.7 25.4 %collective-permute-start.10 = (bf16[512,512]{1,0:T(8,128)(2,1)}, bf16[512,512]{1,0:T(8,128)(2,1)}, u32[]{:S(2)}, u32[]{:S(2)}) collective-permute-start(bf16[512,512]{1,0:T(8,128)(2,1)} %pack_kv.7.own_ref), channel_id=1, source_target_pairs={{0,4},{2,6},{4,8},{6,10},{8,12},{10,14},{12,16},{14,18},{16,20},{1... | collective-permute-start | bytes 1572872 | tf_op jit(solution)/shard_map/ppermute | solution.py:209
  8.4 23.2 %collective-permute-start.9 = (bf16[512,512]{1,0:T(8,128)(2,1)}, bf16[512,512]{1,0:T(8,128)(2,1)}, u32[]{:S(2)}, u32[]{:S(2)}) collective-permute-start(bf16[512,512]{1,0:T(8,128)(2,1)} %pack_kv.7.own_ref), channel_id=1, source_target_pairs={{0,2},{4,6},{8,10},{12,14},{16,18},{20,22},{24,26},{28,30},{1,3},{... | collective-permute-start | bytes 1572872 | tf_op jit(solution)/shard_map/ppermute | solution.py:210
  14.6 18.2 %copy-start.19 = (f32[128]{0:T(128)S(1)}, f32[128]{0:T(128)}, u32[]{:S(2)}) copy-start(f32[128]{0:T(128)} %param.12) | copy-start | bytes 1540
  14.6 19.5 %copy-start.17 = (s32[8192]{0:T(1024)S(1)}, s32[8192]{0:T(1024)}, u32[]{:S(2)}) copy-start(s32[8192]{0:T(1024)} %param.11) | copy-start | bytes 98308
  14.6 41.2 %copy-start = (bf16[512,2048]{1,0:T(8,128)(2,1)S(1)}, bf16[512,2048]{1,0:T(8,128)(2,1)}, u32[]{:S(2)}) copy-start(bf16[512,2048]{1,0:T(8,128)(2,1)} %r_3_.5) | copy-start | bytes 6291460
  14.6 41.2 %copy-start.6 = (bf16[512,512]{1,0:T(8,128)(2,1)S(1)}, bf16[512,512]{1,0:T(8,128)(2,1)}, u32[]{:S(2)}) copy-start(bf16[512,512]{1,0:T(8,128)(2,1)} %pack_kv.7.own_ref) | copy-start | bytes 1572868
  14.6 18.2 %collective-permute-start.7 = (bf16[512,512]{1,0:T(8,128)(2,1)}, bf16[512,512]{1,0:T(8,128)(2,1)}, u32[]{:S(2)}, u32[]{:S(2)}) collective-permute-start(bf16[512,512]{1,0:T(8,128)(2,1)} %pack_kv.6.r_5_), channel_id=1, source_target_pairs={{0,4},{2,6},{4,8},{6,10},{8,12},{10,14},{12,16},{14,18},{16,20},{1... | collective-permute-start | bytes 1572872 | tf_op jit(solution)/shard_map/ppermute | solution.py:209
  18.4 16.0 %collective-permute-start.6 = (bf16[512,512]{1,0:T(8,128)(2,1)}, bf16[512,512]{1,0:T(8,128)(2,1)}, u32[]{:S(2)}, u32[]{:S(2)}) collective-permute-start(bf16[512,512]{1,0:T(8,128)(2,1)} %pack_kv.6.r_5_), channel_id=1, source_target_pairs={{0,2},{4,6},{8,10},{12,14},{16,18},{20,22},{24,26},{28,30},{1,3},{... | collective-permute-start | bytes 1572872 | tf_op jit(solution)/shard_map/ppermute | solution.py:210
  22.5 11.9 %copy-start.4 = (bf16[512,512]{1,0:T(8,128)(2,1)S(1)}, bf16[512,512]{1,0:T(8,128)(2,1)}, u32[]{:S(2)}) copy-start(bf16[512,512]{1,0:T(8,128)(2,1)} %pack_kv.5.r_5_) | copy-start | bytes 1572868
  22.5 20.2 %collective-permute-start.4 = (bf16[512,512]{1,0:T(8,128)(2,1)}, bf16[512,512]{1,0:T(8,128)(2,1)}, u32[]{:S(2)}, u32[]{:S(2)}) collective-permute-start(bf16[512,512]{1,0:T(8,128)(2,1)} %pack_kv.5.r_5_), channel_id=1, source_target_pairs={{0,4},{2,6},{4,8},{6,10},{8,12},{10,14},{12,16},{14,18},{16,20},{1... | collective-permute-start | bytes 1572872 | tf_op jit(solution)/shard_map/ppermute | solution.py:209
  28.1 24.7 %collective-permute-start.1 = (bf16[512,512]{1,0:T(8,128)(2,1)}, bf16[512,512]{1,0:T(8,128)(2,1)}, u32[]{:S(2)}, u32[]{:S(2)}) collective-permute-start(bf16[512,512]{1,0:T(8,128)(2,1)} %pack_kv.4.r_5_), channel_id=1, source_target_pairs={{0,4},{2,6},{4,8},{6,10},{8,12},{10,14},{12,16},{14,18},{16,20},{1... | collective-permute-start | bytes 1572872 | tf_op jit(solution)/shard_map/ppermute | solution.py:209
  31.5 22.5 %collective-permute-start.11 = (bf16[512,512]{1,0:T(8,128)(2,1)}, bf16[512,512]{1,0:T(8,128)(2,1)}, u32[]{:S(2)}, u32[]{:S(2)}) collective-permute-start(bf16[512,512]{1,0:T(8,128)(2,1)} %collective-permute-done.10.h2_ref), channel_id=1, source_target_pairs={{2,0},{6,4},{10,8},{14,12},{18,16},{22,20},{26,24},{30,28},{3,1},{... | collective-permute-start | bytes 1572872 | tf_op jit(solution)/shard_map/ppermute | solution.py:212
  32.9 42.9 %collective-permute-start.8 = (bf16[512,512]{1,0:T(8,128)(2,1)}, bf16[512,512]{1,0:T(8,128)(2,1)}, u32[]{:S(2)}, u32[]{:S(2)}) collective-permute-start(bf16[512,512]{1,0:T(8,128)(2,1)} %collective-permute-done.7.r_8_), channel_id=1, source_target_pairs={{2,0},{6,4},{10,8},{14,12},{18,16},{22,20},{26,24},{30,28},{3,1},{... | collective-permute-start | bytes 1572872 | tf_op jit(solution)/shard_map/ppermute | solution.py:212
  34.3 63.3 %collective-permute-start.3 = (bf16[512,512]{1,0:T(8,128)(2,1)S(1)}, bf16[512,512]{1,0:T(8,128)(2,1)}, u32[]{:S(2)}, u32[]{:S(2)}) collective-permute-start(bf16[512,512]{1,0:T(8,128)(2,1)S(1)} %copy-done.4), channel_id=1, source_target_pairs={{0,2},{4,6},{8,10},{12,14},{16,18},{20,22},{24,26},{28,30},{1,3},{... | collective-permute-start | bytes 1572872 | tf_op jit(solution)/shard_map/ppermute | solution.py:210
  42.6 76.0 %collective-permute-start = (bf16[512,512]{1,0:T(8,128)(2,1)}, bf16[512,512]{1,0:T(8,128)(2,1)}, u32[]{:S(2)}, u32[]{:S(2)}) collective-permute-start(bf16[512,512]{1,0:T(8,128)(2,1)} %pack_kv.4.r_5_), channel_id=1, source_target_pairs={{0,2},{4,6},{8,10},{12,14},{16,18},{20,22},{24,26},{28,30},{1,3},{... | collective-permute-start | bytes 1572872 | tf_op jit(solution)/shard_map/ppermute | solution.py:210
  52.7 44.9 %collective-permute-start.5 = (bf16[512,512]{1,0:T(8,128)(2,1)}, bf16[512,512]{1,0:T(8,128)(2,1)}, u32[]{:S(2)}, u32[]{:S(2)}) collective-permute-start(bf16[512,512]{1,0:T(8,128)(2,1)} %collective-permute-done.4.r_8_), channel_id=1, source_target_pairs={{2,0},{6,4},{10,8},{14,12},{18,16},{22,20},{26,24},{30,28},{3,1},{... | collective-permute-start | bytes 1572872 | tf_op jit(solution)/shard_map/ppermute | solution.py:212
  54.0 64.6 %collective-permute-start.2 = (bf16[512,512]{1,0:T(8,128)(2,1)}, bf16[512,512]{1,0:T(8,128)(2,1)}, u32[]{:S(2)}, u32[]{:S(2)}) collective-permute-start(bf16[512,512]{1,0:T(8,128)(2,1)} %collective-permute-done.1.r_8_), channel_id=1, source_target_pairs={{2,0},{6,4},{10,8},{14,12},{18,16},{22,20},{26,24},{30,28},{3,1},{... | collective-permute-start | bytes 1572872 | tf_op jit(solution)/shard_map/ppermute | solution.py:212
  57.5 22.6 %copy-start.5 = (bf16[512,512]{1,0:T(8,128)(2,1)S(1)}, bf16[512,512]{1,0:T(8,128)(2,1)}, u32[]{:S(2)}) copy-start(bf16[512,512]{1,0:T(8,128)(2,1)} %pack_kv.6.r_5_) | copy-start | bytes 1572868
  75.8 59.5 %collective-permute-start.18 = (bf16[512,512]{1,0:T(8,128)(2,1)}, bf16[512,512]{1,0:T(8,128)(2,1)}, u32[]{:S(2)}, u32[]{:S(2)}) collective-permute-start(bf16[512,512]{1,0:T(8,128)(2,1)} %get-tuple-element.51), channel_id=1, source_target_pairs={{0,2},{2,0},{4,6},{6,4},{8,10},{10,8},{12,14},{14,12},{16,18},{18,... | collective-permute-start | bytes 1572872 | tf_op jit(solution)/shard_map/ppermute | solution.py:235
  97.6 41.4 %collective-permute-start.16 = (bf16[512,512]{1,0:T(8,128)(2,1)}, bf16[512,512]{1,0:T(8,128)(2,1)}, u32[]{:S(2)}, u32[]{:S(2)}) collective-permute-start(bf16[512,512]{1,0:T(8,128)(2,1)} %get-tuple-element.48), channel_id=1, source_target_pairs={{0,2},{2,0},{4,6},{6,4},{8,10},{10,8},{12,14},{14,12},{16,18},{18,... | collective-permute-start | bytes 1572872 | tf_op jit(solution)/shard_map/ppermute | solution.py:235
  99.3 19.4 %copy-start.3 = (bf16[512,512]{1,0:T(8,128)(2,1)S(1)}, bf16[512,512]{1,0:T(8,128)(2,1)}, u32[]{:S(2)}) copy-start(bf16[512,512]{1,0:T(8,128)(2,1)} %pack_kv.4.r_5_) | copy-start | bytes 1572868
  116.7 24.8 %collective-permute-start.14 = (bf16[512,512]{1,0:T(8,128)(2,1)S(1)}, bf16[512,512]{1,0:T(8,128)(2,1)S(1)}, u32[]{:S(2)}, u32[]{:S(2)}) collective-permute-start(bf16[512,512]{1,0:T(8,128)(2,1)S(1)} %get-tuple-element.45), channel_id=1, source_target_pairs={{0,2},{2,0},{4,6},{6,4},{8,10},{10,8},{12,14},{14,12},{16,18},{18,... | collective-permute-start | bytes 1572872 | tf_op jit(solution)/shard_map/ppermute | solution.py:235
  118.7 16.7 %copy-start.12 = (bf16[512,512]{1,0:T(8,128)(2,1)S(1)}, bf16[512,512]{1,0:T(8,128)(2,1)}, u32[]{:S(2)}) copy-start(bf16[512,512]{1,0:T(8,128)(2,1)} %copy-done.11) | copy-start | bytes 1572868
  135.2 6.6 %copy-start.10 = (f32[512,512]{1,0:T(8,128)}, f32[512,512]{1,0:T(8,128)S(1)}, u32[]{:S(2)}) copy-start(f32[512,512]{1,0:T(8,128)S(1)} %get-tuple-element.41.own_ref) | copy-start | bytes 3145732
  135.2 11.7 %collective-permute-start.12 = (bf16[512,512]{1,0:T(8,128)(2,1)S(1)}, bf16[512,512]{1,0:T(8,128)(2,1)S(1)}, u32[]{:S(2)}, u32[]{:S(2)}) collective-permute-start(bf16[512,512]{1,0:T(8,128)(2,1)S(1)} %get-tuple-element.42), channel_id=1, source_target_pairs={{0,2},{2,0},{4,6},{6,4},{8,10},{10,8},{12,14},{14,12},{16,18},{18,... | collective-permute-start | bytes 1572872 | tf_op jit(solution)/shard_map/ppermute | solution.py:235
  137.5 84.7 %collective-permute-start.19 = (bf16[512,512]{1,0:T(8,128)(2,1)}, bf16[512,512]{1,0:T(8,128)(2,1)S(1)}, u32[]{:S(2)}, u32[]{:S(2)}) collective-permute-start(bf16[512,512]{1,0:T(8,128)(2,1)} %fusion.3), channel_id=1, source_target_pairs={{4,0},{6,2},{8,4},{10,6},{12,8},{14,10},{16,12},{18,14},{20,16},{2... | collective-permute-start | bytes 1572872 | tf_op jit(solution)/shard_map/ppermute | solution.py:237
  139.0 9.3 %copy-start.18 = (f32[128]{0:T(128)S(1)}, f32[128]{0:T(128)}, u32[]{:S(2)}) copy-start(f32[128]{0:T(128)} %param.13) | copy-start | bytes 1540
  140.2 85.4 %collective-permute-start.17 = (bf16[512,512]{1,0:T(8,128)(2,1)S(1)}, bf16[512,512]{1,0:T(8,128)(2,1)}, u32[]{:S(2)}, u32[]{:S(2)}) collective-permute-start(bf16[512,512]{1,0:T(8,128)(2,1)S(1)} %fusion.2), channel_id=1, source_target_pairs={{4,0},{6,2},{8,4},{10,6},{12,8},{14,10},{16,12},{18,14},{20,16},{2... | collective-permute-start | bytes 1572872 | tf_op jit(solution)/shard_map/ppermute | solution.py:237
  141.5 5.5 %copy-start.13 = (bf16[512,512]{1,0:T(8,128)(2,1)}, bf16[512,512]{1,0:T(8,128)(2,1)S(1)}, u32[]{:S(2)}) copy-start(bf16[512,512]{1,0:T(8,128)(2,1)S(1)} %collective-permute-done.14.x_ref) | copy-start | bytes 1572868
  141.7 86.4 %collective-permute-start.15 = (bf16[512,512]{1,0:T(8,128)(2,1)S(1)}, bf16[512,512]{1,0:T(8,128)(2,1)}, u32[]{:S(2)}, u32[]{:S(2)}) collective-permute-start(bf16[512,512]{1,0:T(8,128)(2,1)S(1)} %fusion.1), channel_id=1, source_target_pairs={{4,0},{6,2},{8,4},{10,6},{12,8},{14,10},{16,12},{18,14},{20,16},{2... | collective-permute-start | bytes 1572872 | tf_op jit(solution)/shard_map/ppermute | solution.py:237
  146.8 78.7 %copy-start.14 = (bf16[512,512]{1,0:T(8,128)(2,1)}, bf16[512,512]{1,0:T(8,128)(2,1)S(1)}, u32[]{:S(2)}) copy-start(bf16[512,512]{1,0:T(8,128)(2,1)S(1)} %collective-permute-done.12.x_ref) | copy-start | bytes 1572868
  147.0 83.7 %collective-permute-start.13 = (bf16[512,512]{1,0:T(8,128)(2,1)S(1)}, bf16[512,512]{1,0:T(8,128)(2,1)S(1)}, u32[]{:S(2)}, u32[]{:S(2)}) collective-permute-start(bf16[512,512]{1,0:T(8,128)(2,1)S(1)} %fusion), channel_id=1, source_target_pairs={{4,0},{6,2},{8,4},{10,6},{12,8},{14,10},{16,12},{18,14},{20,16},{2... | collective-permute-start | bytes 1572872 | tf_op jit(solution)/shard_map/ppermute | solution.py:237
  (8 other events, 8.6 us)

commit v2 on v1

v2 whole, which is shorter than its diff:
```python
import functools
import math

import jax
import jax.numpy as jnp
from jax import lax
from jax.experimental import pallas as pl
from jax.experimental.pallas import tpu as pltpu
from jax.sharding import PartitionSpec as P

Q_HEADS = 32
KV_HEADS = 16
W = 1024
QUERY_SCALE = 168
EPS = 1e-06
CHUNKS = (2, 2, 2, 2)
GATE = 1
GATE2 = 1
D=128
BF=jnp.bfloat16
F32=jnp.float32
NT=(((1,),(1,)),((),()))
NN=(((1,),(0,)),((),()))
ORDER="half"
ACC="rmw"
def dotf(a,b,dims):
    return lax.dot_general(a,b,dims,preferred_element_type=F32)

def attn_body(T, rows, par_ref, lo_ref, gq_ref, q_ref, g_ref, own_ref, h1a_ref, h1b_ref, h2_ref,
              qg_ref, own_out, r1_out, r2_out, qgain_ref, kgain_ref,
              near, kt, s_s, dp_s, w_s, ds_s, dk_acc, dv_acc):
    h = pl.program_id(0)
    nq = rows // T
    nb = 2 * nq + 1
    @pl.when(par_ref[0] == 1)
    def _(): near[...] = h1a_ref[...]
    @pl.when(par_ref[0] == 0)
    def _(): near[...] = h1b_ref[...]
    @pl.when(h == 0)
    def _():
        qgain_ref[...] = jnp.zeros_like(qgain_ref); kgain_ref[...] = jnp.zeros_like(kgain_ref)
    kv = [h2_ref, near, own_ref]
    def kk(j): return kv[j//nq][(j%nq)*T:(j%nq+1)*T, :D]
    def vv(j): return kv[j//nq][(j%nq)*T:(j%nq+1)*T, D:]
    for p in range(3):
        kt[:, p*rows:(p+1)*rows] = kv[p][:, :D].T
    gq = gq_ref[...]
    iota = lax.broadcasted_iota(jnp.int32, (T, 2*T), 0)
    lane = lax.broadcasted_iota(jnp.int32, (T, 2*T), 1)
    tok = jnp.where(lane >= T, lane - T, lane)
    def fold(x, op):
        return op(x.reshape(T//8, 8, 2*T), axis=0)
    st = [dict() for _ in range(nq)]
    def sl(kb): return slice(kb*T, (kb+1)*T)
    def p0(i):
        t = st[i]
        r = slice(i*T, (i+1)*T)
        qf = jnp.concatenate([q_ref[r, :D].T, q_ref[r, D:].T], axis=1).astype(F32)
        t["inv"] = lax.rsqrt(jnp.mean(qf*qf, axis=0, keepdims=True) + 1e-6)
        unit = qf * t["inv"]
        t["unit"] = unit
        t["qt"] = (unit * gq).astype(BF)
        t["gt"] = jnp.concatenate([g_ref[r, :D].T, g_ref[r, D:].T], axis=1)
        lo = lo_ref[:, r] - i*T
        t["lo"] = jnp.concatenate([lo, lo], axis=1)
        yield
    def p1(i):
        t = st[i]; b = i % 2; m8 = None
        for kb in range(nb):
            s = dotf(kk(i+kb), t["qt"], NN)
            see = iota >= t["lo"] - kb*T
            if kb == nb-1: see = see & (iota <= tok)
            s = jnp.where(see, s, -1e30)
            s_s[b, sl(kb)] = s
            f = fold(s, jnp.max)
            m8 = f if m8 is None else jnp.maximum(m8, f)
            yield
        t["m"] = jnp.max(m8, axis=0, keepdims=True)
    def p2(i):
        t = st[i]; b = i % 2; l8 = None
        for kb in range(nb):
            e = jnp.exp(s_s[b, sl(kb)] - t["m"])
            s_s[b, sl(kb)] = e
            f = fold(e, jnp.sum)
            l8 = f if l8 is None else l8 + f
            dp_s[b, sl(kb)] = dotf(vv(i+kb), t["gt"], NN)
            yield
        t["il"] = 1.0 / jnp.sum(l8, axis=0, keepdims=True)
    def acc(ref, first, j, val):
        r = slice(j*T, (j+1)*T)
        if first: ref[r] = val
        else: ref[r] = ref[r] + val
    def p3(i):
        t = st[i]; b = i % 2; d8 = None
        for kb in range(nb):
            w = (s_s[b, sl(kb)] * t["il"]).astype(BF)
            f = fold(w.astype(F32) * dp_s[b, sl(kb)], jnp.sum)
            d8 = f if d8 is None else d8 + f
            if ACC == "rmw":
                acc(dv_acc, i == 0 or kb == nb-1, i+kb, dotf(w, t["gt"], NT))
            yield
        t["delta"] = jnp.sum(d8, axis=0, keepdims=True)
    def p4(i):
        t = st[i]; b = i % 2
        for kb in range(nb):
            p = s_s[b, sl(kb)] * t["il"]
            ds = (p * (dp_s[b, sl(kb)] - t["delta"])).astype(BF)
            ds_s[b, sl(kb)] = ds
            acc(dk_acc, i == 0 or kb == nb-1, i+kb, dotf(ds, t["qt"], NT))
            yield
    def p5(i):
        t = st[i]; b = i % 2
        dq = dotf(kt[:, i*T:(i+nb)*T], ds_s[b], NN)
        qgain_ref[...] += dq * t["unit"]
        up = dq * gq
        mean = jnp.mean(up * t["unit"], axis=0, keepdims=True)
        qr = (t["inv"] * (up - t["unit"] * mean)).astype(BF)
        r = slice(i*T, (i+1)*T)
        qg_ref[r, :D] = qr[:, :T].T
        qg_ref[r, D:] = qr[:, T:].T
        yield
    def run(*gens):
        gens = list(gens)
        while gens:
            for g in list(gens):
                try: next(g)
                except StopIteration: gens.remove(g)
    def chain(*gs):
        for g in gs: yield from g
    if ORDER == "seq":
        for i in range(nq):
            run(chain(p0(i), p1(i), p2(i), p3(i), p4(i), p5(i)))
    elif ORDER == "half":
        run(chain(p0(0), p1(0), p2(0)))
        for i in range(nq):
            nxt = [chain(p0(i+1), p1(i+1), p2(i+1))] if i+1 < nq else []
            run(chain(p3(i), p4(i), p5(i)), *nxt)
    elif ORDER == "pair":
        for i in range(0, nq, 2):
            run(chain(p0(i), p1(i), p2(i), p3(i), p4(i), p5(i)), chain(p0(i+1), p1(i+1), p2(i+1), p3(i+1), p4(i+1), p5(i+1)))
    own_out[:, :D] = dk_acc[2*rows:]; own_out[:, D:] = dv_acc[2*rows:]
    r1_out[:, :D] = dk_acc[rows:2*rows].astype(BF); r1_out[:, D:] = dv_acc[rows:2*rows].astype(BF)
    r2_out[:, :D] = dk_acc[:rows].astype(BF); r2_out[:, D:] = dv_acc[:rows].astype(BF)
    kg = None
    for p in range(3):
        f = jnp.sum((dk_acc[p*rows:(p+1)*rows] * kv[p][:, :D].astype(F32)).reshape(-1, 8, D), axis=0)
        kg = f if kg is None else kg + f
    kgain_ref[...] += kg

def attn(par, lo, gq, q, g, own, h1a, h1b, h2, off, hc, qg_prev=None):
    rows = q.shape[0]; T = 128
    win = 2*rows + T
    kvs = pl.BlockSpec((rows, 2*D), lambda h: (0, h))
    qs = pl.BlockSpec((rows, 2*D), lambda h: (0, off+h))
    in_specs=[pl.BlockSpec(memory_space=pltpu.SMEM),
              pl.BlockSpec((1,rows), lambda h:(0,0)),
              pl.BlockSpec((D,1), lambda h:(0,0)),
              qs, qs, kvs,kvs,kvs,kvs]
    args=[par,lo,gq,q,g,own,h1a,h1b,h2]
    body = functools.partial(attn_body, T, rows)
    alias={}
    if qg_prev is not None:
        in_specs.append(pl.BlockSpec(memory_space=pl.ANY)); args.append(qg_prev); alias={9:0}
        inner = body
        body = lambda *r: inner(*r[:9], *r[10:])
    return pl.pallas_call(body, grid=(hc,), in_specs=in_specs,
        out_specs=[qs, kvs,kvs,kvs,
                   pl.BlockSpec((D,2*T), lambda h:(0,0)), pl.BlockSpec((8,D), lambda h:(0,0))],
        out_shape=[jax.ShapeDtypeStruct(q.shape,BF), jax.ShapeDtypeStruct((rows,hc*2*D),F32),
                   jax.ShapeDtypeStruct((rows,hc*2*D),BF), jax.ShapeDtypeStruct((rows,hc*2*D),BF),
                   jax.ShapeDtypeStruct((D,2*T),F32), jax.ShapeDtypeStruct((8,D),F32)],
        scratch_shapes=[pltpu.VMEM((rows,2*D),BF),pltpu.VMEM((D,3*rows),BF),
            pltpu.VMEM((2,win,2*T),F32),pltpu.VMEM((2,win,2*T),F32),pltpu.VMEM((16,128),BF),pltpu.VMEM((2,win,2*T),BF),
            pltpu.VMEM((3*rows,D),F32),pltpu.VMEM((3*rows,D),F32)],
        input_output_aliases=alias,
        cost_estimate=pl.CostEstimate(flops=hc*6*10**9, bytes_accessed=hc*rows*D*24, transcendentals=0),
        compiler_params=pltpu.CompilerParams(dimension_semantics=("arbitrary",), vmem_limit_bytes=60*1024*1024),
        name="attn_grad")(*args)


def pack_body(chunks, k_ref, v_ref, gain_ref, *outs):
    h = pl.program_id(0)
    k = k_ref[...].astype(F32)
    inv = lax.rsqrt(jnp.mean(k*k, axis=1, keepdims=True) + EPS)
    k = (k * inv * gain_ref[...]).astype(BF)
    at = 0
    for hc, out in zip(chunks, outs):
        @pl.when((h >= at) & (h < at + hc))
        def _(out=out):
            out[:, :D] = k
            out[:, D:] = v_ref[...]
        at += hc


def pack(k_raw, values, k_gain, off, chunks):
    rows = k_raw.shape[0]
    cb = [pl.BlockSpec((rows, D), lambda h: (0, off + h))] * 2
    outs, at = [], 0
    for hc in chunks:
        outs.append(pl.BlockSpec((rows, 2*D), lambda h, at=at, hc=hc: (0, jnp.clip(h - at, 0, hc - 1))))
        at += hc
    return pl.pallas_call(
        functools.partial(pack_body, chunks), grid=(at,),
        in_specs=cb + [pl.BlockSpec((1, D), lambda h: (0, 0))],
        out_specs=outs,
        out_shape=[jax.ShapeDtypeStruct((rows, hc*2*D), BF) for hc in chunks],
        cost_estimate=pl.CostEstimate(flops=at*10**9, bytes_accessed=at*rows*D*8, transcendentals=0),
        name="pack_kv")(k_raw, values, k_gain)


def finish_body(par_ref, own_ref, x_ref, y_ref, k_ref, gain_ref, *refs):
    kg_ref, vg_ref = refs[-2:]
    even = jnp.where(par_ref[0] == 0, 1.0, 0.0)
    t = own_ref[...] + y_ref[...].astype(F32) + x_ref[...].astype(F32) * even
    vg_ref[...] = t[:, D:].astype(BF)
    k = k_ref[...].astype(F32)
    inv = lax.rsqrt(jnp.mean(k*k, axis=1, keepdims=True) + EPS)
    unit = k * inv
    up = t[:, :D] * gain_ref[...]
    kg_ref[...] = (inv * (up - unit * jnp.mean(up * unit, axis=1, keepdims=True))).astype(BF)


def finish(par, own, x, y, k_raw, k_gain, off, hc, prev):
    rows = own.shape[0]
    kvs = pl.BlockSpec((rows, 2*D), lambda h: (0, h))
    cb = pl.BlockSpec((rows, D), lambda h: (0, off + h))
    in_specs = [pl.BlockSpec(memory_space=pltpu.SMEM), kvs, kvs, kvs, cb, pl.BlockSpec((1, D), lambda h: (0, 0))]
    args = [par, own, x, y, k_raw, k_gain]
    alias = {}
    if prev is not None:
        in_specs += [pl.BlockSpec(memory_space=pl.ANY)] * 2
        args += list(prev)
        alias = {6: 0, 7: 1}
    return pl.pallas_call(
        finish_body, grid=(hc,), in_specs=in_specs, out_specs=[cb, cb],
        out_shape=[jax.ShapeDtypeStruct(k_raw.shape, BF)] * 2,
        cost_estimate=pl.CostEstimate(flops=hc*10**9, bytes_accessed=hc*rows*D*8, transcendentals=0),
        input_output_aliases=alias, name="finish_kv")(*args)


def move(value, pairs, name):
    with jax.named_scope(name):
        return lax.ppermute(value, "ctx", pairs)


def after(value, *others):
    return lax.optimization_barrier((value,) + others)[0]


def sum_all(x):
    for name in ("head", "ctx"):
        count = lax.axis_size(name)
        if count & (count - 1):
            x = lax.psum(x, name)
            continue
        step = 1
        while step < count:
            x = x + lax.ppermute(x, name, [(i, i ^ step) for i in range(count)])
            step *= 2
    return x


def on_device(q_raw, k_raw, values, d_out, doc_ids, q_gain, k_gain):
    rows = q_raw.shape[0]
    kv_local = k_raw.shape[1] // D
    count = lax.axis_size("ctx")
    assert 2 * rows == W and count % 2 == 0 and q_raw.shape[1] == 2 * k_raw.shape[1]
    chunks = CHUNKS if kv_local == sum(CHUNKS) else (1,) * kv_local
    factor = QUERY_SCALE ** (-0.5)
    me = lax.axis_index("ctx")
    par = (me % 2).astype(jnp.int32).reshape(1)
    onward = [(i, i + 2) for i in range(count - 2)]
    back = [(i + 2, i) for i in range(count - 2)]
    swap = [(i, i ^ 1) for i in range(count)]
    up = [(i, i + 1) for i in range(0, count, 2)]
    down = [(i + 1, i) for i in range(0, count, 2)]

    gk = k_gain.reshape(1, D)
    n = len(chunks)
    own = list(pack(k_raw, values, gk, 0, chunks[:1])) + list(pack(k_raw, values, gk, chunks[0], chunks[1:]))
    far, near_a, near_b = [None] * n, [None] * n, [None] * n
    for c in range(n):
        far[c] = move(own[c], onward, f"far{c}")
        near_a[c] = move(own[c], up, f"up{c}")
        near_b[c] = move(far[c], down, f"relay{c}")

    padded = jnp.concatenate([jnp.full((W,), -1, jnp.int32), doc_ids])
    span_ids = lax.dynamic_slice_in_dim(padded, me * rows, W + rows)
    q_ids = span_ids[W:]
    first = jnp.sum((span_ids[:, None] < q_ids[None, :]).astype(jnp.int32), axis=0)
    lo = jnp.maximum(first, jnp.arange(1, rows + 1, dtype=jnp.int32)).reshape(1, rows)
    gq = (q_gain * factor).reshape(D, 1)

    offs = [sum(chunks[:c]) for c in range(n)]
    qg = None
    mine, r1, r2, qs, kss, xs, ys = [], [], [], [], [], [], []

    def give(c, last):
        t = after(r2[c], last)
        both = (t.astype(F32) + xs[c].astype(F32)).astype(BF)
        t = jnp.where(par[0] == 1, both, t)
        ys.append(move(t, back, f"ret{c}"))
        return t

    tok = par
    for c in range(n):
        if c >= 2:
            tok = after(tok, give(c - 2, kss[c - 1]))
        if c >= 3:
            tok, ys[c - 3] = lax.optimization_barrier((tok, ys[c - 3]))
        qg, o, a, b, s, t = attn(tok, lo, gq, q_raw, d_out, own[c], near_a[c], near_b[c], far[c], offs[c], chunks[c], qg)
        mine.append(o); r1.append(a); r2.append(b); qs.append(s); kss.append(t)
        xs.append(move(r1[c], swap, f"swap{c}"))
    out = None
    give(n - 2, kss[n - 1])
    for c in range(n - 2):
        out = finish(after(par, ys[n - 2] if False else kss[n - 1]), mine[c], xs[c], ys[c], k_raw, gk, offs[c], chunks[c], out)
    t = give(n - 1, kss[n - 1] if GATE == 0 or out is None else out[0])
    q_part = jnp.sum(sum(qs), axis=1) * factor
    k_part = jnp.sum(sum(kss), axis=0) / k_gain
    gains = jnp.stack([q_part, k_part])
    if GATE2:
        gains = after(gains, t)
    gains = sum_all(gains)
    for c in range(n - 2, n):
        out = finish(par, mine[c], xs[c], ys[c], k_raw, gk, offs[c], chunks[c], out)
    total = rows * count
    return (qg, out[0], out[1], gains[0] / math.sqrt(total * Q_HEADS), gains[1] / math.sqrt(total * KV_HEADS))


def solution(mesh):
    split = P("ctx", "head")
    return jax.shard_map(
        on_device,
        mesh=mesh,
        in_specs=(split, split, split, split, P(), P(), P()),
        out_specs=(split, split, split, P(), P()),
        check_vma=False,
    )
```

time: 235 us -> 165 us (0.70)
  blocking collectives: 73.4 us -> 0 us
  waiting for transfers between devices: 11.2 us -> 31.7 us
  Pallas kernels: 84.3 us -> 64.6 us
  starting transfers between devices: 50.5 us -> 61.1 us
  local copies, waits for them, and re-layouts: 8.87 us -> 3.38 us
  other arithmetic: 4.75 us -> 2.32 us
    psum x1 -> x0, blocking collectives: 73.4 us -> none  [on_device(): gains = lax.psum(jnp.stack([q_part, k_part]), ('ctx', 'head'))]
    ppermute x20 -> x25, waiting for transfers between devices: 11.2 us -> 31.7 us  [the longest x20 23.1 us: move(): return lax.ppermute(value, 'ctx', pairs)]
    pallas_call x8 -> x6, Pallas kernels: 74.2 us -> 54.5 us  [the longest x4 47.1 us: attn(): pl.pallas_call(body, grid=(hc,), in_specs=in_specs, out_specs=[qs, kvs, k...]
    ppermute x20 -> x25, starting transfers between devices: 50.5 us -> 61.1 us  [the longest x20 48.6 us: move(): return lax.ppermute(value, 'ctx', pairs)]
    unnamed x40 -> x58, local copies, waits for them, and re-layouts: 8.59 us -> 2.47 us
    select_n x4, other arithmetic: 3.68 us -> 0.64 us  [give(): t = jnp.where(par[0] == 1, both, t)]
  transfers between devices with their start and end apart: 20 -> 25, of which waited for: 3 -> 7; matrix products, arithmetic and copies ran while one was open for 2% -> 2% of each run, Pallas kernels for 34% -> 36%
where the time goes in v2:
time: 165 us; the launch traced here: 164 us
  Pallas kernels  64.6 us (39%)
  starting transfers between devices  61.1 us (37%)
  waiting for transfers between devices  31.7 us (19%)
  local copies, waits for them, and re-layouts  3.38 us (2%)
  other arithmetic  2.32 us (1%)
    ppermute x20, starting transfers between devices, move(): return lax.ppermute(value, 'ctx', pairs)  48.6 us
    pallas_call x4, Pallas kernels, attn(): pl.pallas_call(body, grid=(hc,), in_specs=in_specs, out_specs=[qs, kvs, k...  47.1 us
    ppermute x20, waiting for transfers between devices, move(): return lax.ppermute(value, 'ctx', pairs)  23.1 us
    ppermute x5, starting transfers between devices, sum_all(): x = x + lax.ppermute(x, name, [(i, i ^ step) for i in range(count)])  12.5 us
    pallas_call x4, Pallas kernels, finish(): pl.pallas_call(finish_body, grid=(hc,), in_specs=in_specs, out_specs=[cb,...  10.1 us
    ppermute x5, waiting for transfers between devices, sum_all(): x = x + lax.ppermute(x, name, [(i, i ^ step) for i in range(count)])  8.6 us
    pallas_call x2, Pallas kernels, pack(): pl.pallas_call(functools.partial(pack_body, chunks), grid=(at,), in_specs...  7.4 us
  transfers between devices with their start and end apart: 25, of which 7 were waited for; matrix products, arithmetic and copies ran while one was open for 2% of the time, Pallas kernels for 36%

profile of v2, /device:TPU:0, one launch (start us, length us, event | category | flops | bytes accessed | tf_op | source)
XLA Modules:
  0.0 164.4 jit_solution(961166693735421302)
XLA Ops:
  0.6 2.1 %pack_kv.2.own_ref = bf16[512,512]{1,0:T(8,128)(2,1)} custom-call(bf16[512,1024]{1,0:T(8,128)(2,1)} %k_ref.11, bf16[512,1024]{1,0:T(8,128)(2,1)} %v_ref.3, f32[1,128]{1,0:T(1,128)} %bitcast.14), custom_call_target="tpu_custom_call" | custom-call | flops 2000000000 | bytes 1048576 | tf_op jit(solution)/shard_map/pack_kv/pallas_call | solution.py:202
  2.8 5.0 %collective-permute-start.1 = (bf16[512,512]{1,0:T(8,128)(2,1)}, bf16[512,512]{1,0:T(8,128)(2,1)S(1)}, u32[]{:S(2)}, u32[]{:S(2)}) collective-permute-start(bf16[512,512]{1,0:T(8,128)(2,1)} %pack_kv.2.own_ref), channel_id=1, source_target_pairs={{0,4},{2,6},{4,8},{6,10},{8,12},{10,14},{12,16},{14,18},{16,20},{1... | collective-permute-start | bytes 1572872 | tf_op jit(solution)/shard_map/far0/ppermute | solution.py:243
  7.8 3.4 %collective-permute-start = (bf16[512,512]{1,0:T(8,128)(2,1)}, bf16[512,512]{1,0:T(8,128)(2,1)S(1)}, u32[]{:S(2)}, u32[]{:S(2)}) collective-permute-start(bf16[512,512]{1,0:T(8,128)(2,1)} %pack_kv.2.own_ref), channel_id=1, source_target_pairs={{0,2},{4,6},{8,10},{12,14},{16,18},{20,22},{24,26},{28,30},{1,3},{... | collective-permute-start | bytes 1572872 | tf_op jit(solution)/shard_map/up0/ppermute | solution.py:243
  11.2 5.3 %pack_kv.3 = (bf16[512,512]{1,0:T(8,128)(2,1)}, bf16[512,512]{1,0:T(8,128)(2,1)}, bf16[512,512]{1,0:T(8,128)(2,1)}) custom-call(bf16[512,1024]{1,0:T(8,128)(2,1)} %k_ref.11, bf16[512,1024]{1,0:T(8,128)(2,1)} %v_ref.3, f32[1,128]{1,0:T(1,128)} %bitcast.15), custom_call_target="tpu_custom_call" | custom-call | flops 6000000000 | bytes 3145728 | tf_op jit(solution)/shard_map/pack_kv/pallas_call | solution.py:202
  16.5 3.4 %collective-permute-start.4 = (bf16[512,512]{1,0:T(8,128)(2,1)}, bf16[512,512]{1,0:T(8,128)(2,1)S(1)}, u32[]{:S(2)}, u32[]{:S(2)}) collective-permute-start(bf16[512,512]{1,0:T(8,128)(2,1)} %get-tuple-element.51.r_5_), channel_id=1, source_target_pairs={{0,4},{2,6},{4,8},{6,10},{8,12},{10,14},{12,16},{14,18},{16,20},{1... | collective-permute-start | bytes 1572872 | tf_op jit(solution)/shard_map/far1/ppermute | solution.py:243
  19.9 1.3 collective-permute-start.3
  21.3 3.4 %collective-permute-start.8 = (bf16[512,512]{1,0:T(8,128)(2,1)}, bf16[512,512]{1,0:T(8,128)(2,1)S(1)}, u32[]{:S(2)}, u32[]{:S(2)}) collective-permute-start(bf16[512,512]{1,0:T(8,128)(2,1)} %get-tuple-element.58.r_5_), channel_id=1, source_target_pairs={{0,4},{2,6},{4,8},{6,10},{8,12},{10,14},{12,16},{14,18},{16,20},{1... | collective-permute-start | bytes 1572872 | tf_op jit(solution)/shard_map/far2/ppermute | solution.py:243
  27.9 5.4 %collective-permute-start.7 = (bf16[512,512]{1,0:T(8,128)(2,1)}, bf16[512,512]{1,0:T(8,128)(2,1)}, u32[]{:S(2)}, u32[]{:S(2)}) collective-permute-start(bf16[512,512]{1,0:T(8,128)(2,1)} %get-tuple-element.58.r_5_), channel_id=1, source_target_pairs={{0,2},{4,6},{8,10},{12,14},{16,18},{20,22},{24,26},{28,30},{1,3},{... | collective-permute-start | bytes 1572872 | tf_op jit(solution)/shard_map/up2/ppermute | solution.py:243
  33.3 4.3 %collective-permute-start.13 = (bf16[512,512]{1,0:T(8,128)(2,1)}, bf16[512,512]{1,0:T(8,128)(2,1)}, u32[]{:S(2)}, u32[]{:S(2)}) collective-permute-start(bf16[512,512]{1,0:T(8,128)(2,1)} %get-tuple-element.65.r_5_), channel_id=1, source_target_pairs={{0,4},{2,6},{4,8},{6,10},{8,12},{10,14},{12,16},{14,18},{16,20},{1... | collective-permute-start | bytes 1572872 | tf_op jit(solution)/shard_map/far3/ppermute | solution.py:243
  37.7 1.5 collective-permute-done.2.h1b_ref
  40.5 11.7 %attn_grad.4 = (bf16[512,2048]{1,0:T(8,128)(2,1)}, f32[512,512]{1,0:T(8,128)}, bf16[512,512]{1,0:T(8,128)(2,1)}, bf16[512,512]{1,0:T(8,128)(2,1)}, f32[128,256]{1,0:T(8,128)}, /*index=5*/f32[8,128]{1,0:T(8,128)}) custom-call(s32[1]{0:T(128)} %bitcast.par_ref.r_0_, s32[1,512]{1,0:T(1,128)} %add_maximum_fusion.lo_ref.r_1_, f32[128,1]{1,0:T(8,128)} %copy.25.gq_ref.r_2_, ...), custom_call_target="tpu_custom_call" | custom-call | flops 12000000000 | bytes 3145728 | tf_op jit(solution)/shard_map/attn_grad/pallas_call | solution.py:166
  52.2 5.4 %collective-permute-start.12 = (bf16[512,512]{1,0:T(8,128)(2,1)S(1)}, bf16[512,512]{1,0:T(8,128)(2,1)S(1)}, u32[]{:S(2)}, u32[]{:S(2)}) collective-permute-start(bf16[512,512]{1,0:T(8,128)(2,1)S(1)} %copy-done.18), channel_id=1, source_target_pairs={{0,2},{4,6},{8,10},{12,14},{16,18},{20,22},{24,26},{28,30},{1,3},{... | collective-permute-start | bytes 1572872 | tf_op jit(solution)/shard_map/up3/ppermute | solution.py:243
  58.9 1.5 collective-permute-start.14
  60.4 4.0 %collective-permute-start.6 = (bf16[512,512]{1,0:T(8,128)(2,1)}, bf16[512,512]{1,0:T(8,128)(2,1)S(1)}, u32[]{:S(2)}, u32[]{:S(2)}) collective-permute-start(bf16[512,512]{1,0:T(8,128)(2,1)} %get-tuple-element.55), channel_id=1, source_target_pairs={{0,2},{2,0},{4,6},{6,4},{8,10},{10,8},{12,14},{14,12},{16,18},{18,... | collective-permute-start | bytes 1572872 | tf_op jit(solution)/shard_map/swap0/ppermute | solution.py:243
  64.4 11.8 %attn_grad.5 = (bf16[512,2048]{1,0:T(8,128)(2,1)}, f32[512,512]{1,0:T(8,128)}, bf16[512,512]{1,0:T(8,128)(2,1)}, bf16[512,512]{1,0:T(8,128)(2,1)}, f32[128,256]{1,0:T(8,128)}, /*index=5*/f32[8,128]{1,0:T(8,128)}) custom-call(s32[1]{0:T(128)} %bitcast.par_ref.r_0_, s32[1,512]{1,0:T(1,128)} %add_maximum_fusion.lo_ref.r_1_, ...), custom_call_target="tpu_custom_call", output_to_operand_aliasing={{0}: (9, {})} | custom-call | flops 12000000000 | bytes 3145728 | tf_op jit(solution)/shard_map/attn_grad/pallas_call | solution.py:166
  76.2 17.6 %collective-permute-done.6.x_ref = bf16[512,512]{1,0:T(8,128)(2,1)S(1)} collective-permute-done((bf16[512,512]{1,0:T(8,128)(2,1)}, bf16[512,512]{1,0:T(8,128)(2,1)S(1)}, u32[]{:S(2)}, u32[]{:S(2)}) %collective-permute-start.6) | collective-permute-done | bytes 524320 | tf_op jit(solution)/shard_map/swap0/ppermute | solution.py:243
  94.0 1.3 collective-permute-start.11
  95.3 11.9 %attn_grad.6 = (bf16[512,2048]{1,0:T(8,128)(2,1)}, f32[512,512]{1,0:T(8,128)}, bf16[512,512]{1,0:T(8,128)(2,1)}, bf16[512,512]{1,0:T(8,128)(2,1)}, f32[128,256]{1,0:T(8,128)}, /*index=5*/f32[8,128]{1,0:T(8,128)}) custom-call(s32[1]{0:T(128)} %bitcast.par_ref.r_0_, s32[1,512]{1,0:T(1,128)} %add_maximum_fusion.lo_ref.r_1_, ...), custom_call_target="tpu_custom_call", output_to_operand_aliasing={{0}: (9, {})} | custom-call | flops 12000000000 | bytes 3145728 | tf_op jit(solution)/shard_map/attn_grad/pallas_call | solution.py:166
  107.5 1.5 collective-permute-start.16
  109.0 2.1 %collective-permute-start.18 = (bf16[512,512]{1,0:T(8,128)(2,1)}, bf16[512,512]{1,0:T(8,128)(2,1)S(1)}, u32[]{:S(2)}, u32[]{:S(2)}) collective-permute-start(bf16[512,512]{1,0:T(8,128)(2,1)} %get-tuple-element.81), channel_id=1, source_target_pairs={{0,2},{2,0},{4,6},{6,4},{8,10},{10,8},{12,14},{14,12},{16,18},{18,... | collective-permute-start | bytes 1572872 | tf_op jit(solution)/shard_map/swap2/ppermute | solution.py:243
  111.9 11.8 %attn_grad.7 = (bf16[512,2048]{1,0:T(8,128)(2,1)}, f32[512,512]{1,0:T(8,128)}, bf16[512,512]{1,0:T(8,128)(2,1)}, bf16[512,512]{1,0:T(8,128)(2,1)}, f32[128,256]{1,0:T(8,128)}, /*index=5*/f32[8,128]{1,0:T(8,128)}) custom-call(s32[1]{0:T(128)} %bitcast.par_ref.r_0_, s32[1,512]{1,0:T(1,128)} %add_maximum_fusion.lo_ref.r_1_, ...), custom_call_target="tpu_custom_call", output_to_operand_aliasing={{0}: (9, {})} | custom-call | flops 12000000000 | bytes 3145728 | tf_op jit(solution)/shard_map/attn_grad/pallas_call | solution.py:166
  125.2 2.5 %finish_kv.4 = (bf16[512,1024]{1,0:T(8,128)(2,1)}, bf16[512,1024]{1,0:T(8,128)(2,1)}) custom-call(s32[1]{0:T(128)} %bitcast.par_ref.r_0_, f32[512,512]{1,0:T(8,128)} %get-tuple-element.74.own_ref, bf16[512,512]{1,0:T(8,128)(2,1)} %copy-done.2, bf16[512,512]{1,0:T(8,128)(2,1)} %collective-permute-done.11.y_ref, bf16[512,1024]{1,0:T(8,128)(2,1)} %k_ref.11, ...), custom_call_target="tpu_custom_call" | custom-call | flops 2000000000 | bytes 1048576 | tf_op jit(solution)/shard_map/finish_kv/pallas_call | solution.py:234
  127.9 2.6 %finish_kv.5 = (bf16[512,1024]{1,0:T(8,128)(2,1)}, bf16[512,1024]{1,0:T(8,128)(2,1)}) custom-call(s32[1]{0:T(128)} %bitcast.par_ref.r_0_, f32[512,512]{1,0:T(8,128)} %get-tuple-element.73.own_ref, bf16[512,512]{1,0:T(8,128)(2,1)} %copy-done.3, bf16[512,512]{1,0:T(8,128)(2,1)} %collective-permute-done.16.y_ref, ...), custom_call_target="tpu_custom_call", output_to_operand_aliasing={{0}: (6, {}), {1}: (7, {})} | custom-call | flops 2000000000 | bytes 1048576 | tf_op jit(solution)/shard_map/finish_kv/pallas_call | solution.py:234
  130.7 3.9 %collective-permute-done.15.x_ref = bf16[512,512]{1,0:T(8,128)(2,1)S(1)} collective-permute-done((bf16[512,512]{1,0:T(8,128)(2,1)}, bf16[512,512]{1,0:T(8,128)(2,1)S(1)}, u32[]{:S(2)}, u32[]{:S(2)}) %collective-permute-start.15) | collective-permute-done | bytes 524320 | tf_op jit(solution)/shard_map/swap3/ppermute | solution.py:243
  137.3 3.5 %collective-permute-done.21 = f32[2,128]{1,0:T(2,128)S(1)} collective-permute-done((f32[2,128]{1,0:T(2,128)S(1)}, f32[2,128]{1,0:T(2,128)S(1)}, u32[]{:S(2)}, u32[]{:S(2)}) %collective-permute-start.21) | collective-permute-done | bytes 1056 | tf_op jit(solution)/shard_map/ppermute | solution.py:258
  140.9 4.5 %collective-permute-start.22 = (f32[2,128]{1,0:T(2,128)S(1)}, f32[2,128]{1,0:T(2,128)S(1)}, u32[]{:S(2)}, u32[]{:S(2)}) collective-permute-start(f32[2,128]{1,0:T(2,128)S(1)} %add.82), channel_id=1, source_target_pairs={{0,4},{2,6},{4,0},{6,2},{8,12},{10,14},{12,8},{14,10},{16,20},{18,... | collective-permute-start | bytes 3080 | tf_op jit(solution)/shard_map/ppermute | solution.py:258
  145.4 2.4 %collective-permute-done.22 = f32[2,128]{1,0:T(2,128)S(1)} collective-permute-done((f32[2,128]{1,0:T(2,128)S(1)}, f32[2,128]{1,0:T(2,128)S(1)}, u32[]{:S(2)}, u32[]{:S(2)}) %collective-permute-start.22) | collective-permute-done | bytes 1056 | tf_op jit(solution)/shard_map/ppermute | solution.py:258
  147.8 3.5 %collective-permute-start.23 = (f32[2,128]{1,0:T(2,128)S(1)}, f32[2,128]{1,0:T(2,128)S(1)}, u32[]{:S(2)}, u32[]{:S(2)}) collective-permute-start(f32[2,128]{1,0:T(2,128)S(1)} %add.83), channel_id=1, source_target_pairs={{0,8},{2,10},{4,12},{6,14},{8,0},{10,2},{12,4},{14,6},{16,24},{18,... | collective-permute-start | bytes 3080 | tf_op jit(solution)/shard_map/ppermute | solution.py:258
  151.2 1.5 collective-permute-done.23
  152.8 4.4 %collective-permute-start.24 = (f32[2,128]{1,0:T(2,128)S(1)}, f32[2,128]{1,0:T(2,128)S(1)}, u32[]{:S(2)}, u32[]{:S(2)}) collective-permute-start(f32[2,128]{1,0:T(2,128)S(1)} %add.84), channel_id=1, source_target_pairs={{0,16},{2,18},{4,20},{6,22},{8,24},{10,26},{12,28},{14,30},{16,0},... | collective-permute-start | bytes 3080 | tf_op jit(solution)/shard_map/ppermute | solution.py:258
  158.0 2.5 %finish_kv.6 = (bf16[512,1024]{1,0:T(8,128)(2,1)}, bf16[512,1024]{1,0:T(8,128)(2,1)}) custom-call(s32[1]{0:T(128)} %bitcast.par_ref.r_0_, f32[512,512]{1,0:T(8,128)} %get-tuple-element.80.own_ref, bf16[512,512]{1,0:T(8,128)(2,1)} %copy-done, bf16[512,512]{1,0:T(8,128)(2,1)} %copy-done.24, ...), custom_call_target="tpu_custom_call", output_to_operand_aliasing={{0}: (6, {}), {1}: (7, {})} | custom-call | flops 2000000000 | bytes 1048576 | tf_op jit(solution)/shard_map/finish_kv/pallas_call | solution.py:234
  161.8 2.5 %finish_kv.7 = (bf16[512,1024]{1,0:T(8,128)(2,1)}, bf16[512,1024]{1,0:T(8,128)(2,1)}) custom-call(s32[1]{0:T(128)} %bitcast.par_ref.r_0_, f32[512,512]{1,0:T(8,128)} %get-tuple-element.68.own_ref, bf16[512,512]{1,0:T(8,128)(2,1)} %copy-done.1, bf16[512,512]{1,0:T(8,128)(2,1)} %copy-done.26, ...), custom_call_target="tpu_custom_call", output_to_operand_aliasing={{0}: (6, {}), {1}: (7, {})} | custom-call | flops 2000000000 | bytes 1048576 | tf_op jit(solution)/shard_map/finish_kv/pallas_call | solution.py:234
  (106 shorter events, 13.5 us)
Async XLA Ops:
  2.8 21.9 %copy-start.28 = (f32[128]{0:T(128)S(1)}, f32[128]{0:T(128)}, u32[]{:S(2)}) copy-start(f32[128]{0:T(128)} %param.12) | copy-start | bytes 1540
  2.8 23.3 %copy-start.12 = (s32[8192]{0:T(1024)S(1)}, s32[8192]{0:T(1024)}, u32[]{:S(2)}) copy-start(s32[8192]{0:T(1024)} %param.11) | copy-start | bytes 98308
  2.8 22.0 %collective-permute-start.1 = (bf16[512,512]{1,0:T(8,128)(2,1)}, bf16[512,512]{1,0:T(8,128)(2,1)S(1)}, u32[]{:S(2)}, u32[]{:S(2)}) collective-permute-start(bf16[512,512]{1,0:T(8,128)(2,1)} %pack_kv.2.own_ref), channel_id=1, source_target_pairs={{0,4},{2,6},{4,8},{6,10},{8,12},{10,14},{12,16},{14,18},{16,20},{1... | collective-permute-start | bytes 1572872 | tf_op jit(solution)/shard_map/far0/ppermute | solution.py:243
  7.8 20.2 %collective-permute-start = (bf16[512,512]{1,0:T(8,128)(2,1)}, bf16[512,512]{1,0:T(8,128)(2,1)S(1)}, u32[]{:S(2)}, u32[]{:S(2)}) collective-permute-start(bf16[512,512]{1,0:T(8,128)(2,1)} %pack_kv.2.own_ref), channel_id=1, source_target_pairs={{0,2},{4,6},{8,10},{12,14},{16,18},{20,22},{24,26},{28,30},{1,3},{... | collective-permute-start | bytes 1572872 | tf_op jit(solution)/shard_map/up0/ppermute | solution.py:243
  16.5 16.8 %collective-permute-start.4 = (bf16[512,512]{1,0:T(8,128)(2,1)}, bf16[512,512]{1,0:T(8,128)(2,1)S(1)}, u32[]{:S(2)}, u32[]{:S(2)}) collective-permute-start(bf16[512,512]{1,0:T(8,128)(2,1)} %get-tuple-element.51.r_5_), channel_id=1, source_target_pairs={{0,4},{2,6},{4,8},{6,10},{8,12},{10,14},{12,16},{14,18},{16,20},{1... | collective-permute-start | bytes 1572872 | tf_op jit(solution)/shard_map/far1/ppermute | solution.py:243
  19.9 32.3 %collective-permute-start.3 = (bf16[512,512]{1,0:T(8,128)(2,1)}, bf16[512,512]{1,0:T(8,128)(2,1)S(1)}, u32[]{:S(2)}, u32[]{:S(2)}) collective-permute-start(bf16[512,512]{1,0:T(8,128)(2,1)} %get-tuple-element.51.r_5_), channel_id=1, source_target_pairs={{0,2},{4,6},{8,10},{12,14},{16,18},{20,22},{24,26},{28,30},{1,3},{... | collective-permute-start | bytes 1572872 | tf_op jit(solution)/shard_map/up1/ppermute | solution.py:243
  21.3 36.3 %collective-permute-start.8 = (bf16[512,512]{1,0:T(8,128)(2,1)}, bf16[512,512]{1,0:T(8,128)(2,1)S(1)}, u32[]{:S(2)}, u32[]{:S(2)}) collective-permute-start(bf16[512,512]{1,0:T(8,128)(2,1)} %get-tuple-element.58.r_5_), channel_id=1, source_target_pairs={{0,4},{2,6},{4,8},{6,10},{8,12},{10,14},{12,16},{14,18},{16,20},{1... | collective-permute-start | bytes 1572872 | tf_op jit(solution)/shard_map/far2/ppermute | solution.py:243
  24.7 14.4 %collective-permute-start.2 = (bf16[512,512]{1,0:T(8,128)(2,1)S(1)}, bf16[512,512]{1,0:T(8,128)(2,1)S(1)}, u32[]{:S(2)}, u32[]{:S(2)}) collective-permute-start(bf16[512,512]{1,0:T(8,128)(2,1)S(1)} %collective-permute-done.1.h2_ref), channel_id=1, source_target_pairs={{2,0},{6,4},{10,8},{14,12},{18,16},{22,20},{26,24},{30,28},{3,1},{... | collective-permute-start | bytes 1572872 | tf_op jit(solution)/shard_map/relay0/ppermute | solution.py:243
  27.9 66.1 %collective-permute-start.7 = (bf16[512,512]{1,0:T(8,128)(2,1)}, bf16[512,512]{1,0:T(8,128)(2,1)}, u32[]{:S(2)}, u32[]{:S(2)}) collective-permute-start(bf16[512,512]{1,0:T(8,128)(2,1)} %get-tuple-element.58.r_5_), channel_id=1, source_target_pairs={{0,2},{4,6},{8,10},{12,14},{16,18},{20,22},{24,26},{28,30},{1,3},{... | collective-permute-start | bytes 1572872 | tf_op jit(solution)/shard_map/up2/ppermute | solution.py:243
  33.3 18.9 %copy-start.20 = (bf16[512,512]{1,0:T(8,128)(2,1)}, bf16[512,512]{1,0:T(8,128)(2,1)S(1)}, u32[]{:S(2)}) copy-start(bf16[512,512]{1,0:T(8,128)(2,1)S(1)} %collective-permute-done.4.r_8_) | copy-start | bytes 1572868
  33.3 25.6 %collective-permute-start.13 = (bf16[512,512]{1,0:T(8,128)(2,1)}, bf16[512,512]{1,0:T(8,128)(2,1)}, u32[]{:S(2)}, u32[]{:S(2)}) collective-permute-start(bf16[512,512]{1,0:T(8,128)(2,1)} %get-tuple-element.65.r_5_), channel_id=1, source_target_pairs={{0,4},{2,6},{4,8},{6,10},{8,12},{10,14},{12,16},{14,18},{16,20},{1... | collective-permute-start | bytes 1572872 | tf_op jit(solution)/shard_map/far3/ppermute | solution.py:243
  39.2 21.2 %collective-permute-start.5 = (bf16[512,512]{1,0:T(8,128)(2,1)S(1)}, bf16[512,512]{1,0:T(8,128)(2,1)}, u32[]{:S(2)}, u32[]{:S(2)}) collective-permute-start(bf16[512,512]{1,0:T(8,128)(2,1)S(1)} %collective-permute-done.4.r_8_), channel_id=1, source_target_pairs={{2,0},{6,4},{10,8},{14,12},{18,16},{22,20},{26,24},{30,28},{3,1},{... | collective-permute-start | bytes 1572872 | tf_op jit(solution)/shard_map/relay1/ppermute | solution.py:243
  52.2 58.9 %collective-permute-start.12 = (bf16[512,512]{1,0:T(8,128)(2,1)S(1)}, bf16[512,512]{1,0:T(8,128)(2,1)S(1)}, u32[]{:S(2)}, u32[]{:S(2)}) collective-permute-start(bf16[512,512]{1,0:T(8,128)(2,1)S(1)} %copy-done.18), channel_id=1, source_target_pairs={{0,2},{4,6},{8,10},{12,14},{16,18},{20,22},{24,26},{28,30},{1,3},{... | collective-permute-start | bytes 1572872 | tf_op jit(solution)/shard_map/up3/ppermute | solution.py:243
  57.6 18.6 %copy-start.19 = (bf16[512,512]{1,0:T(8,128)(2,1)}, bf16[512,512]{1,0:T(8,128)(2,1)S(1)}, u32[]{:S(2)}) copy-start(bf16[512,512]{1,0:T(8,128)(2,1)S(1)} %collective-permute-done.8.r_8_) | copy-start | bytes 1572868
  57.6 37.7 %collective-permute-start.9 = (bf16[512,512]{1,0:T(8,128)(2,1)S(1)}, bf16[512,512]{1,0:T(8,128)(2,1)}, u32[]{:S(2)}, u32[]{:S(2)}) collective-permute-start(bf16[512,512]{1,0:T(8,128)(2,1)S(1)} %collective-permute-done.8.r_8_), channel_id=1, source_target_pairs={{2,0},{6,4},{10,8},{14,12},{18,16},{22,20},{26,24},{30,28},{3,1},{... | collective-permute-start | bytes 1572872 | tf_op jit(solution)/shard_map/relay2/ppermute | solution.py:243
  58.9 52.2 %collective-permute-start.14 = (bf16[512,512]{1,0:T(8,128)(2,1)}, bf16[512,512]{1,0:T(8,128)(2,1)}, u32[]{:S(2)}, u32[]{:S(2)}) collective-permute-start(bf16[512,512]{1,0:T(8,128)(2,1)} %collective-permute-done.13.r_8_), channel_id=1, source_target_pairs={{2,0},{6,4},{10,8},{14,12},{18,16},{22,20},{26,24},{30,28},{3,1},{... | collective-permute-start | bytes 1572872 | tf_op jit(solution)/shard_map/relay3/ppermute | solution.py:243
  60.4 33.4 %collective-permute-start.6 = (bf16[512,512]{1,0:T(8,128)(2,1)}, bf16[512,512]{1,0:T(8,128)(2,1)S(1)}, u32[]{:S(2)}, u32[]{:S(2)}) collective-permute-start(bf16[512,512]{1,0:T(8,128)(2,1)} %get-tuple-element.55), channel_id=1, source_target_pairs={{0,2},{2,0},{4,6},{6,4},{8,10},{10,8},{12,14},{14,12},{16,18},{18,... | collective-permute-start | bytes 1572872 | tf_op jit(solution)/shard_map/swap0/ppermute | solution.py:243
  64.4 29.4 %copy-start.5 = (bf16[512,512]{1,0:T(8,128)(2,1)S(1)}, bf16[512,512]{1,0:T(8,128)(2,1)}, u32[]{:S(2)}) copy-start(bf16[512,512]{1,0:T(8,128)(2,1)} %get-tuple-element.54) | copy-start | bytes 1572868
  93.8 13.4 %collective-permute-start.10 = (bf16[512,512]{1,0:T(8,128)(2,1)}, bf16[512,512]{1,0:T(8,128)(2,1)S(1)}, u32[]{:S(2)}, u32[]{:S(2)}) collective-permute-start(bf16[512,512]{1,0:T(8,128)(2,1)} %get-tuple-element.62), channel_id=1, source_target_pairs={{0,2},{2,0},{4,6},{6,4},{8,10},{10,8},{12,14},{14,12},{16,18},{18,... | collective-permute-start | bytes 1572872 | tf_op jit(solution)/shard_map/swap1/ppermute | solution.py:243
  94.0 17.0 %collective-permute-start.11 = (bf16[512,512]{1,0:T(8,128)(2,1)S(1)}, bf16[512,512]{1,0:T(8,128)(2,1)}, u32[]{:S(2)}, u32[]{:S(2)}) collective-permute-start(bf16[512,512]{1,0:T(8,128)(2,1)S(1)} %fusion), channel_id=1, source_target_pairs={{4,0},{6,2},{8,4},{10,6},{12,8},{14,10},{16,12},{18,14},{20,16},{2... | collective-permute-start | bytes 1572872 | tf_op jit(solution)/shard_map/ret0/ppermute | solution.py:243
  107.3 16.3 %copy-start.3 = (bf16[512,512]{1,0:T(8,128)(2,1)}, bf16[512,512]{1,0:T(8,128)(2,1)S(1)}, u32[]{:S(2)}) copy-start(bf16[512,512]{1,0:T(8,128)(2,1)S(1)} %collective-permute-done.10.x_ref) | copy-start | bytes 1572868
  107.5 20.3 %collective-permute-start.16 = (bf16[512,512]{1,0:T(8,128)(2,1)S(1)}, bf16[512,512]{1,0:T(8,128)(2,1)}, u32[]{:S(2)}, u32[]{:S(2)}) collective-permute-start(bf16[512,512]{1,0:T(8,128)(2,1)S(1)} %fusion.1), channel_id=1, source_target_pairs={{4,0},{6,2},{8,4},{10,6},{12,8},{14,10},{16,12},{18,14},{20,16},{2... | collective-permute-start | bytes 1572872 | tf_op jit(solution)/shard_map/ret1/ppermute | solution.py:243
  109.0 14.7 %collective-permute-start.18 = (bf16[512,512]{1,0:T(8,128)(2,1)}, bf16[512,512]{1,0:T(8,128)(2,1)S(1)}, u32[]{:S(2)}, u32[]{:S(2)}) collective-permute-start(bf16[512,512]{1,0:T(8,128)(2,1)} %get-tuple-element.81), channel_id=1, source_target_pairs={{0,2},{2,0},{4,6},{6,4},{8,10},{10,8},{12,14},{14,12},{16,18},{18,... | collective-permute-start | bytes 1572872 | tf_op jit(solution)/shard_map/swap2/ppermute | solution.py:243
  123.8 33.4 %collective-permute-start.19 = (bf16[512,512]{1,0:T(8,128)(2,1)S(1)}, bf16[512,512]{1,0:T(8,128)(2,1)S(1)}, u32[]{:S(2)}, u32[]{:S(2)}) collective-permute-start(bf16[512,512]{1,0:T(8,128)(2,1)S(1)} %fusion.3), channel_id=1, source_target_pairs={{4,0},{6,2},{8,4},{10,6},{12,8},{14,10},{16,12},{18,14},{20,16},{2... | collective-permute-start | bytes 1572872 | tf_op jit(solution)/shard_map/ret2/ppermute | solution.py:243
  125.1 9.5 %collective-permute-start.15 = (bf16[512,512]{1,0:T(8,128)(2,1)}, bf16[512,512]{1,0:T(8,128)(2,1)S(1)}, u32[]{:S(2)}, u32[]{:S(2)}) collective-permute-start(bf16[512,512]{1,0:T(8,128)(2,1)} %get-tuple-element.69), channel_id=1, source_target_pairs={{0,2},{2,0},{4,6},{6,4},{8,10},{10,8},{12,14},{14,12},{16,18},{18,... | collective-permute-start | bytes 1572872 | tf_op jit(solution)/shard_map/swap3/ppermute | solution.py:243
  134.6 25.9 %copy-start.1 = (bf16[512,512]{1,0:T(8,128)(2,1)}, bf16[512,512]{1,0:T(8,128)(2,1)S(1)}, u32[]{:S(2)}) copy-start(bf16[512,512]{1,0:T(8,128)(2,1)S(1)} %collective-permute-done.15.x_ref) | copy-start | bytes 1572868
  134.8 26.3 %collective-permute-start.17 = (bf16[512,512]{1,0:T(8,128)(2,1)S(1)}, bf16[512,512]{1,0:T(8,128)(2,1)S(1)}, u32[]{:S(2)}, u32[]{:S(2)}) collective-permute-start(bf16[512,512]{1,0:T(8,128)(2,1)S(1)} %fusion.2), channel_id=1, source_target_pairs={{4,0},{6,2},{8,4},{10,6},{12,8},{14,10},{16,12},{18,14},{20,16},{2... | collective-permute-start | bytes 1572872 | tf_op jit(solution)/shard_map/ret3/ppermute | solution.py:243
  136.1 1.2 collective-permute-start.20
  137.3 3.6 %collective-permute-start.21 = (f32[2,128]{1,0:T(2,128)S(1)}, f32[2,128]{1,0:T(2,128)S(1)}, u32[]{:S(2)}, u32[]{:S(2)}) collective-permute-start(f32[2,128]{1,0:T(2,128)S(1)} %add.81), channel_id=1, source_target_pairs={{0,2},{2,0},{4,6},{6,4},{8,10},{10,8},{12,14},{14,12},{16,18},{18,... | collective-permute-start | bytes 3080 | tf_op jit(solution)/shard_map/ppermute | solution.py:258
  140.9 6.9 %collective-permute-start.22 = (f32[2,128]{1,0:T(2,128)S(1)}, f32[2,128]{1,0:T(2,128)S(1)}, u32[]{:S(2)}, u32[]{:S(2)}) collective-permute-start(f32[2,128]{1,0:T(2,128)S(1)} %add.82), channel_id=1, source_target_pairs={{0,4},{2,6},{4,0},{6,2},{8,12},{10,14},{12,8},{14,10},{16,20},{18,... | collective-permute-start | bytes 3080 | tf_op jit(solution)/shard_map/ppermute | solution.py:258
  147.8 5.0 %collective-permute-start.23 = (f32[2,128]{1,0:T(2,128)S(1)}, f32[2,128]{1,0:T(2,128)S(1)}, u32[]{:S(2)}, u32[]{:S(2)}) collective-permute-start(f32[2,128]{1,0:T(2,128)S(1)} %add.83), channel_id=1, source_target_pairs={{0,8},{2,10},{4,12},{6,14},{8,0},{10,2},{12,4},{14,6},{16,24},{18,... | collective-permute-start | bytes 3080 | tf_op jit(solution)/shard_map/ppermute | solution.py:258
  152.8 7.7 %collective-permute-start.24 = (f32[2,128]{1,0:T(2,128)S(1)}, f32[2,128]{1,0:T(2,128)S(1)}, u32[]{:S(2)}, u32[]{:S(2)}) collective-permute-start(f32[2,128]{1,0:T(2,128)S(1)} %add.84), channel_id=1, source_target_pairs={{0,16},{2,18},{4,20},{6,22},{8,24},{10,26},{12,28},{14,30},{16,0},... | collective-permute-start | bytes 3080 | tf_op jit(solution)/shard_map/ppermute | solution.py:258
  (22 other events, 128.6 us)

commit v3 on v2

--- a/solution.py
+++ b/solution.py
@@ -13,9 +13,11 @@
 W = 1024
 QUERY_SCALE = 168
 EPS = 1e-06
-CHUNKS = (2, 2, 2, 2)
+CHUNKS = (2, 2, 3, 1)
 GATE = 1
-GATE2 = 1
+GATE2 = 0
+EARLY = 2
+DIRECT = 0
 D=128
 BF=jnp.bfloat16
 F32=jnp.float32
@@ -244,19 +246,17 @@
 
 
 def after(value, *others):
-    return lax.optimization_barrier((value,) + others)[0]
-
-
-def sum_all(x):
-    for name in ("head", "ctx"):
-        count = lax.axis_size(name)
-        if count & (count - 1):
-            x = lax.psum(x, name)
-            continue
-        step = 1
-        while step < count:
-            x = x + lax.ppermute(x, name, [(i, i ^ step) for i in range(count)])
-            step *= 2
+    return lax.optimization_barrier((value, others))[0]
+
+
+def sum_over(x, name):
+    count = lax.axis_size(name)
+    if count & (count - 1):
+        return lax.psum(x, name)
+    step = 1
+    while step < count:
+        x = x + lax.ppermute(x, name, [(i, i ^ step) for i in range(count)])
+        step *= 2
     return x
 
 
@@ -282,7 +282,12 @@
     for c in range(n):
         far[c] = move(own[c], onward, f"far{c}")
         near_a[c] = move(own[c], up, f"up{c}")
+
+    def relay(c):
         near_b[c] = move(far[c], down, f"relay{c}")
+
+    for c in range(min(EARLY, n)):
+        relay(c)
 
     padded = jnp.concatenate([jnp.full((W,), -1, jnp.int32), doc_ids])
     span_ids = lax.dynamic_slice_in_dim(padded, me * rows, W + rows)
@@ -304,6 +309,12 @@
 
     tok = par
     for c in range(n):
+        if c + 1 >= EARLY and c + 1 < n:
+            if c:
+                far[c + 1] = after(far[c + 1], kss[c - 1])
+            relay(c + 1)
+        if c + 1 < EARLY and 0 < c < n - 1:
+            tok, near_b[c + 1] = lax.optimization_barrier((tok, near_b[c + 1]))
         if c >= 2:
             tok = after(tok, give(c - 2, kss[c - 1]))
         if c >= 3:
@@ -315,15 +326,13 @@
     give(n - 2, kss[n - 1])
     for c in range(n - 2):
         out = finish(after(par, ys[n - 2] if False else kss[n - 1]), mine[c], xs[c], ys[c], k_raw, gk, offs[c], chunks[c], out)
-    t = give(n - 1, kss[n - 1] if GATE == 0 or out is None else out[0])
+    t = give(n - 1, out[0])
+    out = finish(after(par, t), mine[n - 2], xs[n - 2], ys[n - 2], k_raw, gk, offs[n - 2], chunks[n - 2], out)
     q_part = jnp.sum(sum(qs), axis=1) * factor
     k_part = jnp.sum(sum(kss), axis=0) / k_gain
-    gains = jnp.stack([q_part, k_part])
-    if GATE2:
-        gains = after(gains, t)
-    gains = sum_all(gains)
-    for c in range(n - 2, n):
-        out = finish(par, mine[c], xs[c], ys[c], k_raw, gk, offs[c], chunks[c], out)
+    gains = after(jnp.stack([q_part, k_part]), t, out[0] if GATE2 else t)
+    gains = sum_over(sum_over(gains, "head"), "ctx")
+    out = finish(par, mine[n - 1], xs[n - 1], ys[n - 1], k_raw, gk, offs[n - 1], chunks[n - 1], out)
     total = rows * count
     return (qg, out[0], out[1], gains[0] / math.sqrt(total * Q_HEADS), gains[1] / math.sqrt(total * KV_HEADS))
 

time: 165 us -> 158 us (0.958)
  waiting for transfers between devices: 31.7 us -> 26.7 us
  starting transfers between devices: 61.1 us -> 56.9 us
    ppermute x20, waiting for transfers between devices: 23.1 us -> 18.9 us  [move(): return lax.ppermute(value, 'ctx', pairs)]
    ppermute x5, starting transfers between devices: 12.5 us -> 9.81 us  [sum_over(): x = x + lax.ppermute(x, name, [(i, i ^ step) for i in range(count)])]
  transfers between devices with their start and end apart: 25 -> 25, of which waited for: 7 -> 9; matrix products, arithmetic and copies ran while one was open for 2% -> 3% of each run, Pallas kernels for 36% -> 39%
where the time goes in v3:
time: 158 us; the launch traced here: 157 us
  Pallas kernels  65.2 us (41%)
  starting transfers between devices  56.9 us (36%)
  waiting for transfers between devices  26.7 us (17%)
  other arithmetic  3.9 us (2%)
  local copies, waits for them, and re-layouts  3.27 us (2%)
    ppermute x20, starting transfers between devices, move(): return lax.ppermute(value, 'ctx', pairs)  47 us
    pallas_call x4, Pallas kernels, attn(): pl.pallas_call(body, grid=(hc,), in_specs=in_specs, out_specs=[qs, kvs, k...  46.6 us
    ppermute x20, waiting for transfers between devices, move(): return lax.ppermute(value, 'ctx', pairs)  18.9 us
    pallas_call x4, Pallas kernels, finish(): pl.pallas_call(finish_body, grid=(hc,), in_specs=in_specs, out_specs=[cb,...  11.1 us
    ppermute x5, starting transfers between devices, sum_over(): x = x + lax.ppermute(x, name, [(i, i ^ step) for i in range(count)])  9.81 us
    ppermute x5, waiting for transfers between devices, sum_over(): x = x + lax.ppermute(x, name, [(i, i ^ step) for i in range(count)])  7.76 us
    pallas_call x2, Pallas kernels, pack(): pl.pallas_call(functools.partial(pack_body, chunks), grid=(at,), in_specs...  7.39 us
  transfers between devices with their start and end apart: 25, of which 9 were waited for; matrix products, arithmetic and copies ran while one was open for 3% of the time, Pallas kernels for 39%

profile of v3, /device:TPU:0, one launch (start us, length us, event | category | flops | bytes accessed | tf_op | source)
XLA Modules:
  0.0 157.1 jit_solution(16385649819131455654)
XLA Ops:
  0.6 2.1 %pack_kv.2.own_ref = bf16[512,512]{1,0:T(8,128)(2,1)} custom-call(bf16[512,1024]{1,0:T(8,128)(2,1)} %k_ref.11, bf16[512,1024]{1,0:T(8,128)(2,1)} %v_ref.3, f32[1,128]{1,0:T(1,128)} %bitcast.14), custom_call_target="tpu_custom_call" | custom-call | flops 2000000000 | bytes 1048576 | tf_op jit(solution)/shard_map/pack_kv/pallas_call | solution.py:204
  2.7 5.0 %collective-permute-start.1 = (bf16[512,512]{1,0:T(8,128)(2,1)}, bf16[512,512]{1,0:T(8,128)(2,1)S(1)}, u32[]{:S(2)}, u32[]{:S(2)}) collective-permute-start(bf16[512,512]{1,0:T(8,128)(2,1)} %pack_kv.2.own_ref), channel_id=1, source_target_pairs={{0,4},{2,6},{4,8},{6,10},{8,12},{10,14},{12,16},{14,18},{16,20},{1... | collective-permute-start | bytes 1572872 | tf_op jit(solution)/shard_map/far0/ppermute | solution.py:245
  7.8 3.4 %collective-permute-start = (bf16[512,512]{1,0:T(8,128)(2,1)}, bf16[512,512]{1,0:T(8,128)(2,1)S(1)}, u32[]{:S(2)}, u32[]{:S(2)}) collective-permute-start(bf16[512,512]{1,0:T(8,128)(2,1)} %pack_kv.2.own_ref), channel_id=1, source_target_pairs={{0,2},{4,6},{8,10},{12,14},{16,18},{20,22},{24,26},{28,30},{1,3},{... | collective-permute-start | bytes 1572872 | tf_op jit(solution)/shard_map/up0/ppermute | solution.py:245
  11.2 5.3 %pack_kv.3 = (bf16[512,512]{1,0:T(8,128)(2,1)}, bf16[512,768]{1,0:T(8,128)(2,1)}, bf16[512,256]{1,0:T(8,128)(2,1)}) custom-call(bf16[512,1024]{1,0:T(8,128)(2,1)} %k_ref.11, bf16[512,1024]{1,0:T(8,128)(2,1)} %v_ref.3, f32[1,128]{1,0:T(1,128)} %bitcast.15), custom_call_target="tpu_custom_call" | custom-call | flops 6000000000 | bytes 3145728 | tf_op jit(solution)/shard_map/pack_kv/pallas_call | solution.py:204
  16.5 3.4 %collective-permute-start.4 = (bf16[512,512]{1,0:T(8,128)(2,1)}, bf16[512,512]{1,0:T(8,128)(2,1)S(1)}, u32[]{:S(2)}, u32[]{:S(2)}) collective-permute-start(bf16[512,512]{1,0:T(8,128)(2,1)} %get-tuple-element.54.r_5_), channel_id=1, source_target_pairs={{0,4},{2,6},{4,8},{6,10},{8,12},{10,14},{12,16},{14,18},{16,20},{1... | collective-permute-start | bytes 1572872 | tf_op jit(solution)/shard_map/far1/ppermute | solution.py:245
  19.9 1.3 collective-permute-start.3
  21.2 3.4 %collective-permute-start.8 = (bf16[512,768]{1,0:T(8,128)(2,1)}, bf16[512,768]{1,0:T(8,128)(2,1)S(1)}, u32[]{:S(2)}, u32[]{:S(2)}) collective-permute-start(bf16[512,768]{1,0:T(8,128)(2,1)} %get-tuple-element.61.r_5_), channel_id=1, source_target_pairs={{0,4},{2,6},{4,8},{6,10},{8,12},{10,14},{12,16},{14,18},{16,20},{1... | collective-permute-start | bytes 2359304 | tf_op jit(solution)/shard_map/far2/ppermute | solution.py:245
  24.7 1.3 collective-permute-start.2
  27.9 5.5 %collective-permute-start.7 = (bf16[512,768]{1,0:T(8,128)(2,1)}, bf16[512,768]{1,0:T(8,128)(2,1)}, u32[]{:S(2)}, u32[]{:S(2)}) collective-permute-start(bf16[512,768]{1,0:T(8,128)(2,1)} %get-tuple-element.61.r_5_), channel_id=1, source_target_pairs={{0,2},{4,6},{8,10},{12,14},{16,18},{20,22},{24,26},{28,30},{1,3},{... | collective-permute-start | bytes 2359304 | tf_op jit(solution)/shard_map/up2/ppermute | solution.py:245
  33.4 4.1 %collective-permute-start.13 = (bf16[512,256]{1,0:T(8,128)(2,1)}, bf16[512,256]{1,0:T(8,128)(2,1)}, u32[]{:S(2)}, u32[]{:S(2)}) collective-permute-start(bf16[512,256]{1,0:T(8,128)(2,1)} %get-tuple-element.70.r_5_), channel_id=1, source_target_pairs={{0,4},{2,6},{4,8},{6,10},{8,12},{10,14},{12,16},{14,18},{16,20},{1... | collective-permute-start | bytes 786440 | tf_op jit(solution)/shard_map/far3/ppermute | solution.py:245
  37.5 1.6 %collective-permute-done.2.h1b_ref = bf16[512,512]{1,0:T(8,128)(2,1)S(1)} collective-permute-done((bf16[512,512]{1,0:T(8,128)(2,1)S(1)}, bf16[512,512]{1,0:T(8,128)(2,1)S(1)}, u32[]{:S(2)}, u32[]{:S(2)}) %collective-permute-start.2) | collective-permute-done | bytes 524320 | tf_op jit(solution)/shard_map/relay0/ppermute | solution.py:245
  40.5 11.6 %attn_grad.4 = (bf16[512,2048]{1,0:T(8,128)(2,1)}, f32[512,512]{1,0:T(8,128)}, bf16[512,512]{1,0:T(8,128)(2,1)}, bf16[512,512]{1,0:T(8,128)(2,1)}, f32[128,256]{1,0:T(8,128)}, /*index=5*/f32[8,128]{1,0:T(8,128)}) custom-call(s32[1]{0:T(128)} %bitcast.par_ref.r_0_, s32[1,512]{1,0:T(1,128)} %add_maximum_fusion.lo_ref.r_1_, f32[128,1]{1,0:T(8,128)} %copy.25.gq_ref.r_2_, ...), custom_call_target="tpu_custom_call" | custom-call | flops 12000000000 | bytes 3145728 | tf_op jit(solution)/shard_map/attn_grad/pallas_call | solution.py:168
  52.1 4.6 %collective-permute-start.12 = (bf16[512,256]{1,0:T(8,128)(2,1)}, bf16[512,256]{1,0:T(8,128)(2,1)S(1)}, u32[]{:S(2)}, u32[]{:S(2)}) collective-permute-start(bf16[512,256]{1,0:T(8,128)(2,1)} %get-tuple-element.70.r_5_), channel_id=1, source_target_pairs={{0,2},{4,6},{8,10},{12,14},{16,18},{20,22},{24,26},{28,30},{1,3},{... | collective-permute-start | bytes 786440 | tf_op jit(solution)/shard_map/up3/ppermute | solution.py:245
  58.2 11.8 %attn_grad.5 = (bf16[512,2048]{1,0:T(8,128)(2,1)}, f32[512,512]{1,0:T(8,128)}, bf16[512,512]{1,0:T(8,128)(2,1)}, bf16[512,512]{1,0:T(8,128)(2,1)}, f32[128,256]{1,0:T(8,128)}, /*index=5*/f32[8,128]{1,0:T(8,128)}) custom-call(s32[1]{0:T(128)} %bitcast.par_ref.r_0_, s32[1,512]{1,0:T(1,128)} %add_maximum_fusion.lo_ref.r_1_, ...), custom_call_target="tpu_custom_call", output_to_operand_aliasing={{0}: (9, {})} | custom-call | flops 12000000000 | bytes 3145728 | tf_op jit(solution)/shard_map/attn_grad/pallas_call | solution.py:168
  70.0 3.5 %collective-permute-start.10 = (bf16[512,512]{1,0:T(8,128)(2,1)}, bf16[512,512]{1,0:T(8,128)(2,1)S(1)}, u32[]{:S(2)}, u32[]{:S(2)}) collective-permute-start(bf16[512,512]{1,0:T(8,128)(2,1)} %get-tuple-element.67), channel_id=1, source_target_pairs={{0,2},{2,0},{4,6},{6,4},{8,10},{10,8},{12,14},{14,12},{16,18},{18,... | collective-permute-start | bytes 1572872 | tf_op jit(solution)/shard_map/swap1/ppermute | solution.py:245
  73.6 1.5 collective-permute-start.14
  76.5 12.3 %collective-permute-done.9.r_7_ = bf16[512,768]{1,0:T(8,128)(2,1)} collective-permute-done((bf16[512,768]{1,0:T(8,128)(2,1)S(1)}, bf16[512,768]{1,0:T(8,128)(2,1)}, u32[]{:S(2)}, u32[]{:S(2)}) %collective-permute-start.9) | collective-permute-done | bytes 786464 | tf_op jit(solution)/shard_map/relay2/ppermute | solution.py:245
  88.9 16.3 %attn_grad.6 = (bf16[512,2048]{1,0:T(8,128)(2,1)}, f32[512,768]{1,0:T(8,128)}, bf16[512,768]{1,0:T(8,128)(2,1)}, bf16[512,768]{1,0:T(8,128)(2,1)}, f32[128,256]{1,0:T(8,128)}, /*index=5*/f32[8,128]{1,0:T(8,128)}) custom-call(s32[1]{0:T(128)} %bitcast.par_ref.r_0_, s32[1,512]{1,0:T(1,128)} %add_maximum_fusion.lo_ref.r_1_, ...), custom_call_target="tpu_custom_call", output_to_operand_aliasing={{0}: (9, {})} | custom-call | flops 17999998976 | bytes 4718592 | tf_op jit(solution)/shard_map/attn_grad/pallas_call | solution.py:168
  107.6 6.9 %attn_grad.7 = (bf16[512,2048]{1,0:T(8,128)(2,1)}, f32[512,256]{1,0:T(8,128)}, bf16[512,256]{1,0:T(8,128)(2,1)}, bf16[512,256]{1,0:T(8,128)(2,1)}, f32[128,256]{1,0:T(8,128)}, /*index=5*/f32[8,128]{1,0:T(8,128)}) custom-call(s32[1]{0:T(128)} %bitcast.par_ref.r_0_, s32[1,512]{1,0:T(1,128)} %add_maximum_fusion.lo_ref.r_1_, ...), custom_call_target="tpu_custom_call", output_to_operand_aliasing={{0}: (9, {})} | custom-call | flops 6000000000 | bytes 1572864 | tf_op jit(solution)/shard_map/attn_grad/pallas_call | solution.py:168
  114.5 2.1 %collective-permute-start.15 = (bf16[512,256]{1,0:T(8,128)(2,1)}, bf16[512,256]{1,0:T(8,128)(2,1)S(1)}, u32[]{:S(2)}, u32[]{:S(2)}) collective-permute-start(bf16[512,256]{1,0:T(8,128)(2,1)} %get-tuple-element.75), channel_id=1, source_target_pairs={{0,2},{2,0},{4,6},{6,4},{8,10},{10,8},{12,14},{14,12},{16,18},{18,... | collective-permute-start | bytes 786440 | tf_op jit(solution)/shard_map/swap3/ppermute | solution.py:245
  118.3 3.4 %collective-permute-done.18.x_ref = bf16[512,768]{1,0:T(8,128)(2,1)S(1)} collective-permute-done((bf16[512,768]{1,0:T(8,128)(2,1)}, bf16[512,768]{1,0:T(8,128)(2,1)S(1)}, u32[]{:S(2)}, u32[]{:S(2)}) %collective-permute-start.18) | collective-permute-done | bytes 786464 | tf_op jit(solution)/shard_map/swap2/ppermute | solution.py:245
  123.3 2.6 %finish_kv.4 = (bf16[512,1024]{1,0:T(8,128)(2,1)}, bf16[512,1024]{1,0:T(8,128)(2,1)}) custom-call(s32[1]{0:T(128)} %bitcast.par_ref.r_0_, f32[512,512]{1,0:T(8,128)} %get-tuple-element.80.own_ref, bf16[512,512]{1,0:T(8,128)(2,1)} %copy-done.3, bf16[512,512]{1,0:T(8,128)(2,1)} %collective-permute-done.11.y_ref, bf16[512,1024]{1,0:T(8,128)(2,1)} %k_ref.11, ...), custom_call_target="tpu_custom_call" | custom-call | flops 2000000000 | bytes 1048576 | tf_op jit(solution)/shard_map/finish_kv/pallas_call | solution.py:236
  125.9 2.6 %finish_kv.5 = (bf16[512,1024]{1,0:T(8,128)(2,1)}, bf16[512,1024]{1,0:T(8,128)(2,1)}) custom-call(s32[1]{0:T(128)} %bitcast.par_ref.r_0_, f32[512,512]{1,0:T(8,128)} %get-tuple-element.79.own_ref, bf16[512,512]{1,0:T(8,128)(2,1)} %copy-done.4, bf16[512,512]{1,0:T(8,128)(2,1)} %collective-permute-done.16.y_ref, ...), custom_call_target="tpu_custom_call", output_to_operand_aliasing={{0}: (6, {}), {1}: (7, {})} | custom-call | flops 2000000000 | bytes 1048576 | tf_op jit(solution)/shard_map/finish_kv/pallas_call | solution.py:236
  130.1 3.3 %collective-permute-done.21 = f32[2,128]{1,0:T(2,128)S(1)} collective-permute-done((f32[2,128]{1,0:T(2,128)S(1)}, f32[2,128]{1,0:T(2,128)S(1)}, u32[]{:S(2)}, u32[]{:S(2)}) %collective-permute-start.21) | collective-permute-done | bytes 1056 | tf_op jit(solution)/shard_map/ppermute | solution.py:258
  133.4 3.0 %collective-permute-start.22 = (f32[2,128]{1,0:T(2,128)S(1)}, f32[2,128]{1,0:T(2,128)S(1)}, u32[]{:S(2)}, u32[]{:S(2)}) collective-permute-start(f32[2,128]{1,0:T(2,128)S(1)} %add.82), channel_id=1, source_target_pairs={{0,4},{2,6},{4,0},{6,2},{8,12},{10,14},{12,8},{14,10},{16,20},{18,... | collective-permute-start | bytes 3080 | tf_op jit(solution)/shard_map/ppermute | solution.py:258
  136.4 1.5 collective-permute-done.22
  138.0 3.5 %collective-permute-start.23 = (f32[2,128]{1,0:T(2,128)S(1)}, f32[2,128]{1,0:T(2,128)S(1)}, u32[]{:S(2)}, u32[]{:S(2)}) collective-permute-start(f32[2,128]{1,0:T(2,128)S(1)} %add.83), channel_id=1, source_target_pairs={{0,8},{2,10},{4,12},{6,14},{8,0},{10,2},{12,4},{14,6},{16,24},{18,... | collective-permute-start | bytes 3080 | tf_op jit(solution)/shard_map/ppermute | solution.py:258
  141.4 1.5 collective-permute-done.23
  143.0 3.0 %collective-permute-start.24 = (f32[2,128]{1,0:T(2,128)S(1)}, f32[2,128]{1,0:T(2,128)S(1)}, u32[]{:S(2)}, u32[]{:S(2)}) collective-permute-start(f32[2,128]{1,0:T(2,128)S(1)} %add.84), channel_id=1, source_target_pairs={{0,16},{2,18},{4,20},{6,22},{8,24},{10,26},{12,28},{14,30},{16,0},... | collective-permute-start | bytes 3080 | tf_op jit(solution)/shard_map/ppermute | solution.py:258
  148.9 3.8 %finish_kv.6 = (bf16[512,1024]{1,0:T(8,128)(2,1)}, bf16[512,1024]{1,0:T(8,128)(2,1)}) custom-call(s32[1]{0:T(128)} %bitcast.par_ref.r_0_, f32[512,768]{1,0:T(8,128)} %get-tuple-element.87.own_ref, bf16[512,768]{1,0:T(8,128)(2,1)} %copy-done.1, bf16[512,768]{1,0:T(8,128)(2,1)} %copy-done.18, ...), custom_call_target="tpu_custom_call", output_to_operand_aliasing={{0}: (6, {}), {1}: (7, {})} | custom-call | flops 3000000000 | bytes 1572864 | tf_op jit(solution)/shard_map/finish_kv/pallas_call | solution.py:236
  152.8 1.5 collective-permute-done.17.y_ref
  154.9 2.2 %finish_kv.7 = (bf16[512,1024]{1,0:T(8,128)(2,1)}, bf16[512,1024]{1,0:T(8,128)(2,1)}) custom-call(s32[1]{0:T(128)} %bitcast.par_ref.r_0_, f32[512,256]{1,0:T(8,128)} %get-tuple-element.74.own_ref, bf16[512,256]{1,0:T(8,128)(2,1)} %copy-done, bf16[512,256]{1,0:T(8,128)(2,1)} %copy-done.7, ...), custom_call_target="tpu_custom_call", output_to_operand_aliasing={{0}: (6, {}), {1}: (7, {})} | custom-call | flops 1000000000 | bytes 524288 | tf_op jit(solution)/shard_map/finish_kv/pallas_call | solution.py:236
  (102 shorter events, 16.8 us)
Async XLA Ops:
  2.7 22.0 %copy-start.26 = (f32[128]{0:T(128)S(1)}, f32[128]{0:T(128)}, u32[]{:S(2)}) copy-start(f32[128]{0:T(128)} %param.12) | copy-start | bytes 1540
  2.7 23.3 %copy-start.12 = (s32[8192]{0:T(1024)S(1)}, s32[8192]{0:T(1024)}, u32[]{:S(2)}) copy-start(s32[8192]{0:T(1024)} %param.11) | copy-start | bytes 98308
  2.7 22.0 %collective-permute-start.1 = (bf16[512,512]{1,0:T(8,128)(2,1)}, bf16[512,512]{1,0:T(8,128)(2,1)S(1)}, u32[]{:S(2)}, u32[]{:S(2)}) collective-permute-start(bf16[512,512]{1,0:T(8,128)(2,1)} %pack_kv.2.own_ref), channel_id=1, source_target_pairs={{0,4},{2,6},{4,8},{6,10},{8,12},{10,14},{12,16},{14,18},{16,20},{1... | collective-permute-start | bytes 1572872 | tf_op jit(solution)/shard_map/far0/ppermute | solution.py:245
  7.8 20.2 %collective-permute-start = (bf16[512,512]{1,0:T(8,128)(2,1)}, bf16[512,512]{1,0:T(8,128)(2,1)S(1)}, u32[]{:S(2)}, u32[]{:S(2)}) collective-permute-start(bf16[512,512]{1,0:T(8,128)(2,1)} %pack_kv.2.own_ref), channel_id=1, source_target_pairs={{0,2},{4,6},{8,10},{12,14},{16,18},{20,22},{24,26},{28,30},{1,3},{... | collective-permute-start | bytes 1572872 | tf_op jit(solution)/shard_map/up0/ppermute | solution.py:245
  16.5 16.9 %collective-permute-start.4 = (bf16[512,512]{1,0:T(8,128)(2,1)}, bf16[512,512]{1,0:T(8,128)(2,1)S(1)}, u32[]{:S(2)}, u32[]{:S(2)}) collective-permute-start(bf16[512,512]{1,0:T(8,128)(2,1)} %get-tuple-element.54.r_5_), channel_id=1, source_target_pairs={{0,4},{2,6},{4,8},{6,10},{8,12},{10,14},{12,16},{14,18},{16,20},{1... | collective-permute-start | bytes 1572872 | tf_op jit(solution)/shard_map/far1/ppermute | solution.py:245
  19.9 36.8 %collective-permute-start.3 = (bf16[512,512]{1,0:T(8,128)(2,1)}, bf16[512,512]{1,0:T(8,128)(2,1)S(1)}, u32[]{:S(2)}, u32[]{:S(2)}) collective-permute-start(bf16[512,512]{1,0:T(8,128)(2,1)} %get-tuple-element.54.r_5_), channel_id=1, source_target_pairs={{0,2},{4,6},{8,10},{12,14},{16,18},{20,22},{24,26},{28,30},{1,3},{... | collective-permute-start | bytes 1572872 | tf_op jit(solution)/shard_map/up1/ppermute | solution.py:245
  21.2 30.9 %collective-permute-start.8 = (bf16[512,768]{1,0:T(8,128)(2,1)}, bf16[512,768]{1,0:T(8,128)(2,1)S(1)}, u32[]{:S(2)}, u32[]{:S(2)}) collective-permute-start(bf16[512,768]{1,0:T(8,128)(2,1)} %get-tuple-element.61.r_5_), channel_id=1, source_target_pairs={{0,4},{2,6},{4,8},{6,10},{8,12},{10,14},{12,16},{14,18},{16,20},{1... | collective-permute-start | bytes 2359304 | tf_op jit(solution)/shard_map/far2/ppermute | solution.py:245
  24.7 14.4 %collective-permute-start.2 = (bf16[512,512]{1,0:T(8,128)(2,1)S(1)}, bf16[512,512]{1,0:T(8,128)(2,1)S(1)}, u32[]{:S(2)}, u32[]{:S(2)}) collective-permute-start(bf16[512,512]{1,0:T(8,128)(2,1)S(1)} %collective-permute-done.1.h2_ref), channel_id=1, source_target_pairs={{2,0},{6,4},{10,8},{14,12},{18,16},{22,20},{26,24},{30,28},{3,1},{... | collective-permute-start | bytes 1572872 | tf_op jit(solution)/shard_map/relay0/ppermute | solution.py:245
  27.9 47.3 %collective-permute-start.7 = (bf16[512,768]{1,0:T(8,128)(2,1)}, bf16[512,768]{1,0:T(8,128)(2,1)}, u32[]{:S(2)}, u32[]{:S(2)}) collective-permute-start(bf16[512,768]{1,0:T(8,128)(2,1)} %get-tuple-element.61.r_5_), channel_id=1, source_target_pairs={{0,2},{4,6},{8,10},{12,14},{16,18},{20,22},{24,26},{28,30},{1,3},{... | collective-permute-start | bytes 2359304 | tf_op jit(solution)/shard_map/up2/ppermute | solution.py:245
  33.4 18.7 %copy-start.19 = (bf16[512,512]{1,0:T(8,128)(2,1)}, bf16[512,512]{1,0:T(8,128)(2,1)S(1)}, u32[]{:S(2)}) copy-start(bf16[512,512]{1,0:T(8,128)(2,1)S(1)} %collective-permute-done.4.r_8_) | copy-start | bytes 1572868
  33.4 36.6 %collective-permute-start.13 = (bf16[512,256]{1,0:T(8,128)(2,1)}, bf16[512,256]{1,0:T(8,128)(2,1)}, u32[]{:S(2)}, u32[]{:S(2)}) collective-permute-start(bf16[512,256]{1,0:T(8,128)(2,1)} %get-tuple-element.70.r_5_), channel_id=1, source_target_pairs={{0,4},{2,6},{4,8},{6,10},{8,12},{10,14},{12,16},{14,18},{16,20},{1... | collective-permute-start | bytes 786440 | tf_op jit(solution)/shard_map/far3/ppermute | solution.py:245
  39.2 17.7 %collective-permute-start.5 = (bf16[512,512]{1,0:T(8,128)(2,1)S(1)}, bf16[512,512]{1,0:T(8,128)(2,1)S(1)}, u32[]{:S(2)}, u32[]{:S(2)}) collective-permute-start(bf16[512,512]{1,0:T(8,128)(2,1)S(1)} %collective-permute-done.4.r_8_), channel_id=1, source_target_pairs={{2,0},{6,4},{10,8},{14,12},{18,16},{22,20},{26,24},{30,28},{3,1},{... | collective-permute-start | bytes 1572872 | tf_op jit(solution)/shard_map/relay1/ppermute | solution.py:245
  52.1 17.8 %copy-start.17 = (bf16[512,768]{1,0:T(8,128)(2,1)}, bf16[512,768]{1,0:T(8,128)(2,1)S(1)}, u32[]{:S(2)}) copy-start(bf16[512,768]{1,0:T(8,128)(2,1)S(1)} %collective-permute-done.8.r_8_) | copy-start | bytes 2359300
  52.1 54.7 %collective-permute-start.12 = (bf16[512,256]{1,0:T(8,128)(2,1)}, bf16[512,256]{1,0:T(8,128)(2,1)S(1)}, u32[]{:S(2)}, u32[]{:S(2)}) collective-permute-start(bf16[512,256]{1,0:T(8,128)(2,1)} %get-tuple-element.70.r_5_), channel_id=1, source_target_pairs={{0,2},{4,6},{8,10},{12,14},{16,18},{20,22},{24,26},{28,30},{1,3},{... | collective-permute-start | bytes 786440 | tf_op jit(solution)/shard_map/up3/ppermute | solution.py:245
  56.8 16.8 %collective-permute-start.6 = (bf16[512,512]{1,0:T(8,128)(2,1)}, bf16[512,512]{1,0:T(8,128)(2,1)S(1)}, u32[]{:S(2)}, u32[]{:S(2)}) collective-permute-start(bf16[512,512]{1,0:T(8,128)(2,1)} %get-tuple-element.58), channel_id=1, source_target_pairs={{0,2},{2,0},{4,6},{6,4},{8,10},{10,8},{12,14},{14,12},{16,18},{18,... | collective-permute-start | bytes 1572872 | tf_op jit(solution)/shard_map/swap0/ppermute | solution.py:245
  56.9 32.0 %collective-permute-start.9 = (bf16[512,768]{1,0:T(8,128)(2,1)S(1)}, bf16[512,768]{1,0:T(8,128)(2,1)}, u32[]{:S(2)}, u32[]{:S(2)}) collective-permute-start(bf16[512,768]{1,0:T(8,128)(2,1)S(1)} %collective-permute-done.8.r_8_), channel_id=1, source_target_pairs={{2,0},{6,4},{10,8},{14,12},{18,16},{22,20},{26,24},{30,28},{3,1},{... | collective-permute-start | bytes 2359304 | tf_op jit(solution)/shard_map/relay2/ppermute | solution.py:245
  58.2 16.8 %copy-start.5 = (bf16[512,512]{1,0:T(8,128)(2,1)S(1)}, bf16[512,512]{1,0:T(8,128)(2,1)}, u32[]{:S(2)}) copy-start(bf16[512,512]{1,0:T(8,128)(2,1)} %get-tuple-element.57) | copy-start | bytes 1572868
  70.0 35.2 %collective-permute-start.10 = (bf16[512,512]{1,0:T(8,128)(2,1)}, bf16[512,512]{1,0:T(8,128)(2,1)S(1)}, u32[]{:S(2)}, u32[]{:S(2)}) collective-permute-start(bf16[512,512]{1,0:T(8,128)(2,1)} %get-tuple-element.67), channel_id=1, source_target_pairs={{0,2},{2,0},{4,6},{6,4},{8,10},{10,8},{12,14},{14,12},{16,18},{18,... | collective-permute-start | bytes 1572872 | tf_op jit(solution)/shard_map/swap1/ppermute | solution.py:245
  73.6 31.7 %copy-start.3 = (bf16[512,512]{1,0:T(8,128)(2,1)}, bf16[512,512]{1,0:T(8,128)(2,1)S(1)}, u32[]{:S(2)}) copy-start(bf16[512,512]{1,0:T(8,128)(2,1)S(1)} %collective-permute-done.6.x_ref) | copy-start | bytes 1572868
  73.6 33.3 %collective-permute-start.14 = (bf16[512,256]{1,0:T(8,128)(2,1)}, bf16[512,256]{1,0:T(8,128)(2,1)}, u32[]{:S(2)}, u32[]{:S(2)}) collective-permute-start(bf16[512,256]{1,0:T(8,128)(2,1)} %collective-permute-done.13.r_8_), channel_id=1, source_target_pairs={{2,0},{6,4},{10,8},{14,12},{18,16},{22,20},{26,24},{30,28},{3,1},{... | collective-permute-start | bytes 786440 | tf_op jit(solution)/shard_map/relay3/ppermute | solution.py:245
  75.2 31.6 %collective-permute-start.11 = (bf16[512,512]{1,0:T(8,128)(2,1)S(1)}, bf16[512,512]{1,0:T(8,128)(2,1)}, u32[]{:S(2)}, u32[]{:S(2)}) collective-permute-start(bf16[512,512]{1,0:T(8,128)(2,1)S(1)} %fusion.1), channel_id=1, source_target_pairs={{4,0},{6,2},{8,4},{10,6},{12,8},{14,10},{16,12},{18,14},{20,16},{2... | collective-permute-start | bytes 1572872 | tf_op jit(solution)/shard_map/ret0/ppermute | solution.py:245
  105.4 20.5 %collective-permute-start.16 = (bf16[512,512]{1,0:T(8,128)(2,1)S(1)}, bf16[512,512]{1,0:T(8,128)(2,1)}, u32[]{:S(2)}, u32[]{:S(2)}) collective-permute-start(bf16[512,512]{1,0:T(8,128)(2,1)S(1)} %fusion.2), channel_id=1, source_target_pairs={{4,0},{6,2},{8,4},{10,6},{12,8},{14,10},{16,12},{18,14},{20,16},{2... | collective-permute-start | bytes 1572872 | tf_op jit(solution)/shard_map/ret1/ppermute | solution.py:245
  106.7 15.0 %collective-permute-start.18 = (bf16[512,768]{1,0:T(8,128)(2,1)}, bf16[512,768]{1,0:T(8,128)(2,1)S(1)}, u32[]{:S(2)}, u32[]{:S(2)}) collective-permute-start(bf16[512,768]{1,0:T(8,128)(2,1)} %get-tuple-element.88), channel_id=1, source_target_pairs={{0,2},{2,0},{4,6},{6,4},{8,10},{10,8},{12,14},{14,12},{16,18},{18,... | collective-permute-start | bytes 2359304 | tf_op jit(solution)/shard_map/swap2/ppermute | solution.py:245
  114.5 14.0 %collective-permute-start.15 = (bf16[512,256]{1,0:T(8,128)(2,1)}, bf16[512,256]{1,0:T(8,128)(2,1)S(1)}, u32[]{:S(2)}, u32[]{:S(2)}) collective-permute-start(bf16[512,256]{1,0:T(8,128)(2,1)} %get-tuple-element.75), channel_id=1, source_target_pairs={{0,2},{2,0},{4,6},{6,4},{8,10},{10,8},{12,14},{14,12},{16,18},{18,... | collective-permute-start | bytes 786440 | tf_op jit(solution)/shard_map/swap3/ppermute | solution.py:245
  122.0 26.0 %collective-permute-start.19 = (bf16[512,768]{1,0:T(8,128)(2,1)S(1)}, bf16[512,768]{1,0:T(8,128)(2,1)S(1)}, u32[]{:S(2)}, u32[]{:S(2)}) collective-permute-start(bf16[512,768]{1,0:T(8,128)(2,1)S(1)} %fusion), channel_id=1, source_target_pairs={{4,0},{6,2},{8,4},{10,6},{12,8},{14,10},{16,12},{18,14},{20,16},{2... | collective-permute-start | bytes 2359304 | tf_op jit(solution)/shard_map/ret2/ppermute | solution.py:245
  128.5 24.2 %copy-start = (bf16[512,256]{1,0:T(8,128)(2,1)}, bf16[512,256]{1,0:T(8,128)(2,1)S(1)}, u32[]{:S(2)}) copy-start(bf16[512,256]{1,0:T(8,128)(2,1)S(1)} %collective-permute-done.15.x_ref) | copy-start | bytes 786436
  128.6 1.2 collective-permute-start.20
  129.8 3.6 %collective-permute-start.21 = (f32[2,128]{1,0:T(2,128)S(1)}, f32[2,128]{1,0:T(2,128)S(1)}, u32[]{:S(2)}, u32[]{:S(2)}) collective-permute-start(f32[2,128]{1,0:T(2,128)S(1)} %add.81), channel_id=1, source_target_pairs={{0,2},{2,0},{4,6},{6,4},{8,10},{10,8},{12,14},{14,12},{16,18},{18,... | collective-permute-start | bytes 3080 | tf_op jit(solution)/shard_map/ppermute | solution.py:258
  133.4 4.5 %collective-permute-start.22 = (f32[2,128]{1,0:T(2,128)S(1)}, f32[2,128]{1,0:T(2,128)S(1)}, u32[]{:S(2)}, u32[]{:S(2)}) collective-permute-start(f32[2,128]{1,0:T(2,128)S(1)} %add.82), channel_id=1, source_target_pairs={{0,4},{2,6},{4,0},{6,2},{8,12},{10,14},{12,8},{14,10},{16,20},{18,... | collective-permute-start | bytes 3080 | tf_op jit(solution)/shard_map/ppermute | solution.py:258
  138.0 5.0 %collective-permute-start.23 = (f32[2,128]{1,0:T(2,128)S(1)}, f32[2,128]{1,0:T(2,128)S(1)}, u32[]{:S(2)}, u32[]{:S(2)}) collective-permute-start(f32[2,128]{1,0:T(2,128)S(1)} %add.83), channel_id=1, source_target_pairs={{0,8},{2,10},{4,12},{6,14},{8,0},{10,2},{12,4},{14,6},{16,24},{18,... | collective-permute-start | bytes 3080 | tf_op jit(solution)/shard_map/ppermute | solution.py:258
  143.0 4.5 %collective-permute-start.24 = (f32[2,128]{1,0:T(2,128)S(1)}, f32[2,128]{1,0:T(2,128)S(1)}, u32[]{:S(2)}, u32[]{:S(2)}) collective-permute-start(f32[2,128]{1,0:T(2,128)S(1)} %add.84), channel_id=1, source_target_pairs={{0,16},{2,18},{4,20},{6,22},{8,24},{10,26},{12,28},{14,30},{16,0},... | collective-permute-start | bytes 3080 | tf_op jit(solution)/shard_map/ppermute | solution.py:258
  146.0 8.3 %collective-permute-start.17 = (bf16[512,256]{1,0:T(8,128)(2,1)S(1)}, bf16[512,256]{1,0:T(8,128)(2,1)S(1)}, u32[]{:S(2)}, u32[]{:S(2)}) collective-permute-start(bf16[512,256]{1,0:T(8,128)(2,1)S(1)} %fusion.3), channel_id=1, source_target_pairs={{4,0},{6,2},{8,4},{10,6},{12,8},{14,10},{16,12},{18,14},{20,16},{2... | collective-permute-start | bytes 786440 | tf_op jit(solution)/shard_map/ret3/ppermute | solution.py:245
  (20 other events, 148.3 us)

commit v4 on v3

--- a/solution.py
+++ b/solution.py
@@ -13,7 +13,7 @@
 W = 1024
 QUERY_SCALE = 168
 EPS = 1e-06
-CHUNKS = (2, 2, 3, 1)
+CHUNKS = (2, 3, 2, 1)
 GATE = 1
 GATE2 = 0
 EARLY = 2

time: 158 us -> 155 us (0.981)
  waiting for transfers between devices: 26.7 us -> 22 us
  starting transfers between devices: 56.9 us -> 58.7 us
    ppermute x20, waiting for transfers between devices: 18.9 us -> 14.6 us  [move(): return lax.ppermute(value, 'ctx', pairs)]
    ppermute x20, starting transfers between devices: 47 us -> 49.8 us  [move(): return lax.ppermute(value, 'ctx', pairs)]
  transfers between devices with their start and end apart: 25 -> 25, of which waited for: 9 -> 11; matrix products, arithmetic and copies ran while one was open for 3% -> 3% of each run, Pallas kernels for 39% -> 40%
where the time goes in v4:
time: 155 us; the launch traced here: 154 us
  Pallas kernels  65.1 us (42%)
  starting transfers between devices  58.7 us (38%)
  waiting for transfers between devices  22 us (14%)
  other arithmetic  3.84 us (2%)
  local copies, waits for them, and re-layouts  3.21 us (2%)
    ppermute x20, starting transfers between devices, move(): return lax.ppermute(value, 'ctx', pairs)  49.8 us
    pallas_call x4, Pallas kernels, attn(): pl.pallas_call(body, grid=(hc,), in_specs=in_specs, out_specs=[qs, kvs, k...  46.6 us
    ppermute x20, waiting for transfers between devices, move(): return lax.ppermute(value, 'ctx', pairs)  14.6 us
    pallas_call x4, Pallas kernels, finish(): pl.pallas_call(finish_body, grid=(hc,), in_specs=in_specs, out_specs=[cb,...  11.1 us
    ppermute x5, starting transfers between devices, sum_over(): x = x + lax.ppermute(x, name, [(i, i ^ step) for i in range(count)])  8.87 us
    ppermute x5, waiting for transfers between devices, sum_over(): x = x + lax.ppermute(x, name, [(i, i ^ step) for i in range(count)])  7.43 us
    pallas_call x2, Pallas kernels, pack(): pl.pallas_call(functools.partial(pack_body, chunks), grid=(at,), in_specs...  7.38 us
  transfers between devices with their start and end apart: 25, of which 11 were waited for; matrix products, arithmetic and copies ran while one was open for 3% of the time, Pallas kernels for 40%

profile of v4, /device:TPU:0, one launch (start us, length us, event | category | flops | bytes accessed | tf_op | source)
XLA Modules:
  0.0 154.0 jit_solution(15055151493050136435)
XLA Ops:
  0.6 2.1 %pack_kv.2.own_ref = bf16[512,512]{1,0:T(8,128)(2,1)} custom-call(bf16[512,1024]{1,0:T(8,128)(2,1)} %k_ref.11, bf16[512,1024]{1,0:T(8,128)(2,1)} %v_ref.3, f32[1,128]{1,0:T(1,128)} %bitcast.14), custom_call_target="tpu_custom_call" | custom-call | flops 2000000000 | bytes 1048576 | tf_op jit(solution)/shard_map/pack_kv/pallas_call | solution.py:204
  2.7 5.0 %collective-permute-start.1 = (bf16[512,512]{1,0:T(8,128)(2,1)}, bf16[512,512]{1,0:T(8,128)(2,1)S(1)}, u32[]{:S(2)}, u32[]{:S(2)}) collective-permute-start(bf16[512,512]{1,0:T(8,128)(2,1)} %pack_kv.2.own_ref), channel_id=1, source_target_pairs={{0,4},{2,6},{4,8},{6,10},{8,12},{10,14},{12,16},{14,18},{16,20},{1... | collective-permute-start | bytes 1572872 | tf_op jit(solution)/shard_map/far0/ppermute | solution.py:245
  7.8 3.4 %collective-permute-start = (bf16[512,512]{1,0:T(8,128)(2,1)}, bf16[512,512]{1,0:T(8,128)(2,1)S(1)}, u32[]{:S(2)}, u32[]{:S(2)}) collective-permute-start(bf16[512,512]{1,0:T(8,128)(2,1)} %pack_kv.2.own_ref), channel_id=1, source_target_pairs={{0,2},{4,6},{8,10},{12,14},{16,18},{20,22},{24,26},{28,30},{1,3},{... | collective-permute-start | bytes 1572872 | tf_op jit(solution)/shard_map/up0/ppermute | solution.py:245
  11.2 5.3 %pack_kv.3 = (bf16[512,768]{1,0:T(8,128)(2,1)}, bf16[512,512]{1,0:T(8,128)(2,1)}, bf16[512,256]{1,0:T(8,128)(2,1)}) custom-call(bf16[512,1024]{1,0:T(8,128)(2,1)} %k_ref.11, bf16[512,1024]{1,0:T(8,128)(2,1)} %v_ref.3, f32[1,128]{1,0:T(1,128)} %bitcast.15), custom_call_target="tpu_custom_call" | custom-call | flops 6000000000 | bytes 3145728 | tf_op jit(solution)/shard_map/pack_kv/pallas_call | solution.py:204
  16.5 3.4 %collective-permute-start.4 = (bf16[512,768]{1,0:T(8,128)(2,1)}, bf16[512,768]{1,0:T(8,128)(2,1)S(1)}, u32[]{:S(2)}, u32[]{:S(2)}) collective-permute-start(bf16[512,768]{1,0:T(8,128)(2,1)} %get-tuple-element.54.r_5_), channel_id=1, source_target_pairs={{0,4},{2,6},{4,8},{6,10},{8,12},{10,14},{12,16},{14,18},{16,20},{1... | collective-permute-start | bytes 2359304 | tf_op jit(solution)/shard_map/far1/ppermute | solution.py:245
  19.9 1.3 collective-permute-start.3
  21.3 3.4 %collective-permute-start.8 = (bf16[512,512]{1,0:T(8,128)(2,1)}, bf16[512,512]{1,0:T(8,128)(2,1)S(1)}, u32[]{:S(2)}, u32[]{:S(2)}) collective-permute-start(bf16[512,512]{1,0:T(8,128)(2,1)} %get-tuple-element.61.r_5_), channel_id=1, source_target_pairs={{0,4},{2,6},{4,8},{6,10},{8,12},{10,14},{12,16},{14,18},{16,20},{1... | collective-permute-start | bytes 1572872 | tf_op jit(solution)/shard_map/far2/ppermute | solution.py:245
  27.9 6.2 %collective-permute-start.7 = (bf16[512,512]{1,0:T(8,128)(2,1)}, bf16[512,512]{1,0:T(8,128)(2,1)}, u32[]{:S(2)}, u32[]{:S(2)}) collective-permute-start(bf16[512,512]{1,0:T(8,128)(2,1)} %get-tuple-element.61.r_5_), channel_id=1, source_target_pairs={{0,2},{4,6},{8,10},{12,14},{16,18},{20,22},{24,26},{28,30},{1,3},{... | collective-permute-start | bytes 1572872 | tf_op jit(solution)/shard_map/up2/ppermute | solution.py:245
  34.1 4.1 %collective-permute-done.4.r_8_ = bf16[512,768]{1,0:T(8,128)(2,1)S(1)} collective-permute-done((bf16[512,768]{1,0:T(8,128)(2,1)}, bf16[512,768]{1,0:T(8,128)(2,1)S(1)}, u32[]{:S(2)}, u32[]{:S(2)}) %collective-permute-start.4) | collective-permute-done | bytes 786464 | tf_op jit(solution)/shard_map/far1/ppermute | solution.py:245
  38.2 5.0 %collective-permute-start.13 = (bf16[512,256]{1,0:T(8,128)(2,1)}, bf16[512,256]{1,0:T(8,128)(2,1)}, u32[]{:S(2)}, u32[]{:S(2)}) collective-permute-start(bf16[512,256]{1,0:T(8,128)(2,1)} %get-tuple-element.70.r_5_), channel_id=1, source_target_pairs={{0,4},{2,6},{4,8},{6,10},{8,12},{10,14},{12,16},{14,18},{16,20},{1... | collective-permute-start | bytes 786440 | tf_op jit(solution)/shard_map/far3/ppermute | solution.py:245
  44.4 11.6 %attn_grad.4 = (bf16[512,2048]{1,0:T(8,128)(2,1)}, f32[512,512]{1,0:T(8,128)}, bf16[512,512]{1,0:T(8,128)(2,1)}, bf16[512,512]{1,0:T(8,128)(2,1)}, f32[128,256]{1,0:T(8,128)}, /*index=5*/f32[8,128]{1,0:T(8,128)}) custom-call(s32[1]{0:T(128)} %bitcast.par_ref.r_0_, s32[1,512]{1,0:T(1,128)} %add_maximum_fusion.lo_ref.r_1_, f32[128,1]{1,0:T(8,128)} %copy.25.gq_ref.r_2_, ...), custom_call_target="tpu_custom_call" | custom-call | flops 12000000000 | bytes 3145728 | tf_op jit(solution)/shard_map/attn_grad/pallas_call | solution.py:168
  56.1 5.3 %collective-permute-start.12 = (bf16[512,256]{1,0:T(8,128)(2,1)}, bf16[512,256]{1,0:T(8,128)(2,1)}, u32[]{:S(2)}, u32[]{:S(2)}) collective-permute-start(bf16[512,256]{1,0:T(8,128)(2,1)} %get-tuple-element.70.r_5_), channel_id=1, source_target_pairs={{0,2},{4,6},{8,10},{12,14},{16,18},{20,22},{24,26},{28,30},{1,3},{... | collective-permute-start | bytes 786440 | tf_op jit(solution)/shard_map/up3/ppermute | solution.py:245
  63.0 16.4 %attn_grad.5 = (bf16[512,2048]{1,0:T(8,128)(2,1)}, f32[512,768]{1,0:T(8,128)}, bf16[512,768]{1,0:T(8,128)(2,1)}, bf16[512,768]{1,0:T(8,128)(2,1)}, f32[128,256]{1,0:T(8,128)}, /*index=5*/f32[8,128]{1,0:T(8,128)}) custom-call(s32[1]{0:T(128)} %bitcast.par_ref.r_0_, s32[1,512]{1,0:T(1,128)} %add_maximum_fusion.lo_ref.r_1_, ...), custom_call_target="tpu_custom_call", output_to_operand_aliasing={{0}: (9, {})} | custom-call | flops 17999998976 | bytes 4718592 | tf_op jit(solution)/shard_map/attn_grad/pallas_call | solution.py:168
  79.6 1.5 collective-permute-start.11
  81.0 3.5 %collective-permute-start.10 = (bf16[512,768]{1,0:T(8,128)(2,1)}, bf16[512,768]{1,0:T(8,128)(2,1)S(1)}, u32[]{:S(2)}, u32[]{:S(2)}) collective-permute-start(bf16[512,768]{1,0:T(8,128)(2,1)} %get-tuple-element.67), channel_id=1, source_target_pairs={{0,2},{2,0},{4,6},{6,4},{8,10},{10,8},{12,14},{14,12},{16,18},{18,... | collective-permute-start | bytes 2359304 | tf_op jit(solution)/shard_map/swap1/ppermute | solution.py:245
  84.5 1.3 collective-permute-done.9.r_7_
  85.8 11.8 %attn_grad.6 = (bf16[512,2048]{1,0:T(8,128)(2,1)}, f32[512,512]{1,0:T(8,128)}, bf16[512,512]{1,0:T(8,128)(2,1)}, bf16[512,512]{1,0:T(8,128)(2,1)}, f32[128,256]{1,0:T(8,128)}, /*index=5*/f32[8,128]{1,0:T(8,128)}) custom-call(s32[1]{0:T(128)} %bitcast.par_ref.r_0_, s32[1,512]{1,0:T(1,128)} %add_maximum_fusion.lo_ref.r_1_, ...), custom_call_target="tpu_custom_call", output_to_operand_aliasing={{0}: (9, {})} | custom-call | flops 12000000000 | bytes 3145728 | tf_op jit(solution)/shard_map/attn_grad/pallas_call | solution.py:168
  97.6 1.3 collective-permute-start.14
  98.9 2.7 %collective-permute-start.18 = (bf16[512,512]{1,0:T(8,128)(2,1)}, bf16[512,512]{1,0:T(8,128)(2,1)S(1)}, u32[]{:S(2)}, u32[]{:S(2)}) collective-permute-start(bf16[512,512]{1,0:T(8,128)(2,1)} %get-tuple-element.88), channel_id=1, source_target_pairs={{0,2},{2,0},{4,6},{6,4},{8,10},{10,8},{12,14},{14,12},{16,18},{18,... | collective-permute-start | bytes 1572872 | tf_op jit(solution)/shard_map/swap2/ppermute | solution.py:245
  101.7 1.5 collective-permute-done.10.x_ref
  104.7 4.2 %collective-permute-done.14.r_7_ = bf16[512,256]{1,0:T(8,128)(2,1)S(1)} collective-permute-done((bf16[512,256]{1,0:T(8,128)(2,1)}, bf16[512,256]{1,0:T(8,128)(2,1)S(1)}, u32[]{:S(2)}, u32[]{:S(2)}) %collective-permute-start.14) | collective-permute-done | bytes 262176 | tf_op jit(solution)/shard_map/relay3/ppermute | solution.py:245
  109.7 6.9 %attn_grad.7 = (bf16[512,2048]{1,0:T(8,128)(2,1)}, f32[512,256]{1,0:T(8,128)}, bf16[512,256]{1,0:T(8,128)(2,1)}, bf16[512,256]{1,0:T(8,128)(2,1)}, f32[128,256]{1,0:T(8,128)}, /*index=5*/f32[8,128]{1,0:T(8,128)}) custom-call(s32[1]{0:T(128)} %bitcast.par_ref.r_0_, s32[1,512]{1,0:T(1,128)} %add_maximum_fusion.lo_ref.r_1_, ...), custom_call_target="tpu_custom_call", output_to_operand_aliasing={{0}: (9, {})} | custom-call | flops 6000000000 | bytes 1572864 | tf_op jit(solution)/shard_map/attn_grad/pallas_call | solution.py:168
  116.7 3.1 %collective-permute-done.18.x_ref = bf16[512,512]{1,0:T(8,128)(2,1)S(1)} collective-permute-done((bf16[512,512]{1,0:T(8,128)(2,1)}, bf16[512,512]{1,0:T(8,128)(2,1)S(1)}, u32[]{:S(2)}, u32[]{:S(2)}) %collective-permute-start.18) | collective-permute-done | bytes 524320 | tf_op jit(solution)/shard_map/swap2/ppermute | solution.py:245
  123.1 2.5 %finish_kv.4 = (bf16[512,1024]{1,0:T(8,128)(2,1)}, bf16[512,1024]{1,0:T(8,128)(2,1)}) custom-call(s32[1]{0:T(128)} %bitcast.par_ref.r_0_, f32[512,512]{1,0:T(8,128)} %get-tuple-element.80.own_ref, bf16[512,512]{1,0:T(8,128)(2,1)} %copy-done.4, bf16[512,512]{1,0:T(8,128)(2,1)} %collective-permute-done.11.y_ref, bf16[512,1024]{1,0:T(8,128)(2,1)} %k_ref.11, ...), custom_call_target="tpu_custom_call" | custom-call | flops 2000000000 | bytes 1048576 | tf_op jit(solution)/shard_map/finish_kv/pallas_call | solution.py:236
  125.7 3.9 %finish_kv.5 = (bf16[512,1024]{1,0:T(8,128)(2,1)}, bf16[512,1024]{1,0:T(8,128)(2,1)}) custom-call(s32[1]{0:T(128)} %bitcast.par_ref.r_0_, f32[512,768]{1,0:T(8,128)} %get-tuple-element.79.own_ref, bf16[512,768]{1,0:T(8,128)(2,1)} %copy-done.1, bf16[512,768]{1,0:T(8,128)(2,1)} %collective-permute-done.16.y_ref, ...), custom_call_target="tpu_custom_call", output_to_operand_aliasing={{0}: (6, {}), {1}: (7, {})} | custom-call | flops 3000000000 | bytes 1572864 | tf_op jit(solution)/shard_map/finish_kv/pallas_call | solution.py:236
  130.9 3.6 %collective-permute-done.21 = f32[2,128]{1,0:T(2,128)S(1)} collective-permute-done((f32[2,128]{1,0:T(2,128)S(1)}, f32[2,128]{1,0:T(2,128)S(1)}, u32[]{:S(2)}, u32[]{:S(2)}) %collective-permute-start.21) | collective-permute-done | bytes 1056 | tf_op jit(solution)/shard_map/ppermute | solution.py:258
  134.5 2.6 %collective-permute-start.22 = (f32[2,128]{1,0:T(2,128)S(1)}, f32[2,128]{1,0:T(2,128)S(1)}, u32[]{:S(2)}, u32[]{:S(2)}) collective-permute-start(f32[2,128]{1,0:T(2,128)S(1)} %add.82), channel_id=1, source_target_pairs={{0,4},{2,6},{4,0},{6,2},{8,12},{10,14},{12,8},{14,10},{16,20},{18,... | collective-permute-start | bytes 3080 | tf_op jit(solution)/shard_map/ppermute | solution.py:258
  137.1 1.5 %collective-permute-done.22 = f32[2,128]{1,0:T(2,128)S(1)} collective-permute-done((f32[2,128]{1,0:T(2,128)S(1)}, f32[2,128]{1,0:T(2,128)S(1)}, u32[]{:S(2)}, u32[]{:S(2)}) %collective-permute-start.22) | collective-permute-done | bytes 1056 | tf_op jit(solution)/shard_map/ppermute | solution.py:258
  138.7 3.1 %collective-permute-start.23 = (f32[2,128]{1,0:T(2,128)S(1)}, f32[2,128]{1,0:T(2,128)S(1)}, u32[]{:S(2)}, u32[]{:S(2)}) collective-permute-start(f32[2,128]{1,0:T(2,128)S(1)} %add.83), channel_id=1, source_target_pairs={{0,8},{2,10},{4,12},{6,14},{8,0},{10,2},{12,4},{14,6},{16,24},{18,... | collective-permute-start | bytes 3080 | tf_op jit(solution)/shard_map/ppermute | solution.py:258
  143.3 3.0 %collective-permute-start.24 = (f32[2,128]{1,0:T(2,128)S(1)}, f32[2,128]{1,0:T(2,128)S(1)}, u32[]{:S(2)}, u32[]{:S(2)}) collective-permute-start(f32[2,128]{1,0:T(2,128)S(1)} %add.84), channel_id=1, source_target_pairs={{0,16},{2,18},{4,20},{6,22},{8,24},{10,26},{12,28},{14,30},{16,0},... | collective-permute-start | bytes 3080 | tf_op jit(solution)/shard_map/ppermute | solution.py:258
  147.2 2.5 %finish_kv.6 = (bf16[512,1024]{1,0:T(8,128)(2,1)}, bf16[512,1024]{1,0:T(8,128)(2,1)}) custom-call(s32[1]{0:T(128)} %bitcast.par_ref.r_0_, f32[512,512]{1,0:T(8,128)} %get-tuple-element.87.own_ref, bf16[512,512]{1,0:T(8,128)(2,1)} %copy-done.3, bf16[512,512]{1,0:T(8,128)(2,1)} %copy-done.23, ...), custom_call_target="tpu_custom_call", output_to_operand_aliasing={{0}: (6, {}), {1}: (7, {})} | custom-call | flops 2000000000 | bytes 1048576 | tf_op jit(solution)/shard_map/finish_kv/pallas_call | solution.py:236
  151.9 2.2 %finish_kv.7 = (bf16[512,1024]{1,0:T(8,128)(2,1)}, bf16[512,1024]{1,0:T(8,128)(2,1)}) custom-call(s32[1]{0:T(128)} %bitcast.par_ref.r_0_, f32[512,256]{1,0:T(8,128)} %get-tuple-element.74.own_ref, bf16[512,256]{1,0:T(8,128)(2,1)} %copy-done, bf16[512,256]{1,0:T(8,128)(2,1)} %copy-done.7, ...), custom_call_target="tpu_custom_call", output_to_operand_aliasing={{0}: (6, {}), {1}: (7, {})} | custom-call | flops 1000000000 | bytes 524288 | tf_op jit(solution)/shard_map/finish_kv/pallas_call | solution.py:236
  (100 shorter events, 17.5 us)
Async XLA Ops:
  2.7 22.0 %copy-start.25 = (f32[128]{0:T(128)S(1)}, f32[128]{0:T(128)}, u32[]{:S(2)}) copy-start(f32[128]{0:T(128)} %param.12) | copy-start | bytes 1540
  2.7 23.3 %copy-start.12 = (s32[8192]{0:T(1024)S(1)}, s32[8192]{0:T(1024)}, u32[]{:S(2)}) copy-start(s32[8192]{0:T(1024)} %param.11) | copy-start | bytes 98308
  2.7 22.0 %collective-permute-start.1 = (bf16[512,512]{1,0:T(8,128)(2,1)}, bf16[512,512]{1,0:T(8,128)(2,1)S(1)}, u32[]{:S(2)}, u32[]{:S(2)}) collective-permute-start(bf16[512,512]{1,0:T(8,128)(2,1)} %pack_kv.2.own_ref), channel_id=1, source_target_pairs={{0,4},{2,6},{4,8},{6,10},{8,12},{10,14},{12,16},{14,18},{16,20},{1... | collective-permute-start | bytes 1572872 | tf_op jit(solution)/shard_map/far0/ppermute | solution.py:245
  7.8 20.1 %collective-permute-start = (bf16[512,512]{1,0:T(8,128)(2,1)}, bf16[512,512]{1,0:T(8,128)(2,1)S(1)}, u32[]{:S(2)}, u32[]{:S(2)}) collective-permute-start(bf16[512,512]{1,0:T(8,128)(2,1)} %pack_kv.2.own_ref), channel_id=1, source_target_pairs={{0,2},{4,6},{8,10},{12,14},{16,18},{20,22},{24,26},{28,30},{1,3},{... | collective-permute-start | bytes 1572872 | tf_op jit(solution)/shard_map/up0/ppermute | solution.py:245
  16.5 21.7 %collective-permute-start.4 = (bf16[512,768]{1,0:T(8,128)(2,1)}, bf16[512,768]{1,0:T(8,128)(2,1)S(1)}, u32[]{:S(2)}, u32[]{:S(2)}) collective-permute-start(bf16[512,768]{1,0:T(8,128)(2,1)} %get-tuple-element.54.r_5_), channel_id=1, source_target_pairs={{0,4},{2,6},{4,8},{6,10},{8,12},{10,14},{12,16},{14,18},{16,20},{1... | collective-permute-start | bytes 2359304 | tf_op jit(solution)/shard_map/far1/ppermute | solution.py:245
  19.9 41.5 %collective-permute-start.3 = (bf16[512,768]{1,0:T(8,128)(2,1)}, bf16[512,768]{1,0:T(8,128)(2,1)S(1)}, u32[]{:S(2)}, u32[]{:S(2)}) collective-permute-start(bf16[512,768]{1,0:T(8,128)(2,1)} %get-tuple-element.54.r_5_), channel_id=1, source_target_pairs={{0,2},{4,6},{8,10},{12,14},{16,18},{20,22},{24,26},{28,30},{1,3},{... | collective-permute-start | bytes 2359304 | tf_op jit(solution)/shard_map/up1/ppermute | solution.py:245
  21.3 34.8 %collective-permute-start.8 = (bf16[512,512]{1,0:T(8,128)(2,1)}, bf16[512,512]{1,0:T(8,128)(2,1)S(1)}, u32[]{:S(2)}, u32[]{:S(2)}) collective-permute-start(bf16[512,512]{1,0:T(8,128)(2,1)} %get-tuple-element.61.r_5_), channel_id=1, source_target_pairs={{0,4},{2,6},{4,8},{6,10},{8,12},{10,14},{12,16},{14,18},{16,20},{1... | collective-permute-start | bytes 1572872 | tf_op jit(solution)/shard_map/far2/ppermute | solution.py:245
  24.7 19.7 %copy-start.21 = (bf16[512,512]{1,0:T(8,128)(2,1)}, bf16[512,512]{1,0:T(8,128)(2,1)S(1)}, u32[]{:S(2)}) copy-start(bf16[512,512]{1,0:T(8,128)(2,1)S(1)} %collective-permute-done.1.h2_ref) | copy-start | bytes 1572868
  24.7 18.4 %collective-permute-start.2 = (bf16[512,512]{1,0:T(8,128)(2,1)S(1)}, bf16[512,512]{1,0:T(8,128)(2,1)}, u32[]{:S(2)}, u32[]{:S(2)}) collective-permute-start(bf16[512,512]{1,0:T(8,128)(2,1)S(1)} %collective-permute-done.1.h2_ref), channel_id=1, source_target_pairs={{2,0},{6,4},{10,8},{14,12},{18,16},{22,20},{26,24},{30,28},{3,1},{... | collective-permute-start | bytes 1572872 | tf_op jit(solution)/shard_map/relay0/ppermute | solution.py:245
  27.9 53.2 %collective-permute-start.7 = (bf16[512,512]{1,0:T(8,128)(2,1)}, bf16[512,512]{1,0:T(8,128)(2,1)}, u32[]{:S(2)}, u32[]{:S(2)}) collective-permute-start(bf16[512,512]{1,0:T(8,128)(2,1)} %get-tuple-element.61.r_5_), channel_id=1, source_target_pairs={{0,2},{4,6},{8,10},{12,14},{16,18},{20,22},{24,26},{28,30},{1,3},{... | collective-permute-start | bytes 1572872 | tf_op jit(solution)/shard_map/up2/ppermute | solution.py:245
  38.2 17.9 %copy-start.17 = (bf16[512,768]{1,0:T(8,128)(2,1)}, bf16[512,768]{1,0:T(8,128)(2,1)S(1)}, u32[]{:S(2)}) copy-start(bf16[512,768]{1,0:T(8,128)(2,1)S(1)} %collective-permute-done.4.r_8_) | copy-start | bytes 2359300
  38.2 59.5 %collective-permute-start.13 = (bf16[512,256]{1,0:T(8,128)(2,1)}, bf16[512,256]{1,0:T(8,128)(2,1)}, u32[]{:S(2)}, u32[]{:S(2)}) collective-permute-start(bf16[512,256]{1,0:T(8,128)(2,1)} %get-tuple-element.70.r_5_), channel_id=1, source_target_pairs={{0,4},{2,6},{4,8},{6,10},{8,12},{10,14},{12,16},{14,18},{16,20},{1... | collective-permute-start | bytes 786440 | tf_op jit(solution)/shard_map/far3/ppermute | solution.py:245
  43.1 18.5 %collective-permute-start.5 = (bf16[512,768]{1,0:T(8,128)(2,1)S(1)}, bf16[512,768]{1,0:T(8,128)(2,1)S(1)}, u32[]{:S(2)}, u32[]{:S(2)}) collective-permute-start(bf16[512,768]{1,0:T(8,128)(2,1)S(1)} %collective-permute-done.4.r_8_), channel_id=1, source_target_pairs={{2,0},{6,4},{10,8},{14,12},{18,16},{22,20},{26,24},{30,28},{3,1},{... | collective-permute-start | bytes 2359304 | tf_op jit(solution)/shard_map/relay1/ppermute | solution.py:245
  56.1 23.3 %copy-start.20 = (bf16[512,512]{1,0:T(8,128)(2,1)}, bf16[512,512]{1,0:T(8,128)(2,1)S(1)}, u32[]{:S(2)}) copy-start(bf16[512,512]{1,0:T(8,128)(2,1)S(1)} %collective-permute-done.8.r_8_) | copy-start | bytes 1572868
  56.1 48.6 %collective-permute-start.12 = (bf16[512,256]{1,0:T(8,128)(2,1)}, bf16[512,256]{1,0:T(8,128)(2,1)}, u32[]{:S(2)}, u32[]{:S(2)}) collective-permute-start(bf16[512,256]{1,0:T(8,128)(2,1)} %get-tuple-element.70.r_5_), channel_id=1, source_target_pairs={{0,2},{4,6},{8,10},{12,14},{16,18},{20,22},{24,26},{28,30},{1,3},{... | collective-permute-start | bytes 786440 | tf_op jit(solution)/shard_map/up3/ppermute | solution.py:245
  61.4 18.0 %collective-permute-start.6 = (bf16[512,512]{1,0:T(8,128)(2,1)}, bf16[512,512]{1,0:T(8,128)(2,1)S(1)}, u32[]{:S(2)}, u32[]{:S(2)}) collective-permute-start(bf16[512,512]{1,0:T(8,128)(2,1)} %get-tuple-element.58), channel_id=1, source_target_pairs={{0,2},{2,0},{4,6},{6,4},{8,10},{10,8},{12,14},{14,12},{16,18},{18,... | collective-permute-start | bytes 1572872 | tf_op jit(solution)/shard_map/swap0/ppermute | solution.py:245
  61.7 24.2 %collective-permute-start.9 = (bf16[512,512]{1,0:T(8,128)(2,1)S(1)}, bf16[512,512]{1,0:T(8,128)(2,1)}, u32[]{:S(2)}, u32[]{:S(2)}) collective-permute-start(bf16[512,512]{1,0:T(8,128)(2,1)S(1)} %collective-permute-done.8.r_8_), channel_id=1, source_target_pairs={{2,0},{6,4},{10,8},{14,12},{18,16},{22,20},{26,24},{30,28},{3,1},{... | collective-permute-start | bytes 1572872 | tf_op jit(solution)/shard_map/relay2/ppermute | solution.py:245
  79.4 18.2 %copy-start.4 = (bf16[512,512]{1,0:T(8,128)(2,1)}, bf16[512,512]{1,0:T(8,128)(2,1)S(1)}, u32[]{:S(2)}) copy-start(bf16[512,512]{1,0:T(8,128)(2,1)S(1)} %collective-permute-done.6.x_ref) | copy-start | bytes 1572868
  79.6 25.2 %collective-permute-start.11 = (bf16[512,512]{1,0:T(8,128)(2,1)S(1)}, bf16[512,512]{1,0:T(8,128)(2,1)}, u32[]{:S(2)}, u32[]{:S(2)}) collective-permute-start(bf16[512,512]{1,0:T(8,128)(2,1)S(1)} %fusion.1), channel_id=1, source_target_pairs={{4,0},{6,2},{8,4},{10,6},{12,8},{14,10},{16,12},{18,14},{20,16},{2... | collective-permute-start | bytes 1572872 | tf_op jit(solution)/shard_map/ret0/ppermute | solution.py:245
  81.0 22.1 %collective-permute-start.10 = (bf16[512,768]{1,0:T(8,128)(2,1)}, bf16[512,768]{1,0:T(8,128)(2,1)S(1)}, u32[]{:S(2)}, u32[]{:S(2)}) collective-permute-start(bf16[512,768]{1,0:T(8,128)(2,1)} %get-tuple-element.67), channel_id=1, source_target_pairs={{0,2},{2,0},{4,6},{6,4},{8,10},{10,8},{12,14},{14,12},{16,18},{18,... | collective-permute-start | bytes 2359304 | tf_op jit(solution)/shard_map/swap1/ppermute | solution.py:245
  97.6 11.3 %collective-permute-start.14 = (bf16[512,256]{1,0:T(8,128)(2,1)}, bf16[512,256]{1,0:T(8,128)(2,1)S(1)}, u32[]{:S(2)}, u32[]{:S(2)}) collective-permute-start(bf16[512,256]{1,0:T(8,128)(2,1)} %collective-permute-done.13.r_8_), channel_id=1, source_target_pairs={{2,0},{6,4},{10,8},{14,12},{18,16},{22,20},{26,24},{30,28},{3,1},{... | collective-permute-start | bytes 786440 | tf_op jit(solution)/shard_map/relay3/ppermute | solution.py:245
  98.9 20.9 %collective-permute-start.18 = (bf16[512,512]{1,0:T(8,128)(2,1)}, bf16[512,512]{1,0:T(8,128)(2,1)S(1)}, u32[]{:S(2)}, u32[]{:S(2)}) collective-permute-start(bf16[512,512]{1,0:T(8,128)(2,1)} %get-tuple-element.88), channel_id=1, source_target_pairs={{0,2},{2,0},{4,6},{6,4},{8,10},{10,8},{12,14},{14,12},{16,18},{18,... | collective-permute-start | bytes 1572872 | tf_op jit(solution)/shard_map/swap2/ppermute | solution.py:245
  103.4 22.3 %collective-permute-start.16 = (bf16[512,768]{1,0:T(8,128)(2,1)S(1)}, bf16[512,768]{1,0:T(8,128)(2,1)}, u32[]{:S(2)}, u32[]{:S(2)}) collective-permute-start(bf16[512,768]{1,0:T(8,128)(2,1)S(1)} %fusion), channel_id=1, source_target_pairs={{4,0},{6,2},{8,4},{10,6},{12,8},{14,10},{16,12},{18,14},{20,16},{2... | collective-permute-start | bytes 2359304 | tf_op jit(solution)/shard_map/ret1/ppermute | solution.py:245
  116.7 12.9 %collective-permute-start.15 = (bf16[512,256]{1,0:T(8,128)(2,1)}, bf16[512,256]{1,0:T(8,128)(2,1)S(1)}, u32[]{:S(2)}, u32[]{:S(2)}) collective-permute-start(bf16[512,256]{1,0:T(8,128)(2,1)} %get-tuple-element.75), channel_id=1, source_target_pairs={{0,2},{2,0},{4,6},{6,4},{8,10},{10,8},{12,14},{14,12},{16,18},{18,... | collective-permute-start | bytes 786440 | tf_op jit(solution)/shard_map/swap3/ppermute | solution.py:245
  120.0 26.3 %collective-permute-start.19 = (bf16[512,512]{1,0:T(8,128)(2,1)S(1)}, bf16[512,512]{1,0:T(8,128)(2,1)S(1)}, u32[]{:S(2)}, u32[]{:S(2)}) collective-permute-start(bf16[512,512]{1,0:T(8,128)(2,1)S(1)} %fusion.2), channel_id=1, source_target_pairs={{4,0},{6,2},{8,4},{10,6},{12,8},{14,10},{16,12},{18,14},{20,16},{2... | collective-permute-start | bytes 1572872 | tf_op jit(solution)/shard_map/ret2/ppermute | solution.py:245
  129.6 20.1 %copy-start = (bf16[512,256]{1,0:T(8,128)(2,1)}, bf16[512,256]{1,0:T(8,128)(2,1)S(1)}, u32[]{:S(2)}) copy-start(bf16[512,256]{1,0:T(8,128)(2,1)S(1)} %collective-permute-done.15.x_ref) | copy-start | bytes 786436
  129.7 1.2 collective-permute-start.20
  130.9 3.6 %collective-permute-start.21 = (f32[2,128]{1,0:T(2,128)S(1)}, f32[2,128]{1,0:T(2,128)S(1)}, u32[]{:S(2)}, u32[]{:S(2)}) collective-permute-start(f32[2,128]{1,0:T(2,128)S(1)} %add.81), channel_id=1, source_target_pairs={{0,2},{2,0},{4,6},{6,4},{8,10},{10,8},{12,14},{14,12},{16,18},{18,... | collective-permute-start | bytes 3080 | tf_op jit(solution)/shard_map/ppermute | solution.py:258
  134.5 4.2 %collective-permute-start.22 = (f32[2,128]{1,0:T(2,128)S(1)}, f32[2,128]{1,0:T(2,128)S(1)}, u32[]{:S(2)}, u32[]{:S(2)}) collective-permute-start(f32[2,128]{1,0:T(2,128)S(1)} %add.82), channel_id=1, source_target_pairs={{0,4},{2,6},{4,0},{6,2},{8,12},{10,14},{12,8},{14,10},{16,20},{18,... | collective-permute-start | bytes 3080 | tf_op jit(solution)/shard_map/ppermute | solution.py:258
  138.7 4.7 %collective-permute-start.23 = (f32[2,128]{1,0:T(2,128)S(1)}, f32[2,128]{1,0:T(2,128)S(1)}, u32[]{:S(2)}, u32[]{:S(2)}) collective-permute-start(f32[2,128]{1,0:T(2,128)S(1)} %add.83), channel_id=1, source_target_pairs={{0,8},{2,10},{4,12},{6,14},{8,0},{10,2},{12,4},{14,6},{16,24},{18,... | collective-permute-start | bytes 3080 | tf_op jit(solution)/shard_map/ppermute | solution.py:258
  141.8 9.4 %collective-permute-start.17 = (bf16[512,256]{1,0:T(8,128)(2,1)S(1)}, bf16[512,256]{1,0:T(8,128)(2,1)S(1)}, u32[]{:S(2)}, u32[]{:S(2)}) collective-permute-start(bf16[512,256]{1,0:T(8,128)(2,1)S(1)} %fusion.3), channel_id=1, source_target_pairs={{4,0},{6,2},{8,4},{10,6},{12,8},{14,10},{16,12},{18,14},{20,16},{2... | collective-permute-start | bytes 786440 | tf_op jit(solution)/shard_map/ret3/ppermute | solution.py:245
  143.3 7.3 %collective-permute-start.24 = (f32[2,128]{1,0:T(2,128)S(1)}, f32[2,128]{1,0:T(2,128)S(1)}, u32[]{:S(2)}, u32[]{:S(2)}) collective-permute-start(f32[2,128]{1,0:T(2,128)S(1)} %add.84), channel_id=1, source_target_pairs={{0,16},{2,18},{4,20},{6,22},{8,24},{10,26},{12,28},{14,30},{16,0},... | collective-permute-start | bytes 3080 | tf_op jit(solution)/shard_map/ppermute | solution.py:258
  (19 other events, 166.0 us)
